TPU v7x, 256 devices: a whole 4x4x8 slice. The times are simulated.
256 devices in a mesh: member: 16 (over z, core), domain: 16 (over x, y).
Axes of the slice: x: 4, y: 4, z: 8, core: 2. Of those that a mesh axis runs over, the one named last changes fastest.
Arguments:
- state: bfloat16 [256, 8, 256, 512], P('member', None, 'domain'), may hold values from -6 to 6
- spreading_number: float32 [256, 512], P('domain'), may hold values from 0.04 to 0.2
- zonal_transport_number: float32 [256, 512], P('domain'), may hold values from -0.5 to 0.5
- meridional_transport_number: float32 [256, 512], P('domain'), may hold values from -0.5 to 0.5
- obs_count: int32 [256, 4], P(('domain', 'member')), may hold values from 16 to 128, as said below
- obs_index: int32 [256, 4, 128], P(('domain', 'member')), may hold values from 0 to 1023
- obs_value: float32 [256, 4, 128], P(('domain', 'member')), may hold values from -6 to 6
- obs_weight: float32 [256, 4, 128], P(('domain', 'member')), may hold values from 0.25 to 4
Outputs:
- analysis: bfloat16 [256, 8, 256, 512], P('member', None, 'domain')
Inputs may be any that keep to these rules, and one draw needn't show every extreme that they name: `obs_count`: each latitude row has at least one patch with exactly 128 observations.
All inputs are finite; a program needn't handle non-finite values.
Results may differ from a plain program's by a relative error of at most 0.0067.
Values may be sent and summed in bfloat16 or wider, within the bound.
No kernel may reach another device: no remote copies, remote signals or barrier semaphores. Data moves between devices by JAX's collectives and lax.ppermute only.
A program may use at most 64 MiB of HBM per device.

v0:
```python
import math

import jax
import jax.numpy as jnp
from jax import lax
from jax.experimental import pallas as pl
from jax.experimental.pallas import tpu as pltpu
from jax.sharding import PartitionSpec as P

ITERS = 6
F32 = jnp.float32
BF16 = jnp.bfloat16


def halves(x):
    high = x.astype(BF16)
    return high, (x - high.astype(F32)).astype(BF16)


def thirds(x):
    high = x.astype(BF16)
    rest = x - high.astype(F32)
    mid = rest.astype(BF16)
    return high, mid, (rest - mid.astype(F32)).astype(BF16)


def dot(a, b):
    return jnp.dot(a, b, preferred_element_type=F32)


def row_picker(rows, first_row, span, members):
    out = lax.broadcasted_iota(jnp.int32, (rows * members, members * span), 0)
    src = lax.broadcasted_iota(jnp.int32, (rows * members, members * span), 1)
    row = out // members + first_row
    member = out % members
    return (src == member * span + row).astype(F32).astype(BF16)


def edges_kernel(state_ref, s_ref, z_ref, m_ref, south_ref, north_ref):
    field = pl.program_id(0)
    flat = state_ref[:, 0].reshape(256, 512)
    low = dot(row_picker(2, 0, 16, 16), flat).astype(BF16).reshape(2, 16, 512)
    high = dot(row_picker(2, 14, 16, 16), flat).astype(BF16).reshape(2, 16, 512)
    north_ref[pl.ds(2 * field, 2)] = high
    south_ref[pl.ds(2 * field, 2)] = low

    @pl.when(field == 0)
    def _():
        for out_ref, row in ((south_ref, 0), (north_ref, 15)):
            parts = []
            for ref in (s_ref, z_ref, m_ref):
                parts += list(thirds(ref[row : row + 1]))
            parts.append(jnp.zeros((7, 512), BF16))
            out_ref[16] = jnp.concatenate(parts, axis=0)


def edges(state, s, z, m):
    whole = pl.BlockSpec((16, 512), lambda f: (0, 0))
    shape = jax.ShapeDtypeStruct((17, 16, 512), BF16)
    out = pl.BlockSpec((17, 16, 512), lambda f: (0, 0, 0))
    return pl.pallas_call(
        edges_kernel,
        grid=(8,),
        in_specs=[pl.BlockSpec((16, 1, 16, 512), lambda f: (0, f, 0, 0)), whole, whole, whole],
        out_specs=[out, out],
        out_shape=[shape, shape],
        name="edges",
    )(state, s, z, m)


def coefficients(s, z, m):
    return (
        1.0 - 4.0 * s,
        s - 0.5 * z,
        s + 0.5 * z,
        s - 0.5 * m,
        s + 0.5 * m,
    )


def step_row(centre, north, south, coef):
    east = pltpu.roll(centre, 511, 1)
    west = pltpu.roll(centre, 1, 1)
    c, e, w, n, so = coef
    return centre * c + east * e + west * w + north * n + south * so


def forecast_kernel(
    flags_ref, state_ref, s_ref, z_ref, m_ref, low_ref, high_ref, out_ref, pick, coef, field_rows, middle
):
    field = pl.program_id(0)

    @pl.when(field == 0)
    def _():
        pick[...] = row_picker(16, 0, 16, 16)

        def put(row, s, z, m):
            for k, value in enumerate(coefficients(s, z, m)):
                coef[k, row] = jnp.broadcast_to(value, (8, 512))

        for ref, row in ((low_ref, 0), (high_ref, 17)):
            part = ref[16].astype(F32)
            rows = [part[3 * k : 3 * k + 1] + part[3 * k + 1 : 3 * k + 2] + part[3 * k + 2 : 3 * k + 3] for k in range(3)]
            put(row, *rows)
        for row in range(16):
            put(row + 1, s_ref[row : row + 1], z_ref[row : row + 1], m_ref[row : row + 1])

    flat = state_ref[:, 0].reshape(256, 512)
    field_rows[2:18] = dot(pick[...], flat).reshape(16, 16, 512)
    field_rows[0:2] = low_ref[pl.ds(2 * field, 2)].astype(F32)
    field_rows[18:20] = high_ref[pl.ds(2 * field, 2)].astype(F32)

    def coef_at(row):
        return [jnp.concatenate([coef[k, row]] * 2, axis=0) for k in range(5)]

    def first(row, carry):
        value = step_row(field_rows[row + 1], field_rows[row + 2], field_rows[row], coef_at(row))
        middle[row] = value.astype(BF16).astype(F32)
        return carry

    lax.fori_loop(0, 18, first, 0, unroll=3)
    middle[0] = jnp.where(flags_ref[0] == 1, 0.0, middle[0])
    middle[17] = jnp.where(flags_ref[1] == 1, 0.0, middle[17])

    def second(row, carry):
        value = step_row(middle[row + 1], middle[row + 2], middle[row], coef_at(row + 1))
        out_ref[row, 0] = value.astype(BF16)
        return carry

    lax.fori_loop(0, 16, second, 0, unroll=2)


def forecast(flags, state, s, z, m, low, high):
    whole = pl.BlockSpec((16, 512), lambda f: (0, 0))
    halo = pl.BlockSpec((17, 16, 512), lambda f: (0, 0, 0))
    return pl.pallas_call(
        forecast_kernel,
        grid=(8,),
        in_specs=[
            pl.BlockSpec(memory_space=pltpu.SMEM),
            pl.BlockSpec((16, 1, 16, 512), lambda f: (0, f, 0, 0)),
            whole,
            whole,
            whole,
            halo,
            halo,
        ],
        out_specs=pl.BlockSpec((16, 1, 16, 512), lambda f: (0, f, 0, 0)),
        out_shape=jax.ShapeDtypeStruct((16, 8, 16, 512), BF16),
        scratch_shapes=[
            pltpu.VMEM((256, 256), BF16),
            pltpu.VMEM((5, 18, 8, 512), F32),
            pltpu.VMEM((20, 16, 512), F32),
            pltpu.VMEM((18, 16, 512), F32),
        ],
        name="forecast",
    )(flags, state, s, z, m, low, high)


def left(parts):
    return jnp.concatenate(parts, axis=1)


def right(parts):
    high, low = parts
    top = jnp.concatenate([high, low], axis=1)
    bottom = jnp.concatenate([high, jnp.zeros_like(low)], axis=1)
    return jnp.concatenate([top, bottom], axis=0)


def product(a, b):
    both = dot(a, b)
    return both[:, :128] + both[:, 128:]


def weights_of(patches, members):
    spread = float(members - 1)
    rows = lax.broadcasted_iota(jnp.int32, (128, 128), 0)
    cols = lax.broadcasted_iota(jnp.int32, (128, 128), 1)
    eye = (rows == cols).astype(F32)
    work = []
    for observed, live, value, weight in patches:
        mean = jnp.sum(observed, axis=0, keepdims=True) * (1.0 / members)
        precision_w = weight * live
        root = jnp.sqrt(precision_w)
        scaled = (observed - mean) * root
        work.append({"a": scaled, "v": root * (value - mean)})
    for w in work:
        both = left(halves(w["a"]))
        gram = lax.dot_general(both, both, (((0,), (0,)), ((), ())), preferred_element_type=F32)
        w["g"] = gram[:128, :128] + gram[:128, 128:] + gram[128:, :128]
    for w in work:
        g = w["g"]
        square = jnp.sum(jnp.sum(g * g + (2.0 * spread) * (g * eye), axis=1, keepdims=True), axis=0, keepdims=True)
        scale = jnp.sqrt(square + spread * spread * members)
        inv = 1.0 / scale
        w["scale"], w["inv"] = scale, inv
        w["low"] = spread * inv
        w["y"] = g * inv + w["low"] * eye
        w["z0"] = jnp.ones((1, 1), F32)
    for sweep in range(ITERS):
        last = sweep == ITERS - 1
        for w in work:
            y = w["y"]
            y_parts = halves(y)
            y0 = w["low"] * w["z0"]
            w0 = w["z0"] * y0
            f0 = 1.5 - 0.5 * w0
            if sweep == 0:
                f = 1.5 * eye - 0.5 * y
                fq = -0.5 * eye
                w["next"] = (f, fq, f0, y_parts, None)
            else:
                zz = jnp.concatenate([left(w["z_parts"]), left(w["q_parts"])], axis=0)
                out = product(zz, right(y_parts))
                wq = out[128:] + w["z0"] * (w["low"] * w["q"] + w["z"])
                f = 1.5 * eye - 0.5 * out[:128]
                fq = -0.5 * wq
                w["next"] = (f, fq, f0, y_parts, zz)
        for w in work:
            f, fq, f0, y_parts, zz = w["next"]
            if sweep == 0:
                w["y"] = product(left(y_parts), right(halves(f)))
                w["z"], w["q"] = f, fq
            else:
                rhs = right(halves(f))
                lhs = zz if last else jnp.concatenate([zz, left(y_parts)], axis=0)
                out = product(lhs, rhs)
                w["z"] = out[:128]
                w["q"] = out[128:256] + w["z0"] * fq
                if not last:
                    w["y"] = out[256:]
            w["z0"] = w["z0"] * f0
            if not last:
                w["z_parts"], w["q_parts"] = halves(w["z"]), halves(w["q"])
    for w in work:
        z = right(halves(w["z"]))
        u = jnp.broadcast_to(w["v"], (8, 128))
        u = product(left(halves(u)), z)
        u = product(left(halves(u)), z)
        root = lax.rsqrt(w["scale"])
        w["u"] = u[:1] * root
        w["hat"] = w["a"] * root
        w["c1"] = math.sqrt(spread) * root
    big_rows = lax.broadcasted_iota(jnp.int32, (members, members), 0)
    big_cols = lax.broadcasted_iota(jnp.int32, (members, members), 1)
    big_eye = (big_rows == big_cols).astype(F32)
    result = []
    for w in work:
        hat_high, hat_low = halves(w["hat"])
        t = product(left((hat_high, hat_low)), right(halves(w["q"])))
        t = w["c1"] * t + w["u"]
        t_high, t_low = halves(t)
        nt = (((1,), (1,)), ((), ()))
        full = lax.dot_general(left((t_high, t_low)), left((hat_high, hat_high)), nt, preferred_element_type=F32)
        full = full + lax.dot_general(t_high, hat_low, nt, preferred_element_type=F32)
        result.append((full + (w["c1"] * w["z0"]) * big_eye).astype(BF16))
    return result


def selector(index_row):
    entry = lax.broadcasted_iota(jnp.int32, (1024, 128), 0)
    return (entry == index_row).astype(F32).astype(BF16)


def analysis_kernel(count_ref, x_ref, index_ref, value_ref, weight_ref, out_ref, held):
    slot = lax.broadcasted_iota(jnp.int32, (1, 128), 1)
    patches = []
    for p in range(4):
        for f in range(8):
            held[p, :, f * 128 : (f + 1) * 128] = x_ref[:, f, :, p * 128 : (p + 1) * 128].reshape(256, 128)
    for p in range(4):
        observed = dot(held[p], selector(index_ref[p : p + 1]))
        live = (slot < count_ref[0, p]).astype(F32)
        patches.append((observed, live, value_ref[p : p + 1], weight_ref[p : p + 1]))
    weights = weights_of(patches, 256)
    for p in range(4):
        for f in range(8):
            x = held[p, :, f * 128 : (f + 1) * 128].astype(F32)
            centre = jnp.sum(x, axis=0, keepdims=True) * (1.0 / 256)
            pert = (x - centre).astype(BF16)
            out = dot(weights[p], pert) + centre
            out_ref[:, f, :, p * 128 : (p + 1) * 128] = out.astype(BF16).reshape(16, 16, 128)


def analysis(count, x, index, value, weight):
    vmem = pl.BlockSpec(memory_space=pltpu.VMEM)
    return pl.pallas_call(
        analysis_kernel,
        in_specs=[pl.BlockSpec(memory_space=pltpu.SMEM), vmem, vmem, vmem, vmem],
        out_specs=vmem,
        out_shape=jax.ShapeDtypeStruct((16, 8, 16, 512), BF16),
        scratch_shapes=[pltpu.VMEM((4, 256, 1024), BF16)],
        compiler_params=pltpu.CompilerParams(vmem_limit_bytes=48 * 1024 * 1024),
        name="analysis",
    )(count, x, index, value, weight)


def result_kernel(x_ref, out_ref):
    flat = x_ref[:, 0].reshape(256, 512)
    out_ref[:, 0] = dot(row_picker(16, 0, 16, 16), flat).astype(BF16).reshape(16, 16, 512)


def result(x):
    spec = pl.BlockSpec((16, 1, 16, 512), lambda f: (0, f, 0, 0))
    return pl.pallas_call(
        result_kernel,
        grid=(8,),
        in_specs=[spec],
        out_specs=spec,
        out_shape=jax.ShapeDtypeStruct((16, 8, 16, 512), BF16),
        name="result",
    )(x)


def shards(state, s, z, m, obs_count, obs_index, obs_value, obs_weight):
    domains = lax.axis_size("domain")
    here = lax.axis_index("domain")
    south, north = edges(state, s, z, m)
    up = [(i, i + 1) for i in range(domains - 1)]
    down = [(i + 1, i) for i in range(domains - 1)]
    low = lax.ppermute(north, "domain", up)
    high = lax.ppermute(south, "domain", down)
    flags = jnp.stack([here == 0, here == domains - 1]).astype(jnp.int32)
    grown = forecast(flags, state, s, z, m, low, high)
    gathered = lax.all_to_all(grown, "member", split_axis=0, concat_axis=0, tiled=True)
    analysed = analysis(obs_count, gathered, obs_index[0], obs_value[0], obs_weight[0])
    back = lax.all_to_all(analysed, "member", split_axis=0, concat_axis=0, tiled=True)
    return result(back)


def solution(mesh):
    placed = (
        P("member", None, "domain", None),
        P("domain", None),
        P("domain", None),
        P("domain", None),
        P(("domain", "member"), None),
        P(("domain", "member"), None, None),
        P(("domain", "member"), None, None),
        P(("domain", "member"), None, None),
    )
    return jax.shard_map(
        shards,
        mesh=mesh,
        in_specs=placed,
        out_specs=P("member", None, "domain", None),
        check_vma=False,
    )
```

profile of v0, /device:TPU:7, one launch (start us, length us, event | category | flops | bytes accessed | tf_op | source)
XLA Modules:
  0.0 164.4 jit_solution(9255443702829990334)
XLA Ops:
  0.0 5.7 %edges.1 = (bf16[17,16,512]{2,1,0:T(8,128)(2,1)}, bf16[17,16,512]{2,1,0:T(8,128)(2,1)}) custom-call(bf16[16,8,16,512]{3,2,1,0:T(8,128)(2,1)} %state_ref.3, f32[16,512]{1,0:T(8,128)} %s_ref.3, f32[16,512]{1,0:T(8,128)} %z_ref.3, f32[16,512]{1,0:T(8,128)} %m_ref.3), custom_call_target="tpu_custom_call" | custom-call | tf_op jit(solution)/shard_map/edges/pallas_call | solution.py:61
  5.7 3.2 %collective-permute-start = (bf16[17,16,512]{2,1,0:T(8,128)(2,1)}, bf16[17,16,512]{2,1,0:T(8,128)(2,1)S(1)}, u32[]{:S(2)}, u32[]{:S(2)}) collective-permute-start(bf16[17,16,512]{2,1,0:T(8,128)(2,1)} %get-tuple-element.7), channel_id=1, source_target_pairs={{0,1},{1,2},{2,3},{3,4},{4,5},{5,6},{6,7},{7,8},{8,9},{9,10},{10,1... | collective-permute-start | bytes 835592 | tf_op jit(solution)/shard_map/ppermute | solution.py:322
  8.9 4.2 %collective-permute-start.1 = (bf16[17,16,512]{2,1,0:T(8,128)(2,1)}, bf16[17,16,512]{2,1,0:T(8,128)(2,1)S(1)}, u32[]{:S(2)}, u32[]{:S(2)}) collective-permute-start(bf16[17,16,512]{2,1,0:T(8,128)(2,1)} %get-tuple-element.8), channel_id=1, source_target_pairs={{1,0},{2,1},{3,2},{4,3},{5,4},{6,5},{7,6},{8,7},{9,8},{10,9},{11,1... | collective-permute-start | bytes 835592 | tf_op jit(solution)/shard_map/ppermute | solution.py:323
  13.2 0.6 add_convert_fusion.flags_ref
  13.7 3.7 %collective-permute-done.low_ref = bf16[17,16,512]{2,1,0:T(8,128)(2,1)S(1)} collective-permute-done((bf16[17,16,512]{2,1,0:T(8,128)(2,1)}, bf16[17,16,512]{2,1,0:T(8,128)(2,1)S(1)}, u32[]{:S(2)}, u32[]{:S(2)}) %collective-permute-start) | collective-permute-done | bytes 278560 | tf_op jit(solution)/shard_map/ppermute | solution.py:322
  17.5 0.0 copy-start.4
  17.5 1.0 collective-permute-done.1.high_ref
  18.4 0.0 copy-done.4
  18.4 0.0 copy-start.5
  18.4 0.7 copy-done.5
  19.2 17.4 %forecast.1 = bf16[16,8,16,512]{3,2,1,0:T(8,128)(2,1)} custom-call(s32[2]{0:T(128)} %add_convert_fusion.flags_ref, bf16[16,8,16,512]{3,2,1,0:T(8,128)(2,1)} %state_ref.3, f32[16,512]{1,0:T(8,128)} %s_ref.3, f32[16,512]{1,0:T(8,128)} %z_ref.3, f32[16,512]{1,0:T(8,128)} %m_ref.3, bf16[17,16,512]{2,1,0:T(8,128)(2,1)} %copy-done.4, bf16[17,16,512]{2,1,0:T(8,128)(2,1)} %copy-done.5), custom_call_target="tpu_custom_call" | custom-call | tf_op jit(solution)/shard_map/forecast/pallas_call | solution.py:136
  36.6 0.0 copy-start
  36.6 0.0 copy-start.1
  36.6 0.0 copy-start.2
  36.6 0.0 copy-start.3
  36.6 61.5 %all_to_all.10.x_ref = bf16[16,8,16,512]{3,2,1,0:T(8,128)(2,1)S(1)} all-to-all(bf16[16,8,16,512]{3,2,1,0:T(8,128)(2,1)} %forecast.1), channel_id=1, replica_groups=mesh['member'=16,'domain'=16] {'member'}, dimensions={0} | all-to-all | bytes 4194304 | tf_op jit(solution)/shard_map/all_to_all | solution.py:326
  98.1 0.0 copy-done
  98.1 0.0 copy-done.1
  98.1 0.0 copy-done.2
  98.1 0.0 copy-done.3
  98.1 6.1 %analysis.1 = bf16[16,8,16,512]{3,2,1,0:T(8,128)(2,1)S(1)} custom-call(s32[1,4]{1,0:T(1,128)S(1)} %copy-done.3, bf16[16,8,16,512]{3,2,1,0:T(8,128)(2,1)S(1)} %all_to_all.10.x_ref, s32[4,128]{1,0:T(4,128)S(1)} %bitcast.5, f32[4,128]{1,0:T(4,128)S(1)} %bitcast.6, f32[4,128]{1,0:T(4,128)S(1)} %bitcast.7), custom_call_target="tpu_custom_call" | custom-call | tf_op jit(solution)/shard_map/analysis/pallas_call | solution.py:288
  104.3 53.8 %all_to_all.11.x_ref = bf16[16,8,16,512]{3,2,1,0:T(8,128)(2,1)} all-to-all(bf16[16,8,16,512]{3,2,1,0:T(8,128)(2,1)S(1)} %analysis.1), channel_id=1, replica_groups=mesh['member'=16,'domain'=16] {'member'}, dimensions={0} | all-to-all | bytes 4194304 | tf_op jit(solution)/shard_map/all_to_all | solution.py:328
  158.0 6.4 %result.1 = bf16[16,8,16,512]{3,2,1,0:T(8,128)(2,1)} custom-call(bf16[16,8,16,512]{3,2,1,0:T(8,128)(2,1)} %all_to_all.11.x_ref), custom_call_target="tpu_custom_call" | custom-call | tf_op jit(solution)/shard_map/result/pallas_call | solution.py:306
Async XLA Ops:
  5.7 11.7 %collective-permute-start = (bf16[17,16,512]{2,1,0:T(8,128)(2,1)}, bf16[17,16,512]{2,1,0:T(8,128)(2,1)S(1)}, u32[]{:S(2)}, u32[]{:S(2)}) collective-permute-start(bf16[17,16,512]{2,1,0:T(8,128)(2,1)} %get-tuple-element.7), channel_id=1, source_target_pairs={{0,1},{1,2},{2,3},{3,4},{4,5},{5,6},{6,7},{7,8},{8,9},{9,10},{10,1... | collective-permute-start | bytes 835592 | tf_op jit(solution)/shard_map/ppermute | solution.py:322
  8.9 9.5 %collective-permute-start.1 = (bf16[17,16,512]{2,1,0:T(8,128)(2,1)}, bf16[17,16,512]{2,1,0:T(8,128)(2,1)S(1)}, u32[]{:S(2)}, u32[]{:S(2)}) collective-permute-start(bf16[17,16,512]{2,1,0:T(8,128)(2,1)} %get-tuple-element.8), channel_id=1, source_target_pairs={{1,0},{2,1},{3,2},{4,3},{5,4},{6,5},{7,6},{8,7},{9,8},{10,9},{11,1... | collective-permute-start | bytes 835592 | tf_op jit(solution)/shard_map/ppermute | solution.py:323
  17.5 1.0 copy-start.4
  18.4 0.7 copy-start.5
  36.6 61.5 %copy-start = (s32[1,4,128]{2,1,0:T(4,128)S(1)}, s32[1,4,128]{2,1,0:T(4,128)}, u32[]{:S(2)}) copy-start(s32[1,4,128]{2,1,0:T(4,128)} %param.13) | copy-start | bytes 6148
  36.6 61.5 %copy-start.1 = (f32[1,4,128]{2,1,0:T(4,128)S(1)}, f32[1,4,128]{2,1,0:T(4,128)}, u32[]{:S(2)}) copy-start(f32[1,4,128]{2,1,0:T(4,128)} %param.14) | copy-start | bytes 6148
  36.6 61.5 %copy-start.2 = (f32[1,4,128]{2,1,0:T(4,128)S(1)}, f32[1,4,128]{2,1,0:T(4,128)}, u32[]{:S(2)}) copy-start(f32[1,4,128]{2,1,0:T(4,128)} %param.15) | copy-start | bytes 6148
  36.6 61.5 %copy-start.3 = (s32[1,4]{1,0:T(1,128)S(1)}, s32[1,4]{1,0:T(1,128)}, u32[]{:S(2)}) copy-start(s32[1,4]{1,0:T(1,128)} %count_ref.1) | copy-start | bytes 52
where the time goes:
time: 166 us; the launch traced here: 164 us
  blocking collectives  115 us (69%)
  Pallas kernels  35.7 us (22%)
  starting transfers between devices  7.38 us (4%)
  waiting for transfers between devices  4.7 us (3%)
    all_to_all x1, blocking collectives, shards(): lax.all_to_all(grown, 'member', split_axis=0, concat_axis=0, tiled=True)  61.5 us
    all_to_all x1, blocking collectives, shards(): lax.all_to_all(analysed, 'member', split_axis=0, concat_axis=0, tiled=True)  53.8 us
    pallas_call x1, Pallas kernels, forecast(): pl.pallas_call(forecast_kernel, grid=(8,), in_specs=[pl.BlockSpec(memory_...  17.4 us
    pallas_call x1, Pallas kernels, result(): pl.pallas_call(result_kernel, grid=(8,), in_specs=[spec], out_specs=spec,...  6.4 us
    pallas_call x1, Pallas kernels, analysis(): pl.pallas_call(analysis_kernel, in_specs=[pl.BlockSpec(memory_space=pltpu...  6.14 us
    pallas_call x1, Pallas kernels, edges(): pl.pallas_call(edges_kernel, grid=(8,), in_specs=[pl.BlockSpec((16, 1, 16...  5.75 us
    ppermute x1, starting transfers between devices, shards(): high = lax.ppermute(south, 'domain', down)  4.19 us
    ppermute x1, waiting for transfers between devices, shards(): low = lax.ppermute(north, 'domain', up)  3.73 us
  transfers between devices with their start and end apart: 2, of which 2 were waited for; matrix products, arithmetic and copies ran while one was open for 0% of the time, Pallas kernels for 0%

commit v1 on v0

v1 whole, which is shorter than its diff:
```python
import functools
import math

import jax
import jax.numpy as jnp
from jax import lax
from jax.experimental import pallas as pl
from jax.experimental.pallas import tpu as pltpu
from jax.sharding import PartitionSpec as P

ITERS = 6
F32 = jnp.float32
BF16 = jnp.bfloat16


def halves(x):
    high = x.astype(BF16)
    return high, (x - high.astype(F32)).astype(BF16)


def thirds(x):
    high = x.astype(BF16)
    rest = x - high.astype(F32)
    mid = rest.astype(BF16)
    return high, mid, (rest - mid.astype(F32)).astype(BF16)


def dot(a, b):
    return jnp.dot(a, b, preferred_element_type=F32)


ORDER = (3, 5, 2, 6, 4, 1, 7, 0)
BACK = tuple(ORDER.index((8 - d) % 8) for d in ORDER)
PIECE = (2, 8, 16, 256)
FIELDS = 4


def row_picker(rows, first_row):
    out = lax.broadcasted_iota(jnp.int32, (rows * 16, 256), 0)
    src = lax.broadcasted_iota(jnp.int32, (rows * 16, 256), 1)
    row = (out >> 4) + first_row
    hit = jnp.logical_and((src & 15) == row, (src >> 4) == (out & 15))
    return hit.astype(F32).astype(BF16)


def place():
    member = lax.axis_index("member")
    return member >> 1, member & 1


def coefficients(s, z, m):
    return (1.0 - 4.0 * s, s - 0.5 * z, s + 0.5 * z, s - 0.5 * m, s + 0.5 * m)


def step_row(centre, north, south, coef):
    east = pltpu.roll(centre, 511, 1)
    west = pltpu.roll(centre, 1, 1)
    c, e, w, n, so = coef
    return centre * c + east * e + west * w + north * n + south * so


def forecast_rows(edge, own_ref, sib_ref, numbers, halo_ref, outs, pick, coef, fields, middle, ready):
    step = pl.program_id(0)
    z, c = place()
    base = 12 * c - 2 if edge else 2 + 4 * c

    @pl.when(step == 0)
    def _():
        pick[...] = row_picker(8, base)
        for j in range(6):
            row = jnp.clip(base + 1 + j, 0, 15)
            for k, value in enumerate(coefficients(*[ref[pl.ds(row, 1)] for ref in numbers])):
                coef[k, j] = jnp.broadcast_to(value, (8, 512))
        if edge:
            part = halo_ref[8, 0].astype(F32)
            rows = [part[3 * k : 3 * k + 1] + part[3 * k + 1 : 3 * k + 2] + part[3 * k + 2 : 3 * k + 3] for k in range(3)]
            for k, value in enumerate(coefficients(*rows)):
                coef[k, 5 * c] = jnp.broadcast_to(value, (8, 512))

    if edge:
        domain = lax.axis_index("domain")
        outside = jnp.where(c == 0, domain == 0, domain == lax.axis_size("domain") - 1)

    def coef_at(j):
        return [jnp.concatenate([coef[k, j]] * 4, axis=0) for k in range(5)]

    def one_field(f, carry):
        fields[:, :16] = dot(pick[...], own_ref[:, f].reshape(256, 512)).reshape(8, 16, 512)
        fields[:, 16:] = dot(pick[...], sib_ref[:, f].reshape(256, 512)).reshape(8, 16, 512)
        if edge:
            fields[pl.ds(6 * c, 2)] = halo_ref[FIELDS * step + f].astype(F32)
        for j in range(6):
            value = step_row(fields[j + 1], fields[j + 2], fields[j], coef_at(j))
            middle[j] = value.astype(BF16).astype(F32)
        if edge:

            @pl.when(outside)
            def _():
                middle[5 * c] = jnp.zeros((32, 512), F32)

        for j in range(4):
            value = step_row(middle[j + 1], middle[j + 2], middle[j], coef_at(j + 1)).astype(BF16)
            ready[2 * j] = value[:, :256]
            ready[2 * j + 1] = value[:, 256:]
        for k, out_ref in enumerate(outs):
            out_ref[:, f] = ready[(z + ORDER[k]) & 7].reshape(2, 16, 256)
        return carry

    lax.fori_loop(0, FIELDS, one_field, 0)


def inner_kernel(own_ref, sib_ref, s_ref, z_ref, m_ref, *rest):
    outs, halo_ref, scratch = rest[:8], rest[8], rest[9:]
    step = pl.program_id(0)
    numbers = (s_ref, z_ref, m_ref)
    forecast_rows(False, own_ref, sib_ref, numbers, None, outs, *scratch[:5])
    pick = scratch[5]
    _, c = place()

    @pl.when(step == 0)
    def _():
        pick[...] = row_picker(2, 14 * c)
        parts = []
        for ref in numbers:
            parts += list(thirds(ref[pl.ds(15 * c, 1)]))
        parts.append(jnp.zeros((23, 512), BF16))
        halo_ref[8, 0] = jnp.concatenate(parts, axis=0)
        halo_ref[8, 1] = jnp.zeros((32, 512), BF16)

    def one_field(f, carry):
        own = dot(pick[...], own_ref[:, f].reshape(256, 512)).astype(BF16)
        sib = dot(pick[...], sib_ref[:, f].reshape(256, 512)).astype(BF16)
        halo_ref[FIELDS * step + f, :, :16] = sib.reshape(2, 16, 512)
        halo_ref[FIELDS * step + f, :, 16:] = own.reshape(2, 16, 512)
        return carry

    lax.fori_loop(0, FIELDS, one_field, 0)


def edge_kernel(own_ref, sib_ref, s_ref, z_ref, m_ref, halo_ref, *rest):
    forecast_rows(True, own_ref, sib_ref, (s_ref, z_ref, m_ref), halo_ref, rest[:8], *rest[8:])


FORECAST_SCRATCH = (
    ((128, 256), BF16),
    ((5, 6, 8, 512), F32),
    ((8, 32, 512), F32),
    ((6, 32, 512), F32),
    ((8, 32, 256), BF16),
)


def forecast(own, sib, numbers, halo=None):
    block = pl.BlockSpec((16, FIELDS, 16, 512), lambda f: (0, f, 0, 0))
    whole = pl.BlockSpec((16, 512), lambda f: (0, 0))
    halo_spec = pl.BlockSpec((9, 2, 32, 512), lambda f: (0, 0, 0, 0))
    piece = pl.BlockSpec((2, FIELDS, 16, 256), lambda f: (0, f, 0, 0))
    pieces = [jax.ShapeDtypeStruct(PIECE, BF16)] * 8
    scratch = [pltpu.VMEM(*s) for s in FORECAST_SCRATCH]
    cost = pl.CostEstimate(flops=300_000_000, bytes_accessed=6_000_000, transcendentals=0)
    if halo is None:
        return pl.pallas_call(
            inner_kernel,
            grid=(8 // FIELDS,),
            in_specs=[block, block, whole, whole, whole],
            out_specs=[piece] * 8 + [halo_spec],
            out_shape=pieces + [jax.ShapeDtypeStruct((9, 2, 32, 512), BF16)],
            scratch_shapes=scratch + [pltpu.VMEM((32, 256), BF16)],
            cost_estimate=cost,
            name="inner_forecast",
        )(own, sib, *numbers)
    return pl.pallas_call(
        edge_kernel,
        grid=(8 // FIELDS,),
        in_specs=[block, block, whole, whole, whole, halo_spec],
        out_specs=[piece] * 8,
        out_shape=pieces,
        scratch_shapes=scratch,
        cost_estimate=cost,
        name="edge_forecast",
    )(own, sib, *numbers, halo)


def left(parts):
    return jnp.concatenate(parts, axis=1)


def right(parts):
    high, low = parts
    top = jnp.concatenate([high, low], axis=1)
    bottom = jnp.concatenate([high, jnp.zeros_like(low)], axis=1)
    return jnp.concatenate([top, bottom], axis=0)


def product(a, b):
    both = dot(a, b)
    return both[:, :128] + both[:, 128:]


def weights_of(patches, members):
    spread = float(members - 1)
    rows = lax.broadcasted_iota(jnp.int32, (128, 128), 0)
    cols = lax.broadcasted_iota(jnp.int32, (128, 128), 1)
    eye = (rows == cols).astype(F32)
    work = []
    for observed, live, value, weight in patches:
        mean = jnp.sum(observed, axis=0, keepdims=True) * (1.0 / members)
        precision_w = weight * live
        root = jnp.sqrt(precision_w)
        scaled = (observed - mean) * root
        work.append({"a": scaled, "v": root * (value - mean)})
    for w in work:
        both = left(halves(w["a"]))
        gram = lax.dot_general(both, both, (((0,), (0,)), ((), ())), preferred_element_type=F32)
        w["g"] = gram[:128, :128] + gram[:128, 128:] + gram[128:, :128]
    for w in work:
        g = w["g"]
        square = jnp.sum(jnp.sum(g * g + (2.0 * spread) * (g * eye), axis=1, keepdims=True), axis=0, keepdims=True)
        scale = jnp.sqrt(square + spread * spread * members)
        inv = 1.0 / scale
        w["scale"], w["inv"] = scale, inv
        w["low"] = spread * inv
        w["y"] = g * inv + w["low"] * eye
        w["z0"] = jnp.ones((1, 1), F32)
    for sweep in range(ITERS):
        last = sweep == ITERS - 1
        for w in work:
            y = w["y"]
            y_parts = halves(y)
            y0 = w["low"] * w["z0"]
            w0 = w["z0"] * y0
            f0 = 1.5 - 0.5 * w0
            if sweep == 0:
                f = 1.5 * eye - 0.5 * y
                fq = -0.5 * eye
                w["next"] = (f, fq, f0, y_parts, None)
            else:
                zz = jnp.concatenate([left(w["z_parts"]), left(w["q_parts"])], axis=0)
                out = product(zz, right(y_parts))
                wq = out[128:] + w["z0"] * (w["low"] * w["q"] + w["z"])
                f = 1.5 * eye - 0.5 * out[:128]
                fq = -0.5 * wq
                w["next"] = (f, fq, f0, y_parts, zz)
        for w in work:
            f, fq, f0, y_parts, zz = w["next"]
            if sweep == 0:
                w["y"] = product(left(y_parts), right(halves(f)))
                w["z"], w["q"] = f, fq
            else:
                rhs = right(halves(f))
                lhs = zz if last else jnp.concatenate([zz, left(y_parts)], axis=0)
                out = product(lhs, rhs)
                w["z"] = out[:128]
                w["q"] = out[128:256] + w["z0"] * fq
                if not last:
                    w["y"] = out[256:]
            w["z0"] = w["z0"] * f0
            if not last:
                w["z_parts"], w["q_parts"] = halves(w["z"]), halves(w["q"])
    for w in work:
        z = right(halves(w["z"]))
        u = jnp.broadcast_to(w["v"], (8, 128))
        u = product(left(halves(u)), z)
        u = product(left(halves(u)), z)
        root = lax.rsqrt(w["scale"])
        w["u"] = u[:1] * root
        w["hat"] = w["a"] * root
        w["c1"] = math.sqrt(spread) * root
    big_rows = lax.broadcasted_iota(jnp.int32, (members, members), 0)
    big_cols = lax.broadcasted_iota(jnp.int32, (members, members), 1)
    big_eye = (big_rows == big_cols).astype(F32)
    result = []
    for w in work:
        hat_high, hat_low = halves(w["hat"])
        t = product(left((hat_high, hat_low)), right(halves(w["q"])))
        t = w["c1"] * t + w["u"]
        t_high, t_low = halves(t)
        nt = (((1,), (1,)), ((), ()))
        full = lax.dot_general(left((t_high, t_low)), left((hat_high, hat_high)), nt, preferred_element_type=F32)
        full = full + lax.dot_general(t_high, hat_low, nt, preferred_element_type=F32)
        result.append((full + (w["c1"] * w["z0"]) * big_eye).astype(BF16))
    return result


def selector(index_row):
    entry = lax.broadcasted_iota(jnp.int32, (1024, 128), 0)
    return (entry == index_row).astype(F32).astype(BF16)


def analysis_kernel(edge, even_ref, odd_ref, *rest):
    pieces, outs, held = rest[:8], rest[8:16], rest[16]
    z, _ = place()
    slot = lax.broadcasted_iota(jnp.int32, (1, 128), 1).astype(F32)
    for k in range(8):
        for g in range(2):
            at = k * 32 + g * 16
            for f in range(8):
                for p in range(2):
                    held[p, at : at + 16, f * 128 : (f + 1) * 128] = pieces[k][g, f, :, p * 128 : (p + 1) * 128]
    patches = []
    for p in range(2):
        patch = pl.ds(2 * (z & 1) + p, 1)
        obs = jnp.where((z & 1) == int(edge), even_ref[0, patch], odd_ref[0, patch])
        index = obs[:, :128].astype(jnp.int32)
        observed = dot(held[p], selector(index))
        live = (slot < obs[:, 384:]).astype(F32)
        patches.append((observed, live, obs[:, 128:256], obs[:, 256:384]))
    weights = weights_of(patches, 256)
    for p in range(2):
        for f in range(8):
            x = held[p, :, f * 128 : (f + 1) * 128].astype(F32)
            centre = jnp.sum(x, axis=0, keepdims=True) * (1.0 / 256)
            pert = (x - centre).astype(BF16)
            out = (dot(weights[p], pert) + centre).astype(BF16)
            for k in range(8):
                at = BACK[k] * 32
                outs[k][:, f, :, p * 128 : (p + 1) * 128] = out[at : at + 32].reshape(2, 16, 128)


def analysis(edge, obs, pieces):
    vmem = pl.BlockSpec(memory_space=pltpu.VMEM)
    return pl.pallas_call(
        functools.partial(analysis_kernel, edge),
        in_specs=[vmem] * 10,
        out_specs=[vmem] * 8,
        out_shape=[jax.ShapeDtypeStruct(PIECE, BF16)] * 8,
        scratch_shapes=[pltpu.VMEM((2, 256, 1024), BF16)],
        compiler_params=pltpu.CompilerParams(vmem_limit_bytes=40 * 1024 * 1024),
        cost_estimate=pl.CostEstimate(flops=2_000_000_000, bytes_accessed=6_000_000, transcendentals=0),
        name="edge_analysis" if edge else "inner_analysis",
    )(*obs, *pieces)


def pack_kernel(*refs):
    z, _ = place()
    for k in range(8):
        refs[8][(z - ORDER[k]) & 7] = refs[k][0]


def pack(pieces, name):
    return pl.pallas_call(
        pack_kernel,
        grid=(1,),
        in_specs=[pl.BlockSpec((1, 8, 16, 256), lambda i: (1, 0, 0, 0))] * 8,
        out_specs=pl.BlockSpec((8, 8, 16, 256), lambda i: (0, 0, 0, 0)),
        out_shape=jax.ShapeDtypeStruct((8, 8, 16, 256), BF16),
        name=name,
    )(*pieces)


def result_kernel(*refs):
    mine, theirs, out_ref, pick, rows = refs[:16], refs[16:18], refs[18], refs[19], refs[20]
    z, c = place()

    @pl.when(pl.program_id(0) == 0)
    def _():
        pick[...] = row_picker(16, 0)

    def one_field(f, carry):
        for chunk in range(2):
            own_base = 12 * c if chunk else 4 + 4 * c
            sib_base = 12 - 12 * c if chunk else 8 - 4 * c
            for k in range(8):
                rows[2 * own_base + ((z - ORDER[k]) & 7)] = mine[8 * chunk + k][0, f]
            for source in range(8):
                rows[2 * sib_base + source] = theirs[chunk][source, f]
        both = rows[...].reshape(16, 2, 16, 256)
        for h in range(2):
            out = dot(pick[...], both[:, h].reshape(256, 256)).astype(BF16)
            out_ref[:, f, :, h * 256 : (h + 1) * 256] = out.reshape(16, 16, 256)
        return carry

    lax.fori_loop(0, FIELDS, one_field, 0)


def result(mine, theirs):
    own = pl.BlockSpec((1, FIELDS, 16, 256), lambda f: (0, f, 0, 0))
    sib = pl.BlockSpec((8, FIELDS, 16, 256), lambda f: (0, f, 0, 0))
    return pl.pallas_call(
        result_kernel,
        grid=(8 // FIELDS,),
        in_specs=[own] * 16 + [sib] * 2,
        out_specs=pl.BlockSpec((16, FIELDS, 16, 512), lambda f: (0, f, 0, 0)),
        out_shape=jax.ShapeDtypeStruct((16, 8, 16, 512), BF16),
        scratch_shapes=[pltpu.VMEM((256, 256), BF16), pltpu.VMEM((32, 16, 256), BF16)],
        name="result",
    )(*mine, *theirs)


def obs_pairs():
    def target(row, odd):
        return 2 * (2 * (row % 4) + odd) + row // 8

    inner = range(4, 12)
    first = [(row, target(row, int(row not in inner))) for row in range(16)]
    return first, [(row, target(row, int(row in inner))) for row in range(16)]


def swap(x):
    return lax.ppermute(x, "member", [(i, i ^ 1) for i in range(16)])


def around(x, distance):
    return lax.ppermute(x, "member", [(i, (i + 2 * distance) % 16) for i in range(16)])


def exchange(pieces):
    return [around(x, d) if d else x for x, d in zip(pieces, ORDER)]


def shards(state, s, z, m, obs_count, obs_index, obs_value, obs_weight):
    numbers = (s, z, m)
    count = jnp.broadcast_to(obs_count[:, :, None], obs_index.shape)
    obs = jnp.concatenate([obs_index.astype(F32), obs_value, obs_weight, count.astype(F32)], axis=2)
    sib = swap(state)
    obs = [lax.ppermute(obs, "member", pairs) for pairs in obs_pairs()]
    *inner, halo = forecast(state, sib, numbers)
    domains = lax.axis_size("domain")
    pairs = []
    for chip in range(8):
        for d in range(domains - 1):
            pairs.append(((2 * chip + 1) * domains + d, 2 * chip * domains + d + 1))
            pairs.append((2 * chip * domains + d + 1, (2 * chip + 1) * domains + d))
    inner = exchange(inner)
    halo = lax.ppermute(halo, ("member", "domain"), pairs)
    outer = exchange(forecast(state, sib, numbers, halo))
    inner = exchange(analysis(False, obs, inner))
    inner_sib = swap(pack(inner, "inner_pack"))
    outer = exchange(analysis(True, obs, outer))
    outer_sib = swap(pack(outer, "edge_pack"))
    return result(inner + outer, [inner_sib, outer_sib])


def solution(mesh):
    placed = (
        P("member", None, "domain", None),
        P("domain", None),
        P("domain", None),
        P("domain", None),
        P(("domain", "member"), None),
        P(("domain", "member"), None, None),
        P(("domain", "member"), None, None),
        P(("domain", "member"), None, None),
    )
    return jax.shard_map(
        shards,
        mesh=mesh,
        in_specs=placed,
        out_specs=P("member", None, "domain", None),
        check_vma=False,
    )
```

time: 166 us -> 141 us (0.85)
  blocking collectives: 115 us -> 0 us
  starting transfers between devices: 7.38 us -> 80.8 us
  waiting for transfers between devices: 4.7 us -> 20.3 us
  local copies, waits for them, and re-layouts: 0.73 us -> 4.25 us
    all_to_all x2 -> x0, blocking collectives: 115 us -> none  [the longest x1 61.5 us: shards(): lax.all_to_all(grown, 'member', split_axis=0, concat_axis=0, tiled=True)]
    ppermute x2 -> x34, starting transfers between devices: 7.38 us -> 80.8 us  [the longest x28 52.4 us: around(): lax.ppermute(x, 'member', [(i, (i + 2 * distance) % 16) for i in range(16)])]
    ppermute x2 -> x34, waiting for transfers between devices: 4.7 us -> 20.3 us  [the longest x28 14.6 us: around(): lax.ppermute(x, 'member', [(i, (i + 2 * distance) % 16) for i in range(16)])]
    unnamed x12 -> x58, local copies, waits for them, and re-layouts: 0.73 us -> 4.18 us
    pallas_call x4 -> x7, Pallas kernels: 35.7 us -> 34.2 us  [the longest x1 9.06 us: forecast(): pl.pallas_call(inner_kernel, grid=(8 // FIELDS,), in_specs=[block, block,...]
  transfers between devices with their start and end apart: 2 -> 34, of which waited for: 2 -> 8; matrix products, arithmetic and copies ran while one was open for 0% -> 0% of each run, Pallas kernels for 0% -> 15%
where the time goes in v1:
time: 141 us; the launch traced here: 140 us
  starting transfers between devices  80.8 us (57%)
  Pallas kernels  34.2 us (24%)
  waiting for transfers between devices  20.3 us (14%)
  local copies, waits for them, and re-layouts  4.25 us (3%)
    ppermute x28, starting transfers between devices, around(): lax.ppermute(x, 'member', [(i, (i + 2 * distance) % 16) for i in range(16)])  52.4 us
    ppermute x28, waiting for transfers between devices, around(): lax.ppermute(x, 'member', [(i, (i + 2 * distance) % 16) for i in range(16)])  14.6 us
    ppermute x3, starting transfers between devices, swap(): return lax.ppermute(x, 'member', [(i, i ^ 1) for i in range(16)])  14.3 us
    ppermute x2, starting transfers between devices, shards(): obs = [lax.ppermute(obs, 'member', pairs) for pairs in obs_pairs()]  10.7 us
    pallas_call x1, Pallas kernels, forecast(): pl.pallas_call(inner_kernel, grid=(8 // FIELDS,), in_specs=[block, block,...  9.06 us
    pallas_call x2, Pallas kernels, analysis(): pl.pallas_call(functools.partial(analysis_kernel, edge), in_specs=[vmem]...  8.41 us
    pallas_call x1, Pallas kernels, forecast(): pl.pallas_call(edge_kernel, grid=(8 // FIELDS,), in_specs=[block, block,...  8.4 us
    ppermute x3, waiting for transfers between devices, swap(): return lax.ppermute(x, 'member', [(i, i ^ 1) for i in range(16)])  5.74 us
  transfers between devices with their start and end apart: 34, of which 8 were waited for; matrix products, arithmetic and copies ran while one was open for 0% of the time, Pallas kernels for 15%

profile of v1, /device:TPU:7, one launch (start us, length us, event | category | flops | bytes accessed | tf_op | source)
XLA Modules:
  0.0 140.1 jit_solution(7207132821799293155)
XLA Ops:
  0.8 4.0 %collective-permute-done.2.sib_ref = bf16[16,8,16,512]{3,2,1,0:T(8,128)(2,1)S(1)} collective-permute-done((bf16[16,8,16,512]{3,2,1,0:T(8,128)(2,1)}, bf16[16,8,16,512]{3,2,1,0:T(8,128)(2,1)S(1)}, u32[]{:S(2)}, u32[]{:S(2)}) %collective-permute-start.2) | collective-permute-done | bytes 2097184 | tf_op jit(solution)/shard_map/ppermute | solution.py:400
  6.1 9.1 %inner_forecast.1 = (bf16[2,8,16,256]{3,2,1,0:T(8,128)(2,1)}, bf16[2,8,16,256]{3,2,1,0:T(8,128)(2,1)}, bf16[2,8,16,256]{3,2,1,0:T(8,128)(2,1)}, bf16[2,8,16,256]...) custom-call(bf16[16,8,16,512]{3,2,1,0:T(8,128)(2,1)} %own_ref.3, ...), custom_call_target="tpu_custom_call" | custom-call | flops 300000000 | bytes 6000000 | tf_op jit(solution)/shard_map/inner_forecast/pallas_call | solution.py:162
  15.2 3.5 %collective-permute-start.17 = (bf16[9,2,32,512]{3,2,1,0:T(8,128)(2,1)}, bf16[9,2,32,512]{3,2,1,0:T(8,128)(2,1)S(1)}, u32[]{:S(2)}, u32[]{:S(2)}) collective-permute-start(bf16[9,2,32,512]{3,2,1,0:T(8,128)(2,1)} %get-tuple-element.54), channel_id=1, source_target_pairs={{16,1},{1,16},{17,2},{2,17},{18,3},{3,18},{19,4},{4,19},{20,5},{5,... | collective-permute-start | bytes 1769480 | tf_op jit(solution)/shard_map/ppermute | solution.py:425
  18.8 8.0 %collective-permute-start = (f32[1,4,512]{2,1,0:T(4,128)S(1)}, f32[1,4,512]{2,1,0:T(4,128)S(1)}, u32[]{:S(2)}, u32[]{:S(2)}) collective-permute-start(f32[1,4,512]{2,1,0:T(4,128)S(1)} %pad_maximum_fusion), channel_id=1, source_target_pairs={{0,32},{16,96},{32,160},{48,224},{64,0},{80,64},{96,128},{112,192}... | collective-permute-start | bytes 24584 | tf_op jit(solution)/shard_map/ppermute | solution.py:416
  26.8 3.8 %collective-permute-start.3 = (bf16[2,8,16,256]{3,2,1,0:T(8,128)(2,1)}, bf16[2,8,16,256]{3,2,1,0:T(8,128)(2,1)S(1)}, u32[]{:S(2)}, u32[]{:S(2)}) collective-permute-start(bf16[2,8,16,256]{3,2,1,0:T(8,128)(2,1)} %get-tuple-element.38), channel_id=1, source_target_pairs={{0,96},{16,112},{32,128},{48,144},{64,160},{80,176},{96,192},{112,... | collective-permute-start | bytes 393224 | tf_op jit(solution)/shard_map/ppermute | solution.py:404
  31.4 3.6 %collective-permute-start.6 = (bf16[2,8,16,256]{3,2,1,0:T(8,128)(2,1)}, bf16[2,8,16,256]{3,2,1,0:T(8,128)(2,1)S(1)}, u32[]{:S(2)}, u32[]{:S(2)}) collective-permute-start(bf16[2,8,16,256]{3,2,1,0:T(8,128)(2,1)} %get-tuple-element.41), channel_id=1, source_target_pairs={{0,192},{16,208},{32,224},{48,240},{64,0},{80,16},{96,32},{112,48}... | collective-permute-start | bytes 393224 | tf_op jit(solution)/shard_map/ppermute | solution.py:404
  35.0 2.7 %collective-permute-start.1 = (f32[1,4,512]{2,1,0:T(4,128)S(1)}, f32[1,4,512]{2,1,0:T(4,128)S(1)}, u32[]{:S(2)}, u32[]{:S(2)}) collective-permute-start(f32[1,4,512]{2,1,0:T(4,128)S(1)} %pad_maximum_fusion), channel_id=1, source_target_pairs={{0,0},{16,64},{32,128},{48,192},{64,32},{80,96},{96,160},{112,224}... | collective-permute-start | bytes 24584 | tf_op jit(solution)/shard_map/ppermute | solution.py:416
  37.7 8.4 %edge_forecast.1 = (bf16[2,8,16,256]{3,2,1,0:T(8,128)(2,1)}, bf16[2,8,16,256]{3,2,1,0:T(8,128)(2,1)}, bf16[2,8,16,256]{3,2,1,0:T(8,128)(2,1)}, bf16[2,8,16,256]{...) custom-call(bf16[16,8,16,512]{3,2,1,0:T(8,128)(2,1)} %own_ref.3, ...), custom_call_target="tpu_custom_call" | custom-call | flops 300000000 | bytes 6000000 | tf_op jit(solution)/shard_map/edge_forecast/pallas_call | solution.py:172
  46.2 4.6 %collective-permute-start.7 = (bf16[2,8,16,256]{3,2,1,0:T(8,128)(2,1)S(1)}, bf16[2,8,16,256]{3,2,1,0:T(8,128)(2,1)S(1)}, u32[]{:S(2)}, u32[]{:S(2)}) collective-permute-start(bf16[2,8,16,256]{3,2,1,0:T(8,128)(2,1)S(1)} %copy-done.27), channel_id=1, source_target_pairs={{0,128},{16,144},{32,160},{48,176},{64,192},{80,208},{96,224},{112... | collective-permute-start | bytes 393224 | tf_op jit(solution)/shard_map/ppermute | solution.py:404
  50.8 3.6 %collective-permute-start.9 = (bf16[2,8,16,256]{3,2,1,0:T(8,128)(2,1)S(1)}, bf16[2,8,16,256]{3,2,1,0:T(8,128)(2,1)S(1)}, u32[]{:S(2)}, u32[]{:S(2)}) collective-permute-start(bf16[2,8,16,256]{3,2,1,0:T(8,128)(2,1)S(1)} %copy-done.25), channel_id=1, source_target_pairs={{0,224},{16,240},{32,0},{48,16},{64,32},{80,48},{96,64},{112,80},{... | collective-permute-start | bytes 393224 | tf_op jit(solution)/shard_map/ppermute | solution.py:404
  54.3 4.5 %collective-permute-start.19 = (bf16[2,8,16,256]{3,2,1,0:T(8,128)(2,1)}, bf16[2,8,16,256]{3,2,1,0:T(8,128)(2,1)S(1)}, u32[]{:S(2)}, u32[]{:S(2)}) collective-permute-start(bf16[2,8,16,256]{3,2,1,0:T(8,128)(2,1)} %get-tuple-element.56), channel_id=1, source_target_pairs={{0,160},{16,176},{32,192},{48,208},{64,224},{80,240},{96,0},{112,1... | collective-permute-start | bytes 393224 | tf_op jit(solution)/shard_map/ppermute | solution.py:404
  58.9 3.2 %collective-permute-done.8.rest_5_ = bf16[2,8,16,256]{3,2,1,0:T(8,128)(2,1)S(1)} collective-permute-done((bf16[2,8,16,256]{3,2,1,0:T(8,128)(2,1)S(1)}, bf16[2,8,16,256]{3,2,1,0:T(8,128)(2,1)S(1)}, u32[]{:S(2)}, u32[]{:S(2)}) %collective-permute-start.8) | collective-permute-done | bytes 131104 | tf_op jit(solution)/shard_map/ppermute | solution.py:404
  64.0 4.3 %collective-permute-done.18.rest_0_ = bf16[2,8,16,256]{3,2,1,0:T(8,128)(2,1)S(1)} collective-permute-done((bf16[2,8,16,256]{3,2,1,0:T(8,128)(2,1)}, bf16[2,8,16,256]{3,2,1,0:T(8,128)(2,1)S(1)}, u32[]{:S(2)}, u32[]{:S(2)}) %collective-permute-start.18) | collective-permute-done | bytes 131104 | tf_op jit(solution)/shard_map/ppermute | solution.py:404
  68.3 3.7 %collective-permute-start.24 = (bf16[2,8,16,256]{3,2,1,0:T(8,128)(2,1)}, bf16[2,8,16,256]{3,2,1,0:T(8,128)(2,1)S(1)}, u32[]{:S(2)}, u32[]{:S(2)}) collective-permute-start(bf16[2,8,16,256]{3,2,1,0:T(8,128)(2,1)} %get-tuple-element.61), channel_id=1, source_target_pairs={{0,224},{16,240},{32,0},{48,16},{64,32},{80,48},{96,64},{112,80},{... | collective-permute-start | bytes 393224 | tf_op jit(solution)/shard_map/ppermute | solution.py:404
  72.0 4.2 %inner_analysis.1 = (bf16[2,8,16,256]{3,2,1,0:T(8,128)(2,1)S(1)}, bf16[2,8,16,256]{3,2,1,0:T(8,128)(2,1)S(1)}, bf16[2,8,16,256]{3,2,1,0:T(8,128)(2,1)S(1)}, bf16...) custom-call(f32[1,4,512]{2,1,0:T(4,128)S(1)} %collective-permute-don, ...), custom_call_target="tpu_custom_call" | custom-call | flops 2000000000 | bytes 6000000 | tf_op jit(solution)/shard_map/inner_analysis/pallas_call | solution.py:322
  78.6 2.8 %collective-permute-start.11 = (bf16[2,8,16,256]{3,2,1,0:T(8,128)(2,1)S(1)}, bf16[2,8,16,256]{3,2,1,0:T(8,128)(2,1)S(1)}, u32[]{:S(2)}, u32[]{:S(2)}) collective-permute-start(bf16[2,8,16,256]{3,2,1,0:T(8,128)(2,1)S(1)} %get-tuple-element.47), channel_id=1, source_target_pairs={{0,160},{16,176},{32,192},{48,208},{64,224},{80,240},{96,0},{112,1... | collective-permute-start | bytes 393224 | tf_op jit(solution)/shard_map/ppermute | solution.py:404
  85.5 3.0 %collective-permute-start.14 = (bf16[2,8,16,256]{3,2,1,0:T(8,128)(2,1)S(1)}, bf16[2,8,16,256]{3,2,1,0:T(8,128)(2,1)S(1)}, u32[]{:S(2)}, u32[]{:S(2)}) collective-permute-start(bf16[2,8,16,256]{3,2,1,0:T(8,128)(2,1)S(1)} %get-tuple-element.50), channel_id=1, source_target_pairs={{0,128},{16,144},{32,160},{48,176},{64,192},{80,208},{96,224},{112... | collective-permute-start | bytes 393224 | tf_op jit(solution)/shard_map/ppermute | solution.py:404
  88.6 4.2 %edge_analysis.1 = (bf16[2,8,16,256]{3,2,1,0:T(8,128)(2,1)S(1)}, bf16[2,8,16,256]{3,2,1,0:T(8,128)(2,1)S(1)}, bf16[2,8,16,256]{3,2,1,0:T(8,128)(2,1)S(1)}, bf16[...) custom-call(f32[1,4,512]{2,1,0:T(4,128)S(1)} %collective-permute-don, ...), custom_call_target="tpu_custom_call" | custom-call | flops 2000000000 | bytes 6000000 | tf_op jit(solution)/shard_map/edge_analysis/pallas_call | solution.py:322
  97.7 4.1 %collective-permute-start.26 = (bf16[2,8,16,256]{3,2,1,0:T(8,128)(2,1)S(1)}, bf16[2,8,16,256]{3,2,1,0:T(8,128)(2,1)S(1)}, u32[]{:S(2)}, u32[]{:S(2)}) collective-permute-start(bf16[2,8,16,256]{3,2,1,0:T(8,128)(2,1)S(1)} %get-tuple-element.64), channel_id=1, source_target_pairs={{0,160},{16,176},{32,192},{48,208},{64,224},{80,240},{96,0},{112,1... | collective-permute-start | bytes 393224 | tf_op jit(solution)/shard_map/ppermute | solution.py:404
  103.0 3.5 %collective-permute-done.15.refs_5_ = bf16[2,8,16,256]{3,2,1,0:T(8,128)(2,1)S(1)} collective-permute-done((bf16[2,8,16,256]{3,2,1,0:T(8,128)(2,1)S(1)}, bf16[2,8,16,256]{3,2,1,0:T(8,128)(2,1)S(1)}, u32[]{:S(2)}, u32[]{:S(2)}) %collective-permute-start.15) | collective-permute-done | bytes 131104 | tf_op jit(solution)/shard_map/ppermute | solution.py:404
  107.5 2.8 %collective-permute-start.29 = (bf16[2,8,16,256]{3,2,1,0:T(8,128)(2,1)S(1)}, bf16[2,8,16,256]{3,2,1,0:T(8,128)(2,1)S(1)}, u32[]{:S(2)}, u32[]{:S(2)}) collective-permute-start(bf16[2,8,16,256]{3,2,1,0:T(8,128)(2,1)S(1)} %get-tuple-element.67), channel_id=1, source_target_pairs={{0,128},{16,144},{32,160},{48,176},{64,192},{80,208},{96,224},{112... | collective-permute-start | bytes 393224 | tf_op jit(solution)/shard_map/ppermute | solution.py:404
  115.0 11.2 %collective-permute-start.32 = (bf16[8,8,16,256]{3,2,1,0:T(8,128)(2,1)}, bf16[8,8,16,256]{3,2,1,0:T(8,128)(2,1)S(1)}, u32[]{:S(2)}, u32[]{:S(2)}) collective-permute-start(bf16[8,8,16,256]{3,2,1,0:T(8,128)(2,1)} %inner_pack.1), channel_id=1, source_target_pairs={{0,16},{16,0},{32,48},{48,32},{64,80},{80,64},{96,112},{112,96},{1... | collective-permute-start | bytes 1572872 | tf_op jit(solution)/shard_map/ppermute | solution.py:400
  130.5 2.3 %collective-permute-start.33 = (bf16[8,8,16,256]{3,2,1,0:T(8,128)(2,1)}, bf16[8,8,16,256]{3,2,1,0:T(8,128)(2,1)S(1)}, u32[]{:S(2)}, u32[]{:S(2)}) collective-permute-start(bf16[8,8,16,256]{3,2,1,0:T(8,128)(2,1)} %edge_pack.1), channel_id=1, source_target_pairs={{0,16},{16,0},{32,48},{48,32},{64,80},{80,64},{96,112},{112,96},{1... | collective-permute-start | bytes 1572872 | tf_op jit(solution)/shard_map/ppermute | solution.py:400
  135.4 4.5 %result.1 = bf16[16,8,16,512]{3,2,1,0:T(8,128)(2,1)} custom-call(bf16[2,8,16,256]{3,2,1,0:T(8,128)(2,1)} %copy-done.8, bf16[2,8,16,256]{3,2,1,0:T(8,128)(2,1)} %copy-done.9, bf16[2,8,16,256]{3,2,1,0:T(8,128)(2,1)} %copy-done.10, bf16[2,8,16,256]{3,2,1,0:T(8,128)(2,1)} %copy-done.11, bf16[2,8,16,256]{3,2,1,0:T(8,128)(2,1)} %copy-done.12, ...), custom_call_target="tpu_custom_call" | custom-call | tf_op jit(solution)/shard_map/result/pallas_call | solution.py:379
  (113 shorter events, 30.2 us)
Async XLA Ops:
  15.2 19.8 %collective-permute-start.17 = (bf16[9,2,32,512]{3,2,1,0:T(8,128)(2,1)}, bf16[9,2,32,512]{3,2,1,0:T(8,128)(2,1)S(1)}, u32[]{:S(2)}, u32[]{:S(2)}) collective-permute-start(bf16[9,2,32,512]{3,2,1,0:T(8,128)(2,1)} %get-tuple-element.54), channel_id=1, source_target_pairs={{16,1},{1,16},{17,2},{2,17},{18,3},{3,18},{19,4},{4,19},{20,5},{5,... | collective-permute-start | bytes 1769480 | tf_op jit(solution)/shard_map/ppermute | solution.py:425
  26.8 23.9 %collective-permute-start.3 = (bf16[2,8,16,256]{3,2,1,0:T(8,128)(2,1)}, bf16[2,8,16,256]{3,2,1,0:T(8,128)(2,1)S(1)}, u32[]{:S(2)}, u32[]{:S(2)}) collective-permute-start(bf16[2,8,16,256]{3,2,1,0:T(8,128)(2,1)} %get-tuple-element.38), channel_id=1, source_target_pairs={{0,96},{16,112},{32,128},{48,144},{64,160},{80,176},{96,192},{112,... | collective-permute-start | bytes 393224 | tf_op jit(solution)/shard_map/ppermute | solution.py:404
  30.6 20.2 %collective-permute-start.4 = (bf16[2,8,16,256]{3,2,1,0:T(8,128)(2,1)}, bf16[2,8,16,256]{3,2,1,0:T(8,128)(2,1)S(1)}, u32[]{:S(2)}, u32[]{:S(2)}) collective-permute-start(bf16[2,8,16,256]{3,2,1,0:T(8,128)(2,1)} %get-tuple-element.39), channel_id=1, source_target_pairs={{0,160},{16,176},{32,192},{48,208},{64,224},{80,240},{96,0},{112,1... | collective-permute-start | bytes 393224 | tf_op jit(solution)/shard_map/ppermute | solution.py:404
  31.3 23.0 %collective-permute-start.5 = (bf16[2,8,16,256]{3,2,1,0:T(8,128)(2,1)}, bf16[2,8,16,256]{3,2,1,0:T(8,128)(2,1)S(1)}, u32[]{:S(2)}, u32[]{:S(2)}) collective-permute-start(bf16[2,8,16,256]{3,2,1,0:T(8,128)(2,1)} %get-tuple-element.40), channel_id=1, source_target_pairs={{0,64},{16,80},{32,96},{48,112},{64,128},{80,144},{96,160},{112,17... | collective-permute-start | bytes 393224 | tf_op jit(solution)/shard_map/ppermute | solution.py:404
  31.4 23.0 %collective-permute-start.6 = (bf16[2,8,16,256]{3,2,1,0:T(8,128)(2,1)}, bf16[2,8,16,256]{3,2,1,0:T(8,128)(2,1)S(1)}, u32[]{:S(2)}, u32[]{:S(2)}) collective-permute-start(bf16[2,8,16,256]{3,2,1,0:T(8,128)(2,1)} %get-tuple-element.41), channel_id=1, source_target_pairs={{0,192},{16,208},{32,224},{48,240},{64,0},{80,16},{96,32},{112,48}... | collective-permute-start | bytes 393224 | tf_op jit(solution)/shard_map/ppermute | solution.py:404
  54.3 14.0 %collective-permute-start.18 = (bf16[2,8,16,256]{3,2,1,0:T(8,128)(2,1)}, bf16[2,8,16,256]{3,2,1,0:T(8,128)(2,1)S(1)}, u32[]{:S(2)}, u32[]{:S(2)}) collective-permute-start(bf16[2,8,16,256]{3,2,1,0:T(8,128)(2,1)} %get-tuple-element.55), channel_id=1, source_target_pairs={{0,96},{16,112},{32,128},{48,144},{64,160},{80,176},{96,192},{112,... | collective-permute-start | bytes 393224 | tf_op jit(solution)/shard_map/ppermute | solution.py:404
  54.3 14.0 %collective-permute-start.19 = (bf16[2,8,16,256]{3,2,1,0:T(8,128)(2,1)}, bf16[2,8,16,256]{3,2,1,0:T(8,128)(2,1)S(1)}, u32[]{:S(2)}, u32[]{:S(2)}) collective-permute-start(bf16[2,8,16,256]{3,2,1,0:T(8,128)(2,1)} %get-tuple-element.56), channel_id=1, source_target_pairs={{0,160},{16,176},{32,192},{48,208},{64,224},{80,240},{96,0},{112,1... | collective-permute-start | bytes 393224 | tf_op jit(solution)/shard_map/ppermute | solution.py:404
  58.8 18.1 %collective-permute-start.20 = (bf16[2,8,16,256]{3,2,1,0:T(8,128)(2,1)}, bf16[2,8,16,256]{3,2,1,0:T(8,128)(2,1)S(1)}, u32[]{:S(2)}, u32[]{:S(2)}) collective-permute-start(bf16[2,8,16,256]{3,2,1,0:T(8,128)(2,1)} %get-tuple-element.57), channel_id=1, source_target_pairs={{0,64},{16,80},{32,96},{48,112},{64,128},{80,144},{96,160},{112,17... | collective-permute-start | bytes 393224 | tf_op jit(solution)/shard_map/ppermute | solution.py:404
  62.0 16.6 %collective-permute-start.21 = (bf16[2,8,16,256]{3,2,1,0:T(8,128)(2,1)}, bf16[2,8,16,256]{3,2,1,0:T(8,128)(2,1)S(1)}, u32[]{:S(2)}, u32[]{:S(2)}) collective-permute-start(bf16[2,8,16,256]{3,2,1,0:T(8,128)(2,1)} %get-tuple-element.58), channel_id=1, source_target_pairs={{0,192},{16,208},{32,224},{48,240},{64,0},{80,16},{96,32},{112,48}... | collective-permute-start | bytes 393224 | tf_op jit(solution)/shard_map/ppermute | solution.py:404
  62.4 19.0 %collective-permute-start.22 = (bf16[2,8,16,256]{3,2,1,0:T(8,128)(2,1)}, bf16[2,8,16,256]{3,2,1,0:T(8,128)(2,1)S(1)}, u32[]{:S(2)}, u32[]{:S(2)}) collective-permute-start(bf16[2,8,16,256]{3,2,1,0:T(8,128)(2,1)} %get-tuple-element.59), channel_id=1, source_target_pairs={{0,128},{16,144},{32,160},{48,176},{64,192},{80,208},{96,224},{112... | collective-permute-start | bytes 393224 | tf_op jit(solution)/shard_map/ppermute | solution.py:404
  68.3 15.1 %collective-permute-start.23 = (bf16[2,8,16,256]{3,2,1,0:T(8,128)(2,1)}, bf16[2,8,16,256]{3,2,1,0:T(8,128)(2,1)S(1)}, u32[]{:S(2)}, u32[]{:S(2)}) collective-permute-start(bf16[2,8,16,256]{3,2,1,0:T(8,128)(2,1)} %get-tuple-element.60), channel_id=1, source_target_pairs={{0,32},{16,48},{32,64},{48,80},{64,96},{80,112},{96,128},{112,144}... | collective-permute-start | bytes 393224 | tf_op jit(solution)/shard_map/ppermute | solution.py:404
  68.3 17.2 %collective-permute-start.24 = (bf16[2,8,16,256]{3,2,1,0:T(8,128)(2,1)}, bf16[2,8,16,256]{3,2,1,0:T(8,128)(2,1)S(1)}, u32[]{:S(2)}, u32[]{:S(2)}) collective-permute-start(bf16[2,8,16,256]{3,2,1,0:T(8,128)(2,1)} %get-tuple-element.61), channel_id=1, source_target_pairs={{0,224},{16,240},{32,0},{48,16},{64,32},{80,48},{96,64},{112,80},{... | collective-permute-start | bytes 393224 | tf_op jit(solution)/shard_map/ppermute | solution.py:404
  76.9 16.5 %collective-permute-start.10 = (bf16[2,8,16,256]{3,2,1,0:T(8,128)(2,1)S(1)}, bf16[2,8,16,256]{3,2,1,0:T(8,128)(2,1)S(1)}, u32[]{:S(2)}, u32[]{:S(2)}) collective-permute-start(bf16[2,8,16,256]{3,2,1,0:T(8,128)(2,1)S(1)} %get-tuple-element.46), channel_id=1, source_target_pairs={{0,96},{16,112},{32,128},{48,144},{64,160},{80,176},{96,192},{112,... | collective-permute-start | bytes 393224 | tf_op jit(solution)/shard_map/ppermute | solution.py:404
  78.6 16.7 %collective-permute-start.11 = (bf16[2,8,16,256]{3,2,1,0:T(8,128)(2,1)S(1)}, bf16[2,8,16,256]{3,2,1,0:T(8,128)(2,1)S(1)}, u32[]{:S(2)}, u32[]{:S(2)}) collective-permute-start(bf16[2,8,16,256]{3,2,1,0:T(8,128)(2,1)S(1)} %get-tuple-element.47), channel_id=1, source_target_pairs={{0,160},{16,176},{32,192},{48,208},{64,224},{80,240},{96,0},{112,1... | collective-permute-start | bytes 393224 | tf_op jit(solution)/shard_map/ppermute | solution.py:404
  81.4 14.7 %collective-permute-start.12 = (bf16[2,8,16,256]{3,2,1,0:T(8,128)(2,1)S(1)}, bf16[2,8,16,256]{3,2,1,0:T(8,128)(2,1)S(1)}, u32[]{:S(2)}, u32[]{:S(2)}) collective-permute-start(bf16[2,8,16,256]{3,2,1,0:T(8,128)(2,1)S(1)} %get-tuple-element.48), channel_id=1, source_target_pairs={{0,64},{16,80},{32,96},{48,112},{64,128},{80,144},{96,160},{112,17... | collective-permute-start | bytes 393224 | tf_op jit(solution)/shard_map/ppermute | solution.py:404
  83.4 14.4 %collective-permute-start.13 = (bf16[2,8,16,256]{3,2,1,0:T(8,128)(2,1)S(1)}, bf16[2,8,16,256]{3,2,1,0:T(8,128)(2,1)S(1)}, u32[]{:S(2)}, u32[]{:S(2)}) collective-permute-start(bf16[2,8,16,256]{3,2,1,0:T(8,128)(2,1)S(1)} %get-tuple-element.49), channel_id=1, source_target_pairs={{0,192},{16,208},{32,224},{48,240},{64,0},{80,16},{96,32},{112,48}... | collective-permute-start | bytes 393224 | tf_op jit(solution)/shard_map/ppermute | solution.py:404
  85.5 16.3 %collective-permute-start.14 = (bf16[2,8,16,256]{3,2,1,0:T(8,128)(2,1)S(1)}, bf16[2,8,16,256]{3,2,1,0:T(8,128)(2,1)S(1)}, u32[]{:S(2)}, u32[]{:S(2)}) collective-permute-start(bf16[2,8,16,256]{3,2,1,0:T(8,128)(2,1)S(1)} %get-tuple-element.50), channel_id=1, source_target_pairs={{0,128},{16,144},{32,160},{48,176},{64,192},{80,208},{96,224},{112... | collective-permute-start | bytes 393224 | tf_op jit(solution)/shard_map/ppermute | solution.py:404
  96.1 14.1 %collective-permute-start.25 = (bf16[2,8,16,256]{3,2,1,0:T(8,128)(2,1)S(1)}, bf16[2,8,16,256]{3,2,1,0:T(8,128)(2,1)S(1)}, u32[]{:S(2)}, u32[]{:S(2)}) collective-permute-start(bf16[2,8,16,256]{3,2,1,0:T(8,128)(2,1)S(1)} %get-tuple-element.63), channel_id=1, source_target_pairs={{0,96},{16,112},{32,128},{48,144},{64,160},{80,176},{96,192},{112,... | collective-permute-start | bytes 393224 | tf_op jit(solution)/shard_map/ppermute | solution.py:404
  97.7 14.5 %collective-permute-start.26 = (bf16[2,8,16,256]{3,2,1,0:T(8,128)(2,1)S(1)}, bf16[2,8,16,256]{3,2,1,0:T(8,128)(2,1)S(1)}, u32[]{:S(2)}, u32[]{:S(2)}) collective-permute-start(bf16[2,8,16,256]{3,2,1,0:T(8,128)(2,1)S(1)} %get-tuple-element.64), channel_id=1, source_target_pairs={{0,160},{16,176},{32,192},{48,208},{64,224},{80,240},{96,0},{112,1... | collective-permute-start | bytes 393224 | tf_op jit(solution)/shard_map/ppermute | solution.py:404
  106.5 19.7 %collective-permute-start.28 = (bf16[2,8,16,256]{3,2,1,0:T(8,128)(2,1)S(1)}, bf16[2,8,16,256]{3,2,1,0:T(8,128)(2,1)S(1)}, u32[]{:S(2)}, u32[]{:S(2)}) collective-permute-start(bf16[2,8,16,256]{3,2,1,0:T(8,128)(2,1)S(1)} %get-tuple-element.66), channel_id=1, source_target_pairs={{0,192},{16,208},{32,224},{48,240},{64,0},{80,16},{96,32},{112,48}... | collective-permute-start | bytes 393224 | tf_op jit(solution)/shard_map/ppermute | solution.py:404
  107.5 18.7 %collective-permute-start.29 = (bf16[2,8,16,256]{3,2,1,0:T(8,128)(2,1)S(1)}, bf16[2,8,16,256]{3,2,1,0:T(8,128)(2,1)S(1)}, u32[]{:S(2)}, u32[]{:S(2)}) collective-permute-start(bf16[2,8,16,256]{3,2,1,0:T(8,128)(2,1)S(1)} %get-tuple-element.67), channel_id=1, source_target_pairs={{0,128},{16,144},{32,160},{48,176},{64,192},{80,208},{96,224},{112... | collective-permute-start | bytes 393224 | tf_op jit(solution)/shard_map/ppermute | solution.py:404
  110.2 17.7 %collective-permute-start.30 = (bf16[2,8,16,256]{3,2,1,0:T(8,128)(2,1)S(1)}, bf16[2,8,16,256]{3,2,1,0:T(8,128)(2,1)S(1)}, u32[]{:S(2)}, u32[]{:S(2)}) collective-permute-start(bf16[2,8,16,256]{3,2,1,0:T(8,128)(2,1)S(1)} %get-tuple-element.68), channel_id=1, source_target_pairs={{0,32},{16,48},{32,64},{48,80},{64,96},{80,112},{96,128},{112,144}... | collective-permute-start | bytes 393224 | tf_op jit(solution)/shard_map/ppermute | solution.py:404
  112.2 15.7 %collective-permute-start.31 = (bf16[2,8,16,256]{3,2,1,0:T(8,128)(2,1)S(1)}, bf16[2,8,16,256]{3,2,1,0:T(8,128)(2,1)S(1)}, u32[]{:S(2)}, u32[]{:S(2)}) collective-permute-start(bf16[2,8,16,256]{3,2,1,0:T(8,128)(2,1)S(1)} %get-tuple-element.69), channel_id=1, source_target_pairs={{0,224},{16,240},{32,0},{48,16},{64,32},{80,48},{96,64},{112,80},{... | collective-permute-start | bytes 393224 | tf_op jit(solution)/shard_map/ppermute | solution.py:404
  115.0 17.9 %collective-permute-start.32 = (bf16[8,8,16,256]{3,2,1,0:T(8,128)(2,1)}, bf16[8,8,16,256]{3,2,1,0:T(8,128)(2,1)S(1)}, u32[]{:S(2)}, u32[]{:S(2)}) collective-permute-start(bf16[8,8,16,256]{3,2,1,0:T(8,128)(2,1)} %inner_pack.1), channel_id=1, source_target_pairs={{0,16},{16,0},{32,48},{48,32},{64,80},{80,64},{96,112},{112,96},{1... | collective-permute-start | bytes 1572872 | tf_op jit(solution)/shard_map/ppermute | solution.py:400
  (39 other events, 444.1 us)

commit v2 on v1

--- a/solution.py
+++ b/solution.py
@@ -32,7 +32,6 @@
 ORDER = (3, 5, 2, 6, 4, 1, 7, 0)
 BACK = tuple(ORDER.index((8 - d) % 8) for d in ORDER)
 PIECE = (2, 8, 16, 256)
-FIELDS = 4
 
 
 def row_picker(rows, first_row):
@@ -59,126 +58,186 @@
     return centre * c + east * e + west * w + north * n + south * so
 
 
-def forecast_rows(edge, own_ref, sib_ref, numbers, halo_ref, outs, pick, coef, fields, middle, ready):
-    step = pl.program_id(0)
+def two_steps(rows_at, coef_at, outside, groups, middle, ready):
+    coefs = [coef_at(j) for j in range(6)]
+    rows = [rows_at(j) for j in range(8)]
+    for j in range(6):
+        value = step_row(rows[j + 1], rows[j + 2], rows[j], coefs[j])
+        middle[j] = value.astype(BF16).astype(F32)
+    if outside is not None:
+        beyond, at = outside
+
+        @pl.when(beyond)
+        def _():
+            middle[at] = jnp.zeros((16 * groups, 512), F32)
+
+    for j in range(4):
+        value = step_row(middle[j + 1], middle[j + 2], middle[j], coefs[j + 1]).astype(BF16)
+        ready[2 * j] = value[:, :256]
+        ready[2 * j + 1] = value[:, 256:]
+
+
+def put_coef(coef, j, numbers):
+    for k, value in enumerate(coefficients(*numbers)):
+        coef[k, j] = jnp.broadcast_to(value, (8, 512))
+
+
+def inner_field(pick, flat, c, coef, fields, middle, ready):
+    picked = dot(pick[...], flat)
+    fields[...] = picked[:128].reshape(8, 16, 512)
+    two_steps(
+        lambda j: fields[j],
+        lambda j: [jnp.concatenate([coef[k, j]] * 2, axis=0) for k in range(5)],
+        None,
+        1,
+        middle,
+        ready,
+    )
+    return picked[128:].astype(BF16).reshape(2, 16, 512)
+
+
+def own_kernel(own_ref, numbers, inner_coef, edge_coef, part_ref, halo_ref, pick, fields, middle, ready):
     z, c = place()
-    base = 12 * c - 2 if edge else 2 + 4 * c
-
-    @pl.when(step == 0)
-    def _():
-        pick[...] = row_picker(8, base)
-        for j in range(6):
-            row = jnp.clip(base + 1 + j, 0, 15)
-            for k, value in enumerate(coefficients(*[ref[pl.ds(row, 1)] for ref in numbers])):
-                coef[k, j] = jnp.broadcast_to(value, (8, 512))
-        if edge:
-            part = halo_ref[8, 0].astype(F32)
-            rows = [part[3 * k : 3 * k + 1] + part[3 * k + 1 : 3 * k + 2] + part[3 * k + 2 : 3 * k + 3] for k in range(3)]
-            for k, value in enumerate(coefficients(*rows)):
-                coef[k, 5 * c] = jnp.broadcast_to(value, (8, 512))
-
-    if edge:
-        domain = lax.axis_index("domain")
-        outside = jnp.where(c == 0, domain == 0, domain == lax.axis_size("domain") - 1)
-
-    def coef_at(j):
-        return [jnp.concatenate([coef[k, j]] * 4, axis=0) for k in range(5)]
+    pick[:128] = row_picker(8, 2 + 4 * c)
+    pick[128:] = row_picker(2, 14 * c)
+
+    def number_rows(row):
+        return [numbers[i, pl.ds(row, 1)] for i in range(3)]
+
+    for j in range(6):
+        put_coef(inner_coef, j, number_rows(3 + 4 * c + j))
+        put_coef(edge_coef, j, number_rows(jnp.clip(12 * c - 1 + j, 0, 15)))
+    parts = []
+    for value in number_rows(15 * c):
+        parts += list(thirds(value))
+    parts.append(jnp.zeros((7, 512), BF16))
+    halo_ref[8, 0] = jnp.concatenate(parts, axis=0)
+    halo_ref[8, 1] = jnp.zeros((16, 512), BF16)
+
+    def one_field(f, carry):
+        flat = own_ref[:, f].reshape(256, 512)
+        halo_ref[f] = inner_field(pick, flat, c, inner_coef, fields, middle, ready)
+        for k in range(8):
+            part_ref[k, f] = ready[(z + ORDER[k]) & 7]
+        return carry
+
+    lax.fori_loop(0, 8, one_field, 0)
+
+
+def sib_kernel(sib_ref, coef, part_ref, own_halo_ref, *rest):
+    outs, halo_ref = rest[:8], rest[8]
+    pick, fields, middle, ready = rest[9:]
+    z, c = place()
+    pick[:128] = row_picker(8, 2 + 4 * c)
+    pick[128:] = row_picker(2, 14 * c)
+
+    def one_field(f, carry):
+        flat = sib_ref[:, f].reshape(256, 512)
+        halo_ref[f, :, :16] = inner_field(pick, flat, c, coef, fields, middle, ready)
+        halo_ref[f, :, 16:] = own_halo_ref[f]
+        for k, out_ref in enumerate(outs):
+            out_ref[0, f] = part_ref[k, f]
+            out_ref[1, f] = ready[(z + ORDER[k]) & 7]
+        return carry
+
+    lax.fori_loop(0, 8, one_field, 0)
+    halo_ref[8, :, :16] = own_halo_ref[8]
+    halo_ref[8, :, 16:] = jnp.zeros((2, 16, 512), BF16)
+
+
+def edge_kernel(own_ref, sib_ref, coef_ref, halo_ref, *rest):
+    outs = rest[:8]
+    pick, coef, fields, middle, ready = rest[8:]
+    z, c = place()
+    pick[...] = row_picker(8, 12 * c - 2)
+    coef[...] = coef_ref[...]
+    part = halo_ref[8, 0].astype(F32)
+    put_coef(coef, 5 * c, [part[3 * k : 3 * k + 1] + part[3 * k + 1 : 3 * k + 2] + part[3 * k + 2 : 3 * k + 3] for k in range(3)])
+    domain = lax.axis_index("domain")
+    outside = jnp.where(c == 0, domain == 0, domain == lax.axis_size("domain") - 1)
 
     def one_field(f, carry):
         fields[:, :16] = dot(pick[...], own_ref[:, f].reshape(256, 512)).reshape(8, 16, 512)
         fields[:, 16:] = dot(pick[...], sib_ref[:, f].reshape(256, 512)).reshape(8, 16, 512)
-        if edge:
-            fields[pl.ds(6 * c, 2)] = halo_ref[FIELDS * step + f].astype(F32)
-        for j in range(6):
-            value = step_row(fields[j + 1], fields[j + 2], fields[j], coef_at(j))
-            middle[j] = value.astype(BF16).astype(F32)
-        if edge:
-
-            @pl.when(outside)
-            def _():
-                middle[5 * c] = jnp.zeros((32, 512), F32)
-
-        for j in range(4):
-            value = step_row(middle[j + 1], middle[j + 2], middle[j], coef_at(j + 1)).astype(BF16)
-            ready[2 * j] = value[:, :256]
-            ready[2 * j + 1] = value[:, 256:]
+        fields[pl.ds(6 * c, 2)] = halo_ref[f].astype(F32)
+        two_steps(
+            lambda j: fields[j],
+            lambda j: [jnp.concatenate([coef[k, j]] * 4, axis=0) for k in range(5)],
+            (outside, 5 * c),
+            2,
+            middle,
+            ready,
+        )
         for k, out_ref in enumerate(outs):
             out_ref[:, f] = ready[(z + ORDER[k]) & 7].reshape(2, 16, 256)
         return carry
 
-    lax.fori_loop(0, FIELDS, one_field, 0)
-
-
-def inner_kernel(own_ref, sib_ref, s_ref, z_ref, m_ref, *rest):
-    outs, halo_ref, scratch = rest[:8], rest[8], rest[9:]
-    step = pl.program_id(0)
-    numbers = (s_ref, z_ref, m_ref)
-    forecast_rows(False, own_ref, sib_ref, numbers, None, outs, *scratch[:5])
-    pick = scratch[5]
-    _, c = place()
-
-    @pl.when(step == 0)
-    def _():
-        pick[...] = row_picker(2, 14 * c)
-        parts = []
-        for ref in numbers:
-            parts += list(thirds(ref[pl.ds(15 * c, 1)]))
-        parts.append(jnp.zeros((23, 512), BF16))
-        halo_ref[8, 0] = jnp.concatenate(parts, axis=0)
-        halo_ref[8, 1] = jnp.zeros((32, 512), BF16)
-
-    def one_field(f, carry):
-        own = dot(pick[...], own_ref[:, f].reshape(256, 512)).astype(BF16)
-        sib = dot(pick[...], sib_ref[:, f].reshape(256, 512)).astype(BF16)
-        halo_ref[FIELDS * step + f, :, :16] = sib.reshape(2, 16, 512)
-        halo_ref[FIELDS * step + f, :, 16:] = own.reshape(2, 16, 512)
-        return carry
-
-    lax.fori_loop(0, FIELDS, one_field, 0)
-
-
-def edge_kernel(own_ref, sib_ref, s_ref, z_ref, m_ref, halo_ref, *rest):
-    forecast_rows(True, own_ref, sib_ref, (s_ref, z_ref, m_ref), halo_ref, rest[:8], *rest[8:])
-
-
-FORECAST_SCRATCH = (
-    ((128, 256), BF16),
-    ((5, 6, 8, 512), F32),
-    ((8, 32, 512), F32),
-    ((6, 32, 512), F32),
-    ((8, 32, 256), BF16),
-)
-
-
-def forecast(own, sib, numbers, halo=None):
-    block = pl.BlockSpec((16, FIELDS, 16, 512), lambda f: (0, f, 0, 0))
-    whole = pl.BlockSpec((16, 512), lambda f: (0, 0))
-    halo_spec = pl.BlockSpec((9, 2, 32, 512), lambda f: (0, 0, 0, 0))
-    piece = pl.BlockSpec((2, FIELDS, 16, 256), lambda f: (0, f, 0, 0))
-    pieces = [jax.ShapeDtypeStruct(PIECE, BF16)] * 8
-    scratch = [pltpu.VMEM(*s) for s in FORECAST_SCRATCH]
-    cost = pl.CostEstimate(flops=300_000_000, bytes_accessed=6_000_000, transcendentals=0)
-    if halo is None:
-        return pl.pallas_call(
-            inner_kernel,
-            grid=(8 // FIELDS,),
-            in_specs=[block, block, whole, whole, whole],
-            out_specs=[piece] * 8 + [halo_spec],
-            out_shape=pieces + [jax.ShapeDtypeStruct((9, 2, 32, 512), BF16)],
-            scratch_shapes=scratch + [pltpu.VMEM((32, 256), BF16)],
-            cost_estimate=cost,
-            name="inner_forecast",
-        )(own, sib, *numbers)
+    lax.fori_loop(0, 8, one_field, 0)
+
+
+VMEM = pl.BlockSpec(memory_space=pltpu.VMEM)
+ANY = pl.BlockSpec(memory_space=pl.ANY)
+LIMIT = pltpu.CompilerParams(vmem_limit_bytes=40 * 1024 * 1024)
+
+
+def cost(flops, transfer):
+    return pl.CostEstimate(flops=flops, bytes_accessed=transfer, transcendentals=0)
+
+
+def own_forecast(own, numbers):
+    shapes = [((5, 6, 8, 512), F32)] * 2 + [((8, 8, 16, 256), BF16), ((9, 2, 16, 512), BF16)]
+    return pl.pallas_call(
+        own_kernel,
+        in_specs=[VMEM] * 2,
+        out_specs=[VMEM] * 4,
+        out_shape=[jax.ShapeDtypeStruct(*shape) for shape in shapes],
+        scratch_shapes=[
+            pltpu.VMEM((160, 256), BF16),
+            pltpu.VMEM((8, 16, 512), F32),
+            pltpu.VMEM((6, 16, 512), F32),
+            pltpu.VMEM((8, 16, 256), BF16),
+        ],
+        compiler_params=LIMIT,
+        cost_estimate=cost(300_000_000, 6_000_000),
+        name="own_forecast",
+    )(own, numbers)
+
+
+def sib_forecast(sib, coef, part, halo):
+    return pl.pallas_call(
+        sib_kernel,
+        in_specs=[VMEM] * 4,
+        out_specs=[VMEM] * 9,
+        out_shape=[jax.ShapeDtypeStruct(PIECE, BF16)] * 8 + [jax.ShapeDtypeStruct((9, 2, 32, 512), BF16)],
+        scratch_shapes=[
+            pltpu.VMEM((160, 256), BF16),
+            pltpu.VMEM((8, 16, 512), F32),
+            pltpu.VMEM((6, 16, 512), F32),
+            pltpu.VMEM((8, 16, 256), BF16),
+        ],
+        compiler_params=LIMIT,
+        cost_estimate=cost(300_000_000, 6_000_000),
+        name="sib_forecast",
+    )(sib, coef, part, halo)
+
+
+def edge_forecast(own, sib, coef, halo):
     return pl.pallas_call(
         edge_kernel,
-        grid=(8 // FIELDS,),
-        in_specs=[block, block, whole, whole, whole, halo_spec],
-        out_specs=[piece] * 8,
-        out_shape=pieces,
-        scratch_shapes=scratch,
-        cost_estimate=cost,
+        in_specs=[VMEM] * 4,
+        out_specs=[VMEM] * 8,
+        out_shape=[jax.ShapeDtypeStruct(PIECE, BF16)] * 8,
+        scratch_shapes=[
+            pltpu.VMEM((128, 256), BF16),
+            pltpu.VMEM((5, 6, 8, 512), F32),
+            pltpu.VMEM((8, 32, 512), F32),
+            pltpu.VMEM((6, 32, 512), F32),
+            pltpu.VMEM((8, 32, 256), BF16),
+        ],
+        compiler_params=LIMIT,
+        cost_estimate=cost(300_000_000, 6_000_000),
         name="edge_forecast",
-    )(own, sib, *numbers, halo)
+    )(own, sib, coef, halo)
 
 
 def left(parts):
@@ -300,11 +359,11 @@
     patches = []
     for p in range(2):
         patch = pl.ds(2 * (z & 1) + p, 1)
-        obs = jnp.where((z & 1) == int(edge), even_ref[0, patch], odd_ref[0, patch])
-        index = obs[:, :128].astype(jnp.int32)
-        observed = dot(held[p], selector(index))
-        live = (slot < obs[:, 384:]).astype(F32)
-        patches.append((observed, live, obs[:, 128:256], obs[:, 256:384]))
+        index, value, weight, count = [
+            jnp.where((z & 1) == int(edge), even_ref[0, i, patch], odd_ref[0, i, patch]) for i in range(4)
+        ]
+        observed = dot(held[p], selector(index.astype(jnp.int32)))
+        patches.append((observed, (slot < count).astype(F32), value, weight))
     weights = weights_of(patches, 256)
     for p in range(2):
         for f in range(8):
@@ -318,15 +377,14 @@
 
 
 def analysis(edge, obs, pieces):
-    vmem = pl.BlockSpec(memory_space=pltpu.VMEM)
     return pl.pallas_call(
         functools.partial(analysis_kernel, edge),
-        in_specs=[vmem] * 10,
-        out_specs=[vmem] * 8,
+        in_specs=[VMEM] * 10,
+        out_specs=[VMEM] * 8,
         out_shape=[jax.ShapeDtypeStruct(PIECE, BF16)] * 8,
         scratch_shapes=[pltpu.VMEM((2, 256, 1024), BF16)],
-        compiler_params=pltpu.CompilerParams(vmem_limit_bytes=40 * 1024 * 1024),
-        cost_estimate=pl.CostEstimate(flops=2_000_000_000, bytes_accessed=6_000_000, transcendentals=0),
+        compiler_params=LIMIT,
+        cost_estimate=cost(2_000_000_000, 6_000_000),
         name="edge_analysis" if edge else "inner_analysis",
     )(*obs, *pieces)
 
@@ -334,27 +392,27 @@
 def pack_kernel(*refs):
     z, _ = place()
     for k in range(8):
-        refs[8][(z - ORDER[k]) & 7] = refs[k][0]
+        refs[8][(z - ORDER[k]) & 7] = refs[k][1]
 
 
 def pack(pieces, name):
     return pl.pallas_call(
         pack_kernel,
-        grid=(1,),
-        in_specs=[pl.BlockSpec((1, 8, 16, 256), lambda i: (1, 0, 0, 0))] * 8,
-        out_specs=pl.BlockSpec((8, 8, 16, 256), lambda i: (0, 0, 0, 0)),
+        in_specs=[VMEM] * 8,
+        out_specs=VMEM,
+        compiler_params=LIMIT,
         out_shape=jax.ShapeDtypeStruct((8, 8, 16, 256), BF16),
         name=name,
     )(*pieces)
 
 
 def result_kernel(*refs):
-    mine, theirs, out_ref, pick, rows = refs[:16], refs[16:18], refs[18], refs[19], refs[20]
+    mine, theirs, out_ref, pick, rows, ready, sent = refs[:16], refs[16:18], refs[18], refs[19], refs[20], refs[21], refs[22]
     z, c = place()
-
-    @pl.when(pl.program_id(0) == 0)
-    def _():
-        pick[...] = row_picker(16, 0)
+    pick[...] = row_picker(16, 0)
+
+    def send(f):
+        return pltpu.make_async_copy(ready.at[f], out_ref.at[:, f], sent.at[f])
 
     def one_field(f, carry):
         for chunk in range(2):
@@ -367,22 +425,31 @@
         both = rows[...].reshape(16, 2, 16, 256)
         for h in range(2):
             out = dot(pick[...], both[:, h].reshape(256, 256)).astype(BF16)
-            out_ref[:, f, :, h * 256 : (h + 1) * 256] = out.reshape(16, 16, 256)
+            ready[f, :, :, h * 256 : (h + 1) * 256] = out.reshape(16, 16, 256)
+        send(f).start()
         return carry
 
-    lax.fori_loop(0, FIELDS, one_field, 0)
+    def finish(f, carry):
+        send(f).wait()
+        return carry
+
+    lax.fori_loop(0, 8, one_field, 0)
+    lax.fori_loop(0, 8, finish, 0)
 
 
 def result(mine, theirs):
-    own = pl.BlockSpec((1, FIELDS, 16, 256), lambda f: (0, f, 0, 0))
-    sib = pl.BlockSpec((8, FIELDS, 16, 256), lambda f: (0, f, 0, 0))
     return pl.pallas_call(
         result_kernel,
-        grid=(8 // FIELDS,),
-        in_specs=[own] * 16 + [sib] * 2,
-        out_specs=pl.BlockSpec((16, FIELDS, 16, 512), lambda f: (0, f, 0, 0)),
+        in_specs=[VMEM] * 18,
+        out_specs=pl.BlockSpec(memory_space=pl.ANY),
         out_shape=jax.ShapeDtypeStruct((16, 8, 16, 512), BF16),
-        scratch_shapes=[pltpu.VMEM((256, 256), BF16), pltpu.VMEM((32, 16, 256), BF16)],
+        scratch_shapes=[
+            pltpu.VMEM((256, 256), BF16),
+            pltpu.VMEM((32, 16, 256), BF16),
+            pltpu.VMEM((8, 16, 16, 512), BF16),
+            pltpu.SemaphoreType.DMA((8,)),
+        ],
+        compiler_params=LIMIT,
         name="result",
     )(*mine, *theirs)
 
@@ -409,12 +476,21 @@
 
 
 def shards(state, s, z, m, obs_count, obs_index, obs_value, obs_weight):
-    numbers = (s, z, m)
-    count = jnp.broadcast_to(obs_count[:, :, None], obs_index.shape)
-    obs = jnp.concatenate([obs_index.astype(F32), obs_value, obs_weight, count.astype(F32)], axis=2)
+    kind = lax.broadcasted_iota(jnp.int32, (1, 4, 4, 128), 1)
+    obs = jnp.where(
+        kind == 0,
+        obs_index.astype(F32)[:, None],
+        jnp.where(
+            kind == 1,
+            obs_value[:, None],
+            jnp.where(kind == 2, obs_weight[:, None], obs_count.astype(F32)[:, None, :, None]),
+        ),
+    )
+    which = lax.broadcasted_iota(jnp.int32, (3, 16, 512), 0)
+    numbers = jnp.where(which == 0, s, jnp.where(which == 1, z, m))
     sib = swap(state)
-    obs = [lax.ppermute(obs, "member", pairs) for pairs in obs_pairs()]
-    *inner, halo = forecast(state, sib, numbers)
+    inner_coef, edge_coef, part, halo = own_forecast(state, numbers)
+    *inner, halo = sib_forecast(sib, inner_coef, part, halo)
     domains = lax.axis_size("domain")
     pairs = []
     for chip in range(8):
@@ -423,7 +499,10 @@
             pairs.append((2 * chip * domains + d + 1, (2 * chip + 1) * domains + d))
     inner = exchange(inner)
     halo = lax.ppermute(halo, ("member", "domain"), pairs)
-    outer = exchange(forecast(state, sib, numbers, halo))
+    outer = edge_forecast(state, sib, edge_coef, halo)
+    first, obs = lax.optimization_barrier((outer[0], obs))
+    outer = exchange([first, *outer[1:]])
+    obs = [lax.ppermute(obs, "member", pairs) for pairs in obs_pairs()]
     inner = exchange(analysis(False, obs, inner))
     inner_sib = swap(pack(inner, "inner_pack"))
     outer = exchange(analysis(True, obs, outer))

time: 141 us -> 127 us (0.901)
  Pallas kernels: 34.2 us -> 24 us
  waiting for transfers between devices: 20.3 us -> 13.6 us
  starting transfers between devices: 80.8 us -> 86 us
  local copies, waits for them, and re-layouts: 4.25 us -> 1.62 us
    ppermute x28, starting transfers between devices: 52.4 us -> 63.5 us  [around(): lax.ppermute(x, 'member', [(i, (i + 2 * distance) % 16) for i in range(16)])]
    pallas_call x7 -> x8, Pallas kernels: 34.2 us -> 24 us  [the longest x2 8.4 us: analysis(): pl.pallas_call(functools.partial(analysis_kernel, edge), in_specs=[VMEM]...]
    ppermute x3, starting transfers between devices: 14.3 us -> 5.88 us  [swap(): return lax.ppermute(x, 'member', [(i, i ^ 1) for i in range(16)])]
    ppermute x3, waiting for transfers between devices: 5.74 us -> 1.54 us  [swap(): return lax.ppermute(x, 'member', [(i, i ^ 1) for i in range(16)])]
    ppermute x2, starting transfers between devices: 10.7 us -> 13.6 us  [shards(): obs = [lax.ppermute(obs, 'member', pairs) for pairs in obs_pairs()]]
    unnamed x58 -> x12, local copies, waits for them, and re-layouts: 4.18 us -> 1.62 us
    ppermute x28, waiting for transfers between devices: 14.6 us -> 12.1 us  [around(): lax.ppermute(x, 'member', [(i, (i + 2 * distance) % 16) for i in range(16)])]
  transfers between devices with their start and end apart: 34 -> 34, of which waited for: 8 -> 6; matrix products, arithmetic and copies ran while one was open for 0% -> 1% of each run, Pallas kernels for 15% -> 14%
where the time goes in v2:
time: 127 us
  starting transfers between devices  86 us (68%)
  Pallas kernels  24 us (19%)
  waiting for transfers between devices  13.6 us (11%)
  local copies, waits for them, and re-layouts  1.62 us (1%)
    ppermute x28, starting transfers between devices, around(): lax.ppermute(x, 'member', [(i, (i + 2 * distance) % 16) for i in range(16)])  63.5 us
    ppermute x2, starting transfers between devices, shards(): obs = [lax.ppermute(obs, 'member', pairs) for pairs in obs_pairs()]  13.6 us
    ppermute x28, waiting for transfers between devices, around(): lax.ppermute(x, 'member', [(i, (i + 2 * distance) % 16) for i in range(16)])  12.1 us
    pallas_call x2, Pallas kernels, analysis(): pl.pallas_call(functools.partial(analysis_kernel, edge), in_specs=[VMEM]...  8.4 us
    ppermute x3, starting transfers between devices, swap(): return lax.ppermute(x, 'member', [(i, i ^ 1) for i in range(16)])  5.88 us
    pallas_call x1, Pallas kernels, edge_forecast(): pl.pallas_call(edge_kernel, in_specs=[VMEM] * 4, out_specs=[VMEM] * 8, ou...  5.78 us
    pallas_call x1, Pallas kernels, own_forecast(): pl.pallas_call(own_kernel, in_specs=[VMEM] * 2, out_specs=[VMEM] * 4, out...  3.42 us
    pallas_call x1, Pallas kernels, sib_forecast(): pl.pallas_call(sib_kernel, in_specs=[VMEM] * 4, out_specs=[VMEM] * 9, out...  3.33 us
  transfers between devices with their start and end apart: 34, of which 6 were waited for; matrix products, arithmetic and copies ran while one was open for 1% of the time, Pallas kernels for 14%

profile of v2, /device:TPU:7, one launch (start us, length us, event | category | flops | bytes accessed | tf_op | source)
XLA Modules:
  0.0 126.7 jit_solution(1333371536735824932)
XLA Ops:
  3.2 3.4 %own_forecast.1 = (f32[5,6,8,512]{3,2,1,0:T(8,128)S(1)}, f32[5,6,8,512]{3,2,1,0:T(8,128)S(1)}, bf16[8,8,16,256]{3,2,1,0:T(8,128)(2,1)S(1)}, bf16[9,2,16,512]{3,2,1,0:T(8,128)(2,1)S(1)}) custom-call(bf16[16,8,16,512]{3,2,1,0:T(8,128)(2,1)S(1)} %copy-done, f32[3,16,512]{2,1,0:T(8,128)S(1)} %select_select_fusion.numbers), custom_call_target="tpu_custom_call" | custom-call | flops 300000000 | bytes 6000000 | tf_op jit(solution)/shard_map/own_forecast/pallas_call | solution.py:189
  6.7 3.3 %sib_forecast.1 = (bf16[2,8,16,256]{3,2,1,0:T(8,128)(2,1)S(1)}, bf16[2,8,16,256]{3,2,1,0:T(8,128)(2,1)S(1)}, bf16[2,8,16,256]{3,2,1,0:T(8,128)(2,1)S(1)}, bf16[2...) custom-call(bf16[16,8,16,512]{3,2,1,0:T(8,128)(2,1)S(1)} %collective, ...), custom_call_target="tpu_custom_call" | custom-call | flops 300000000 | bytes 6000000 | tf_op jit(solution)/shard_map/sib_forecast/pallas_call | solution.py:207
  10.0 3.1 %collective-permute-start.1 = (bf16[9,2,32,512]{3,2,1,0:T(8,128)(2,1)S(1)}, bf16[9,2,32,512]{3,2,1,0:T(8,128)(2,1)S(1)}, u32[]{:S(2)}, u32[]{:S(2)}) collective-permute-start(bf16[9,2,32,512]{3,2,1,0:T(8,128)(2,1)S(1)} %get-tuple-element.48), channel_id=1, source_target_pairs={{16,1},{1,16},{17,2},{2,17},{18,3},{3,18},{19,4},{4,19},{20,5},{5,... | collective-permute-start | bytes 1769480 | tf_op jit(solution)/shard_map/ppermute | solution.py:501
  13.1 4.4 %collective-permute-start.4 = (bf16[2,8,16,256]{3,2,1,0:T(8,128)(2,1)S(1)}, bf16[2,8,16,256]{3,2,1,0:T(8,128)(2,1)S(1)}, u32[]{:S(2)}, u32[]{:S(2)}) collective-permute-start(bf16[2,8,16,256]{3,2,1,0:T(8,128)(2,1)S(1)} %get-tuple-element.51), channel_id=1, source_target_pairs={{0,96},{16,112},{32,128},{48,144},{64,160},{80,176},{96,192},{112,... | collective-permute-start | bytes 393224 | tf_op jit(solution)/shard_map/ppermute | solution.py:471
  21.0 2.8 %collective-permute-start.7 = (bf16[2,8,16,256]{3,2,1,0:T(8,128)(2,1)S(1)}, bf16[2,8,16,256]{3,2,1,0:T(8,128)(2,1)S(1)}, u32[]{:S(2)}, u32[]{:S(2)}) collective-permute-start(bf16[2,8,16,256]{3,2,1,0:T(8,128)(2,1)S(1)} %get-tuple-element.54), channel_id=1, source_target_pairs={{0,192},{16,208},{32,224},{48,240},{64,0},{80,16},{96,32},{112,48}... | collective-permute-start | bytes 393224 | tf_op jit(solution)/shard_map/ppermute | solution.py:471
  23.8 6.4 %collective-permute-start.8 = (bf16[2,8,16,256]{3,2,1,0:T(8,128)(2,1)S(1)}, bf16[2,8,16,256]{3,2,1,0:T(8,128)(2,1)S(1)}, u32[]{:S(2)}, u32[]{:S(2)}) collective-permute-start(bf16[2,8,16,256]{3,2,1,0:T(8,128)(2,1)S(1)} %get-tuple-element.55), channel_id=1, source_target_pairs={{0,128},{16,144},{32,160},{48,176},{64,192},{80,208},{96,224},{112... | collective-permute-start | bytes 393224 | tf_op jit(solution)/shard_map/ppermute | solution.py:471
  32.9 5.8 %edge_forecast.1 = (bf16[2,8,16,256]{3,2,1,0:T(8,128)(2,1)S(1)}, bf16[2,8,16,256]{3,2,1,0:T(8,128)(2,1)S(1)}, bf16[2,8,16,256]{3,2,1,0:T(8,128)(2,1)S(1)}, bf16[...) custom-call(bf16[16,8,16,512]{3,2,1,0:T(8,128)(2,1)S(1)} %copy-done., ...), custom_call_target="tpu_custom_call" | custom-call | flops 300000000 | bytes 6000000 | tf_op jit(solution)/shard_map/edge_forecast/pallas_call | solution.py:225
  40.4 2.8 %collective-permute-start.19 = (bf16[2,8,16,256]{3,2,1,0:T(8,128)(2,1)S(1)}, bf16[2,8,16,256]{3,2,1,0:T(8,128)(2,1)S(1)}, u32[]{:S(2)}, u32[]{:S(2)}) collective-permute-start(bf16[2,8,16,256]{3,2,1,0:T(8,128)(2,1)S(1)} %get-tuple-element.68), channel_id=1, source_target_pairs={{0,160},{16,176},{32,192},{48,208},{64,224},{80,240},{96,0},{112,1... | collective-permute-start | bytes 393224 | tf_op jit(solution)/shard_map/ppermute | solution.py:471
  43.2 8.8 %collective-permute-start.2 = (f32[1,4,4,128]{3,2,1,0:T(4,128)S(1)}, f32[1,4,4,128]{3,2,1,0:T(4,128)S(1)}, u32[]{:S(2)}, u32[]{:S(2)}) collective-permute-start(f32[1,4,4,128]{3,2,1,0:T(4,128)S(1)} %select_select_fusion.1), channel_id=1, source_target_pairs={{0,32},{16,96},{32,160},{48,224},{64,0},{80,64},{96,128},{112,192}... | collective-permute-start | bytes 24584 | tf_op jit(solution)/shard_map/ppermute | solution.py:505
  52.0 4.8 %collective-permute-start.3 = (f32[1,4,4,128]{3,2,1,0:T(4,128)S(1)}, f32[1,4,4,128]{3,2,1,0:T(4,128)S(1)}, u32[]{:S(2)}, u32[]{:S(2)}) collective-permute-start(f32[1,4,4,128]{3,2,1,0:T(4,128)S(1)} %select_select_fusion.1), channel_id=1, source_target_pairs={{0,0},{16,64},{32,128},{48,192},{64,32},{80,96},{96,160},{112,224}... | collective-permute-start | bytes 24584 | tf_op jit(solution)/shard_map/ppermute | solution.py:505
  56.9 3.6 %collective-permute-start.21 = (bf16[2,8,16,256]{3,2,1,0:T(8,128)(2,1)S(1)}, bf16[2,8,16,256]{3,2,1,0:T(8,128)(2,1)S(1)}, u32[]{:S(2)}, u32[]{:S(2)}) collective-permute-start(bf16[2,8,16,256]{3,2,1,0:T(8,128)(2,1)S(1)} %get-tuple-element.70), channel_id=1, source_target_pairs={{0,192},{16,208},{32,224},{48,240},{64,0},{80,16},{96,32},{112,48}... | collective-permute-start | bytes 393224 | tf_op jit(solution)/shard_map/ppermute | solution.py:471
  61.5 2.7 %collective-permute-start.24 = (bf16[2,8,16,256]{3,2,1,0:T(8,128)(2,1)S(1)}, bf16[2,8,16,256]{3,2,1,0:T(8,128)(2,1)S(1)}, u32[]{:S(2)}, u32[]{:S(2)}) collective-permute-start(bf16[2,8,16,256]{3,2,1,0:T(8,128)(2,1)S(1)} %get-tuple-element.73), channel_id=1, source_target_pairs={{0,224},{16,240},{32,0},{48,16},{64,32},{80,48},{96,64},{112,80},{... | collective-permute-start | bytes 393224 | tf_op jit(solution)/shard_map/ppermute | solution.py:471
  64.1 4.2 %inner_analysis.1 = (bf16[2,8,16,256]{3,2,1,0:T(8,128)(2,1)S(1)}, bf16[2,8,16,256]{3,2,1,0:T(8,128)(2,1)S(1)}, bf16[2,8,16,256]{3,2,1,0:T(8,128)(2,1)S(1)}, bf16...) custom-call(f32[1,4,4,128]{3,2,1,0:T(4,128)S(1)} %collective-permute, ...), custom_call_target="tpu_custom_call" | custom-call | flops 2000000000 | bytes 6000000 | tf_op jit(solution)/shard_map/inner_analysis/pallas_call | solution.py:380
  70.5 2.4 %collective-permute-start.12 = (bf16[2,8,16,256]{3,2,1,0:T(8,128)(2,1)S(1)}, bf16[2,8,16,256]{3,2,1,0:T(8,128)(2,1)S(1)}, u32[]{:S(2)}, u32[]{:S(2)}) collective-permute-start(bf16[2,8,16,256]{3,2,1,0:T(8,128)(2,1)S(1)} %get-tuple-element.60), channel_id=1, source_target_pairs={{0,160},{16,176},{32,192},{48,208},{64,224},{80,240},{96,0},{112,1... | collective-permute-start | bytes 393224 | tf_op jit(solution)/shard_map/ppermute | solution.py:471
  73.9 2.6 %collective-permute-start.14 = (bf16[2,8,16,256]{3,2,1,0:T(8,128)(2,1)S(1)}, bf16[2,8,16,256]{3,2,1,0:T(8,128)(2,1)S(1)}, u32[]{:S(2)}, u32[]{:S(2)}) collective-permute-start(bf16[2,8,16,256]{3,2,1,0:T(8,128)(2,1)S(1)} %get-tuple-element.62), channel_id=1, source_target_pairs={{0,192},{16,208},{32,224},{48,240},{64,0},{80,16},{96,32},{112,48}... | collective-permute-start | bytes 393224 | tf_op jit(solution)/shard_map/ppermute | solution.py:471
  76.5 4.4 %collective-permute-start.15 = (bf16[2,8,16,256]{3,2,1,0:T(8,128)(2,1)S(1)}, bf16[2,8,16,256]{3,2,1,0:T(8,128)(2,1)S(1)}, u32[]{:S(2)}, u32[]{:S(2)}) collective-permute-start(bf16[2,8,16,256]{3,2,1,0:T(8,128)(2,1)S(1)} %get-tuple-element.63), channel_id=1, source_target_pairs={{0,128},{16,144},{32,160},{48,176},{64,192},{80,208},{96,224},{112... | collective-permute-start | bytes 393224 | tf_op jit(solution)/shard_map/ppermute | solution.py:471
  80.9 4.2 %edge_analysis.1 = (bf16[2,8,16,256]{3,2,1,0:T(8,128)(2,1)S(1)}, bf16[2,8,16,256]{3,2,1,0:T(8,128)(2,1)S(1)}, bf16[2,8,16,256]{3,2,1,0:T(8,128)(2,1)S(1)}, bf16[...) custom-call(f32[1,4,4,128]{3,2,1,0:T(4,128)S(1)} %collective-permute, ...), custom_call_target="tpu_custom_call" | custom-call | flops 2000000000 | bytes 6000000 | tf_op jit(solution)/shard_map/edge_analysis/pallas_call | solution.py:380
  85.2 2.8 %collective-permute-start.17 = (bf16[2,8,16,256]{3,2,1,0:T(8,128)(2,1)S(1)}, bf16[2,8,16,256]{3,2,1,0:T(8,128)(2,1)S(1)}, u32[]{:S(2)}, u32[]{:S(2)}) collective-permute-start(bf16[2,8,16,256]{3,2,1,0:T(8,128)(2,1)S(1)} %get-tuple-element.65), channel_id=1, source_target_pairs={{0,224},{16,240},{32,0},{48,16},{64,32},{80,48},{96,64},{112,80},{... | collective-permute-start | bytes 393224 | tf_op jit(solution)/shard_map/ppermute | solution.py:471
  88.1 5.7 %collective-permute-start.25 = (bf16[2,8,16,256]{3,2,1,0:T(8,128)(2,1)S(1)}, bf16[2,8,16,256]{3,2,1,0:T(8,128)(2,1)S(1)}, u32[]{:S(2)}, u32[]{:S(2)}) collective-permute-start(bf16[2,8,16,256]{3,2,1,0:T(8,128)(2,1)S(1)} %get-tuple-element.75), channel_id=1, source_target_pairs={{0,96},{16,112},{32,128},{48,144},{64,160},{80,176},{96,192},{112,... | collective-permute-start | bytes 393224 | tf_op jit(solution)/shard_map/ppermute | solution.py:471
  99.2 2.4 %collective-permute-start.29 = (bf16[2,8,16,256]{3,2,1,0:T(8,128)(2,1)S(1)}, bf16[2,8,16,256]{3,2,1,0:T(8,128)(2,1)S(1)}, u32[]{:S(2)}, u32[]{:S(2)}) collective-permute-start(bf16[2,8,16,256]{3,2,1,0:T(8,128)(2,1)S(1)} %get-tuple-element.79), channel_id=1, source_target_pairs={{0,128},{16,144},{32,160},{48,176},{64,192},{80,208},{96,224},{112... | collective-permute-start | bytes 393224 | tf_op jit(solution)/shard_map/ppermute | solution.py:471
  101.5 3.5 %collective-permute-done.25.refs_0_.refs_8_ = bf16[2,8,16,256]{3,2,1,0:T(8,128)(2,1)S(1)} collective-permute-done((bf16[2,8,16,256]{3,2,1,0:T(8,128)(2,1)S(1)}, bf16[2,8,16,256]{3,2,1,0:T(8,128)(2,1)S(1)}, u32[]{:S(2)}, u32[]{:S(2)}) %collective-permute-start.25) | collective-permute-done | bytes 131104 | tf_op jit(solution)/shard_map/ppermute | solution.py:471
  109.8 2.9 %collective-permute-start.32 = (bf16[8,8,16,256]{3,2,1,0:T(8,128)(2,1)S(1)}, bf16[8,8,16,256]{3,2,1,0:T(8,128)(2,1)S(1)}, u32[]{:S(2)}, u32[]{:S(2)}) collective-permute-start(bf16[8,8,16,256]{3,2,1,0:T(8,128)(2,1)S(1)} %inner_pack.1), channel_id=1, source_target_pairs={{0,16},{16,0},{32,48},{48,32},{64,80},{80,64},{96,112},{112,96},{1... | collective-permute-start | bytes 1572872 | tf_op jit(solution)/shard_map/ppermute | solution.py:467
  113.2 5.1 %collective-permute-done.30.refs_5_.refs_13_ = bf16[2,8,16,256]{3,2,1,0:T(8,128)(2,1)S(1)} collective-permute-done((bf16[2,8,16,256]{3,2,1,0:T(8,128)(2,1)S(1)}, bf16[2,8,16,256]{3,2,1,0:T(8,128)(2,1)S(1)}, u32[]{:S(2)}, u32[]{:S(2)}) %collective-permute-start.30) | collective-permute-done | bytes 131104 | tf_op jit(solution)/shard_map/ppermute | solution.py:471
  123.5 2.9 %result.1 = bf16[16,8,16,512]{3,2,1,0:T(8,128)(2,1)} custom-call(bf16[2,8,16,256]{3,2,1,0:T(8,128)(2,1)S(1)} %collective-permute-done.11.refs_0_, bf16[2,8,16,256]{3,2,1,0:T(8,128)(2,1)S(1)} %collective-permute-done.12.refs_1_, bf16[2,8,16,256]{3,2,1,0:T(8,128)(2,1)S(1)} %collective-permute-done.13.refs_2_, ...), custom_call_target="tpu_custom_call" | custom-call | tf_op jit(solution)/shard_map/result/pallas_call | solution.py:441
  (71 shorter events, 31.2 us)
Async XLA Ops:
  10.0 21.9 %collective-permute-start.1 = (bf16[9,2,32,512]{3,2,1,0:T(8,128)(2,1)S(1)}, bf16[9,2,32,512]{3,2,1,0:T(8,128)(2,1)S(1)}, u32[]{:S(2)}, u32[]{:S(2)}) collective-permute-start(bf16[9,2,32,512]{3,2,1,0:T(8,128)(2,1)S(1)} %get-tuple-element.48), channel_id=1, source_target_pairs={{16,1},{1,16},{17,2},{2,17},{18,3},{3,18},{19,4},{4,19},{20,5},{5,... | collective-permute-start | bytes 1769480 | tf_op jit(solution)/shard_map/ppermute | solution.py:501
  19.8 18.9 %collective-permute-start.6 = (bf16[2,8,16,256]{3,2,1,0:T(8,128)(2,1)S(1)}, bf16[2,8,16,256]{3,2,1,0:T(8,128)(2,1)S(1)}, u32[]{:S(2)}, u32[]{:S(2)}) collective-permute-start(bf16[2,8,16,256]{3,2,1,0:T(8,128)(2,1)S(1)} %get-tuple-element.53), channel_id=1, source_target_pairs={{0,64},{16,80},{32,96},{48,112},{64,128},{80,144},{96,160},{112,17... | collective-permute-start | bytes 393224 | tf_op jit(solution)/shard_map/ppermute | solution.py:471
  21.0 19.5 %collective-permute-start.7 = (bf16[2,8,16,256]{3,2,1,0:T(8,128)(2,1)S(1)}, bf16[2,8,16,256]{3,2,1,0:T(8,128)(2,1)S(1)}, u32[]{:S(2)}, u32[]{:S(2)}) collective-permute-start(bf16[2,8,16,256]{3,2,1,0:T(8,128)(2,1)S(1)} %get-tuple-element.54), channel_id=1, source_target_pairs={{0,192},{16,208},{32,224},{48,240},{64,0},{80,16},{96,32},{112,48}... | collective-permute-start | bytes 393224 | tf_op jit(solution)/shard_map/ppermute | solution.py:471
  23.8 19.4 %collective-permute-start.8 = (bf16[2,8,16,256]{3,2,1,0:T(8,128)(2,1)S(1)}, bf16[2,8,16,256]{3,2,1,0:T(8,128)(2,1)S(1)}, u32[]{:S(2)}, u32[]{:S(2)}) collective-permute-start(bf16[2,8,16,256]{3,2,1,0:T(8,128)(2,1)S(1)} %get-tuple-element.55), channel_id=1, source_target_pairs={{0,128},{16,144},{32,160},{48,176},{64,192},{80,208},{96,224},{112... | collective-permute-start | bytes 393224 | tf_op jit(solution)/shard_map/ppermute | solution.py:471
  30.2 21.8 %collective-permute-start.9 = (bf16[2,8,16,256]{3,2,1,0:T(8,128)(2,1)S(1)}, bf16[2,8,16,256]{3,2,1,0:T(8,128)(2,1)S(1)}, u32[]{:S(2)}, u32[]{:S(2)}) collective-permute-start(bf16[2,8,16,256]{3,2,1,0:T(8,128)(2,1)S(1)} %get-tuple-element.56), channel_id=1, source_target_pairs={{0,32},{16,48},{32,64},{48,80},{64,96},{80,112},{96,128},{112,144}... | collective-permute-start | bytes 393224 | tf_op jit(solution)/shard_map/ppermute | solution.py:471
  31.9 25.0 %collective-permute-start.10 = (bf16[2,8,16,256]{3,2,1,0:T(8,128)(2,1)S(1)}, bf16[2,8,16,256]{3,2,1,0:T(8,128)(2,1)S(1)}, u32[]{:S(2)}, u32[]{:S(2)}) collective-permute-start(bf16[2,8,16,256]{3,2,1,0:T(8,128)(2,1)S(1)} %get-tuple-element.57), channel_id=1, source_target_pairs={{0,224},{16,240},{32,0},{48,16},{64,32},{80,48},{96,64},{112,80},{... | collective-permute-start | bytes 393224 | tf_op jit(solution)/shard_map/ppermute | solution.py:471
  38.7 22.8 %collective-permute-start.18 = (bf16[2,8,16,256]{3,2,1,0:T(8,128)(2,1)S(1)}, bf16[2,8,16,256]{3,2,1,0:T(8,128)(2,1)S(1)}, u32[]{:S(2)}, u32[]{:S(2)}) collective-permute-start(bf16[2,8,16,256]{3,2,1,0:T(8,128)(2,1)S(1)} %get-tuple-element.67), channel_id=1, source_target_pairs={{0,96},{16,112},{32,128},{48,144},{64,160},{80,176},{96,192},{112,... | collective-permute-start | bytes 393224 | tf_op jit(solution)/shard_map/ppermute | solution.py:471
  40.4 21.0 %collective-permute-start.19 = (bf16[2,8,16,256]{3,2,1,0:T(8,128)(2,1)S(1)}, bf16[2,8,16,256]{3,2,1,0:T(8,128)(2,1)S(1)}, u32[]{:S(2)}, u32[]{:S(2)}) collective-permute-start(bf16[2,8,16,256]{3,2,1,0:T(8,128)(2,1)S(1)} %get-tuple-element.68), channel_id=1, source_target_pairs={{0,160},{16,176},{32,192},{48,208},{64,224},{80,240},{96,0},{112,1... | collective-permute-start | bytes 393224 | tf_op jit(solution)/shard_map/ppermute | solution.py:471
  43.2 13.7 %collective-permute-start.2 = (f32[1,4,4,128]{3,2,1,0:T(4,128)S(1)}, f32[1,4,4,128]{3,2,1,0:T(4,128)S(1)}, u32[]{:S(2)}, u32[]{:S(2)}) collective-permute-start(f32[1,4,4,128]{3,2,1,0:T(4,128)S(1)} %select_select_fusion.1), channel_id=1, source_target_pairs={{0,32},{16,96},{32,160},{48,224},{64,0},{80,64},{96,128},{112,192}... | collective-permute-start | bytes 24584 | tf_op jit(solution)/shard_map/ppermute | solution.py:505
  56.9 13.5 %collective-permute-start.21 = (bf16[2,8,16,256]{3,2,1,0:T(8,128)(2,1)S(1)}, bf16[2,8,16,256]{3,2,1,0:T(8,128)(2,1)S(1)}, u32[]{:S(2)}, u32[]{:S(2)}) collective-permute-start(bf16[2,8,16,256]{3,2,1,0:T(8,128)(2,1)S(1)} %get-tuple-element.70), channel_id=1, source_target_pairs={{0,192},{16,208},{32,224},{48,240},{64,0},{80,16},{96,32},{112,48}... | collective-permute-start | bytes 393224 | tf_op jit(solution)/shard_map/ppermute | solution.py:471
  61.5 15.0 %collective-permute-start.24 = (bf16[2,8,16,256]{3,2,1,0:T(8,128)(2,1)S(1)}, bf16[2,8,16,256]{3,2,1,0:T(8,128)(2,1)S(1)}, u32[]{:S(2)}, u32[]{:S(2)}) collective-permute-start(bf16[2,8,16,256]{3,2,1,0:T(8,128)(2,1)S(1)} %get-tuple-element.73), channel_id=1, source_target_pairs={{0,224},{16,240},{32,0},{48,16},{64,32},{80,48},{96,64},{112,80},{... | collective-permute-start | bytes 393224 | tf_op jit(solution)/shard_map/ppermute | solution.py:471
  68.3 16.8 %collective-permute-start.11 = (bf16[2,8,16,256]{3,2,1,0:T(8,128)(2,1)S(1)}, bf16[2,8,16,256]{3,2,1,0:T(8,128)(2,1)S(1)}, u32[]{:S(2)}, u32[]{:S(2)}) collective-permute-start(bf16[2,8,16,256]{3,2,1,0:T(8,128)(2,1)S(1)} %get-tuple-element.59), channel_id=1, source_target_pairs={{0,96},{16,112},{32,128},{48,144},{64,160},{80,176},{96,192},{112,... | collective-permute-start | bytes 393224 | tf_op jit(solution)/shard_map/ppermute | solution.py:471
  70.5 14.8 %collective-permute-start.12 = (bf16[2,8,16,256]{3,2,1,0:T(8,128)(2,1)S(1)}, bf16[2,8,16,256]{3,2,1,0:T(8,128)(2,1)S(1)}, u32[]{:S(2)}, u32[]{:S(2)}) collective-permute-start(bf16[2,8,16,256]{3,2,1,0:T(8,128)(2,1)S(1)} %get-tuple-element.60), channel_id=1, source_target_pairs={{0,160},{16,176},{32,192},{48,208},{64,224},{80,240},{96,0},{112,1... | collective-permute-start | bytes 393224 | tf_op jit(solution)/shard_map/ppermute | solution.py:471
  72.9 15.2 %collective-permute-start.13 = (bf16[2,8,16,256]{3,2,1,0:T(8,128)(2,1)S(1)}, bf16[2,8,16,256]{3,2,1,0:T(8,128)(2,1)S(1)}, u32[]{:S(2)}, u32[]{:S(2)}) collective-permute-start(bf16[2,8,16,256]{3,2,1,0:T(8,128)(2,1)S(1)} %get-tuple-element.61), channel_id=1, source_target_pairs={{0,64},{16,80},{32,96},{48,112},{64,128},{80,144},{96,160},{112,17... | collective-permute-start | bytes 393224 | tf_op jit(solution)/shard_map/ppermute | solution.py:471
  73.9 19.9 %collective-permute-start.14 = (bf16[2,8,16,256]{3,2,1,0:T(8,128)(2,1)S(1)}, bf16[2,8,16,256]{3,2,1,0:T(8,128)(2,1)S(1)}, u32[]{:S(2)}, u32[]{:S(2)}) collective-permute-start(bf16[2,8,16,256]{3,2,1,0:T(8,128)(2,1)S(1)} %get-tuple-element.62), channel_id=1, source_target_pairs={{0,192},{16,208},{32,224},{48,240},{64,0},{80,16},{96,32},{112,48}... | collective-permute-start | bytes 393224 | tf_op jit(solution)/shard_map/ppermute | solution.py:471
  76.5 19.1 %collective-permute-start.15 = (bf16[2,8,16,256]{3,2,1,0:T(8,128)(2,1)S(1)}, bf16[2,8,16,256]{3,2,1,0:T(8,128)(2,1)S(1)}, u32[]{:S(2)}, u32[]{:S(2)}) collective-permute-start(bf16[2,8,16,256]{3,2,1,0:T(8,128)(2,1)S(1)} %get-tuple-element.63), channel_id=1, source_target_pairs={{0,128},{16,144},{32,160},{48,176},{64,192},{80,208},{96,224},{112... | collective-permute-start | bytes 393224 | tf_op jit(solution)/shard_map/ppermute | solution.py:471
  85.1 12.8 %collective-permute-start.16 = (bf16[2,8,16,256]{3,2,1,0:T(8,128)(2,1)S(1)}, bf16[2,8,16,256]{3,2,1,0:T(8,128)(2,1)S(1)}, u32[]{:S(2)}, u32[]{:S(2)}) collective-permute-start(bf16[2,8,16,256]{3,2,1,0:T(8,128)(2,1)S(1)} %get-tuple-element.64), channel_id=1, source_target_pairs={{0,32},{16,48},{32,64},{48,80},{64,96},{80,112},{96,128},{112,144}... | collective-permute-start | bytes 393224 | tf_op jit(solution)/shard_map/ppermute | solution.py:471
  85.2 13.9 %collective-permute-start.17 = (bf16[2,8,16,256]{3,2,1,0:T(8,128)(2,1)S(1)}, bf16[2,8,16,256]{3,2,1,0:T(8,128)(2,1)S(1)}, u32[]{:S(2)}, u32[]{:S(2)}) collective-permute-start(bf16[2,8,16,256]{3,2,1,0:T(8,128)(2,1)S(1)} %get-tuple-element.65), channel_id=1, source_target_pairs={{0,224},{16,240},{32,0},{48,16},{64,32},{80,48},{96,64},{112,80},{... | collective-permute-start | bytes 393224 | tf_op jit(solution)/shard_map/ppermute | solution.py:471
  88.1 16.9 %collective-permute-start.25 = (bf16[2,8,16,256]{3,2,1,0:T(8,128)(2,1)S(1)}, bf16[2,8,16,256]{3,2,1,0:T(8,128)(2,1)S(1)}, u32[]{:S(2)}, u32[]{:S(2)}) collective-permute-start(bf16[2,8,16,256]{3,2,1,0:T(8,128)(2,1)S(1)} %get-tuple-element.75), channel_id=1, source_target_pairs={{0,96},{16,112},{32,128},{48,144},{64,160},{80,176},{96,192},{112,... | collective-permute-start | bytes 393224 | tf_op jit(solution)/shard_map/ppermute | solution.py:471
  95.6 14.2 %collective-permute-start.27 = (bf16[2,8,16,256]{3,2,1,0:T(8,128)(2,1)S(1)}, bf16[2,8,16,256]{3,2,1,0:T(8,128)(2,1)S(1)}, u32[]{:S(2)}, u32[]{:S(2)}) collective-permute-start(bf16[2,8,16,256]{3,2,1,0:T(8,128)(2,1)S(1)} %get-tuple-element.77), channel_id=1, source_target_pairs={{0,64},{16,80},{32,96},{48,112},{64,128},{80,144},{96,160},{112,17... | collective-permute-start | bytes 393224 | tf_op jit(solution)/shard_map/ppermute | solution.py:471
  97.9 14.7 %collective-permute-start.28 = (bf16[2,8,16,256]{3,2,1,0:T(8,128)(2,1)S(1)}, bf16[2,8,16,256]{3,2,1,0:T(8,128)(2,1)S(1)}, u32[]{:S(2)}, u32[]{:S(2)}) collective-permute-start(bf16[2,8,16,256]{3,2,1,0:T(8,128)(2,1)S(1)} %get-tuple-element.78), channel_id=1, source_target_pairs={{0,192},{16,208},{32,224},{48,240},{64,0},{80,16},{96,32},{112,48}... | collective-permute-start | bytes 393224 | tf_op jit(solution)/shard_map/ppermute | solution.py:471
  99.2 14.0 %collective-permute-start.29 = (bf16[2,8,16,256]{3,2,1,0:T(8,128)(2,1)S(1)}, bf16[2,8,16,256]{3,2,1,0:T(8,128)(2,1)S(1)}, u32[]{:S(2)}, u32[]{:S(2)}) collective-permute-start(bf16[2,8,16,256]{3,2,1,0:T(8,128)(2,1)S(1)} %get-tuple-element.79), channel_id=1, source_target_pairs={{0,128},{16,144},{32,160},{48,176},{64,192},{80,208},{96,224},{112... | collective-permute-start | bytes 393224 | tf_op jit(solution)/shard_map/ppermute | solution.py:471
  105.0 13.3 %collective-permute-start.30 = (bf16[2,8,16,256]{3,2,1,0:T(8,128)(2,1)S(1)}, bf16[2,8,16,256]{3,2,1,0:T(8,128)(2,1)S(1)}, u32[]{:S(2)}, u32[]{:S(2)}) collective-permute-start(bf16[2,8,16,256]{3,2,1,0:T(8,128)(2,1)S(1)} %get-tuple-element.80), channel_id=1, source_target_pairs={{0,32},{16,48},{32,64},{48,80},{64,96},{80,112},{96,128},{112,144}... | collective-permute-start | bytes 393224 | tf_op jit(solution)/shard_map/ppermute | solution.py:471
  106.0 13.6 %collective-permute-start.31 = (bf16[2,8,16,256]{3,2,1,0:T(8,128)(2,1)S(1)}, bf16[2,8,16,256]{3,2,1,0:T(8,128)(2,1)S(1)}, u32[]{:S(2)}, u32[]{:S(2)}) collective-permute-start(bf16[2,8,16,256]{3,2,1,0:T(8,128)(2,1)S(1)} %get-tuple-element.81), channel_id=1, source_target_pairs={{0,224},{16,240},{32,0},{48,16},{64,32},{80,48},{96,64},{112,80},{... | collective-permute-start | bytes 393224 | tf_op jit(solution)/shard_map/ppermute | solution.py:471
  (16 other events, 178.2 us)

commit v3 on v2

--- a/solution.py
+++ b/solution.py
@@ -56,6 +56,15 @@
     west = pltpu.roll(centre, 1, 1)
     c, e, w, n, so = coef
     return centre * c + east * e + west * w + north * n + south * so
+
+
+def each_field(work):
+    def pair(i, carry):
+        for u in range(2):
+            work(2 * i + u, u)
+        return carry
+
+    lax.fori_loop(0, 4, pair, 0)
 
 
 def two_steps(rows_at, coef_at, outside, groups, middle, ready):
@@ -114,14 +123,13 @@
     halo_ref[8, 0] = jnp.concatenate(parts, axis=0)
     halo_ref[8, 1] = jnp.zeros((16, 512), BF16)
 
-    def one_field(f, carry):
+    def one_field(f, u):
         flat = own_ref[:, f].reshape(256, 512)
-        halo_ref[f] = inner_field(pick, flat, c, inner_coef, fields, middle, ready)
+        halo_ref[f] = inner_field(pick, flat, c, inner_coef, fields.at[u], middle.at[u], ready.at[u])
         for k in range(8):
-            part_ref[k, f] = ready[(z + ORDER[k]) & 7]
-        return carry
-
-    lax.fori_loop(0, 8, one_field, 0)
+            part_ref[k, f] = ready[u, (z + ORDER[k]) & 7]
+
+    each_field(one_field)
 
 
 def sib_kernel(sib_ref, coef, part_ref, own_halo_ref, *rest):
@@ -131,16 +139,15 @@
     pick[:128] = row_picker(8, 2 + 4 * c)
     pick[128:] = row_picker(2, 14 * c)
 
-    def one_field(f, carry):
+    def one_field(f, u):
         flat = sib_ref[:, f].reshape(256, 512)
-        halo_ref[f, :, :16] = inner_field(pick, flat, c, coef, fields, middle, ready)
+        halo_ref[f, :, :16] = inner_field(pick, flat, c, coef, fields.at[u], middle.at[u], ready.at[u])
         halo_ref[f, :, 16:] = own_halo_ref[f]
         for k, out_ref in enumerate(outs):
             out_ref[0, f] = part_ref[k, f]
-            out_ref[1, f] = ready[(z + ORDER[k]) & 7]
-        return carry
-
-    lax.fori_loop(0, 8, one_field, 0)
+            out_ref[1, f] = ready[u, (z + ORDER[k]) & 7]
+
+    each_field(one_field)
     halo_ref[8, :, :16] = own_halo_ref[8]
     halo_ref[8, :, 16:] = jnp.zeros((2, 16, 512), BF16)
 
@@ -156,23 +163,22 @@
     domain = lax.axis_index("domain")
     outside = jnp.where(c == 0, domain == 0, domain == lax.axis_size("domain") - 1)
 
-    def one_field(f, carry):
-        fields[:, :16] = dot(pick[...], own_ref[:, f].reshape(256, 512)).reshape(8, 16, 512)
-        fields[:, 16:] = dot(pick[...], sib_ref[:, f].reshape(256, 512)).reshape(8, 16, 512)
-        fields[pl.ds(6 * c, 2)] = halo_ref[f].astype(F32)
+    def one_field(f, u):
+        fields[u, :, :16] = dot(pick[...], own_ref[:, f].reshape(256, 512)).reshape(8, 16, 512)
+        fields[u, :, 16:] = dot(pick[...], sib_ref[:, f].reshape(256, 512)).reshape(8, 16, 512)
+        fields[u, pl.ds(6 * c, 2)] = halo_ref[f].astype(F32)
         two_steps(
-            lambda j: fields[j],
+            lambda j: fields[u, j],
             lambda j: [jnp.concatenate([coef[k, j]] * 4, axis=0) for k in range(5)],
             (outside, 5 * c),
             2,
-            middle,
-            ready,
+            middle.at[u],
+            ready.at[u],
         )
         for k, out_ref in enumerate(outs):
-            out_ref[:, f] = ready[(z + ORDER[k]) & 7].reshape(2, 16, 256)
-        return carry
-
-    lax.fori_loop(0, 8, one_field, 0)
+            out_ref[:, f] = ready[u, (z + ORDER[k]) & 7].reshape(2, 16, 256)
+
+    each_field(one_field)
 
 
 VMEM = pl.BlockSpec(memory_space=pltpu.VMEM)
@@ -193,9 +199,9 @@
         out_shape=[jax.ShapeDtypeStruct(*shape) for shape in shapes],
         scratch_shapes=[
             pltpu.VMEM((160, 256), BF16),
-            pltpu.VMEM((8, 16, 512), F32),
-            pltpu.VMEM((6, 16, 512), F32),
-            pltpu.VMEM((8, 16, 256), BF16),
+            pltpu.VMEM((2, 8, 16, 512), F32),
+            pltpu.VMEM((2, 6, 16, 512), F32),
+            pltpu.VMEM((2, 8, 16, 256), BF16),
         ],
         compiler_params=LIMIT,
         cost_estimate=cost(300_000_000, 6_000_000),
@@ -211,9 +217,9 @@
         out_shape=[jax.ShapeDtypeStruct(PIECE, BF16)] * 8 + [jax.ShapeDtypeStruct((9, 2, 32, 512), BF16)],
         scratch_shapes=[
             pltpu.VMEM((160, 256), BF16),
-            pltpu.VMEM((8, 16, 512), F32),
-            pltpu.VMEM((6, 16, 512), F32),
-            pltpu.VMEM((8, 16, 256), BF16),
+            pltpu.VMEM((2, 8, 16, 512), F32),
+            pltpu.VMEM((2, 6, 16, 512), F32),
+            pltpu.VMEM((2, 8, 16, 256), BF16),
         ],
         compiler_params=LIMIT,
         cost_estimate=cost(300_000_000, 6_000_000),
@@ -230,9 +236,9 @@
         scratch_shapes=[
             pltpu.VMEM((128, 256), BF16),
             pltpu.VMEM((5, 6, 8, 512), F32),
-            pltpu.VMEM((8, 32, 512), F32),
-            pltpu.VMEM((6, 32, 512), F32),
-            pltpu.VMEM((8, 32, 256), BF16),
+            pltpu.VMEM((2, 8, 32, 512), F32),
+            pltpu.VMEM((2, 6, 32, 512), F32),
+            pltpu.VMEM((2, 8, 32, 256), BF16),
         ],
         compiler_params=LIMIT,
         cost_estimate=cost(300_000_000, 6_000_000),
@@ -414,26 +420,25 @@
     def send(f):
         return pltpu.make_async_copy(ready.at[f], out_ref.at[:, f], sent.at[f])
 
-    def one_field(f, carry):
+    def one_field(f, u):
         for chunk in range(2):
             own_base = 12 * c if chunk else 4 + 4 * c
             sib_base = 12 - 12 * c if chunk else 8 - 4 * c
             for k in range(8):
-                rows[2 * own_base + ((z - ORDER[k]) & 7)] = mine[8 * chunk + k][0, f]
+                rows[u, 2 * own_base + ((z - ORDER[k]) & 7)] = mine[8 * chunk + k][0, f]
             for source in range(8):
-                rows[2 * sib_base + source] = theirs[chunk][source, f]
-        both = rows[...].reshape(16, 2, 16, 256)
+                rows[u, 2 * sib_base + source] = theirs[chunk][source, f]
+        both = rows[u].reshape(16, 2, 16, 256)
         for h in range(2):
             out = dot(pick[...], both[:, h].reshape(256, 256)).astype(BF16)
             ready[f, :, :, h * 256 : (h + 1) * 256] = out.reshape(16, 16, 256)
         send(f).start()
-        return carry
 
     def finish(f, carry):
         send(f).wait()
         return carry
 
-    lax.fori_loop(0, 8, one_field, 0)
+    each_field(one_field)
     lax.fori_loop(0, 8, finish, 0)
 
 
@@ -445,7 +450,7 @@
         out_shape=jax.ShapeDtypeStruct((16, 8, 16, 512), BF16),
         scratch_shapes=[
             pltpu.VMEM((256, 256), BF16),
-            pltpu.VMEM((32, 16, 256), BF16),
+            pltpu.VMEM((2, 32, 16, 256), BF16),
             pltpu.VMEM((8, 16, 16, 512), BF16),
             pltpu.SemaphoreType.DMA((8,)),
         ],
@@ -500,8 +505,9 @@
     inner = exchange(inner)
     halo = lax.ppermute(halo, ("member", "domain"), pairs)
     outer = edge_forecast(state, sib, edge_coef, halo)
-    first, obs = lax.optimization_barrier((outer[0], obs))
-    outer = exchange([first, *outer[1:]])
+    outer = exchange(outer)
+    first, obs = lax.optimization_barrier((inner[0], obs))
+    inner = [first, *inner[1:]]
     obs = [lax.ppermute(obs, "member", pairs) for pairs in obs_pairs()]
     inner = exchange(analysis(False, obs, inner))
     inner_sib = swap(pack(inner, "inner_pack"))

time: 127 us -> 121 us (0.953); the launches traced: 127 us -> 119 us
  starting transfers between devices: 86 us -> 82.2 us
  Pallas kernels: 24 us -> 20.5 us
    ppermute x28, starting transfers between devices: 63.5 us -> 59 us  [around(): lax.ppermute(x, 'member', [(i, (i + 2 * distance) % 16) for i in range(16)])]
    ppermute x3, starting transfers between devices: 5.88 us -> 8.4 us  [swap(): return lax.ppermute(x, 'member', [(i, i ^ 1) for i in range(16)])]
    ppermute x2, starting transfers between devices: 13.6 us -> 11.7 us  [shards(): obs = [lax.ppermute(obs, 'member', pairs) for pairs in obs_pairs()]]
  transfers between devices with their start and end apart: 34 -> 34, of which waited for: 6 -> 7; matrix products, arithmetic and copies ran while one was open for 1% -> 1% of each run, Pallas kernels for 14% -> 13%
where the time goes in v3:
time: 121 us; the launch traced here: 119 us
  starting transfers between devices  82.2 us (68%)
  Pallas kernels  20.5 us (17%)
  waiting for transfers between devices  13.6 us (11%)
  local copies, waits for them, and re-layouts  1.61 us (1%)
    ppermute x28, starting transfers between devices, around(): lax.ppermute(x, 'member', [(i, (i + 2 * distance) % 16) for i in range(16)])  59 us
    ppermute x2, starting transfers between devices, shards(): obs = [lax.ppermute(obs, 'member', pairs) for pairs in obs_pairs()]  11.7 us
    ppermute x28, waiting for transfers between devices, around(): lax.ppermute(x, 'member', [(i, (i + 2 * distance) % 16) for i in range(16)])  11.3 us
    pallas_call x2, Pallas kernels, analysis(): pl.pallas_call(functools.partial(analysis_kernel, edge), in_specs=[VMEM]...  8.41 us
    ppermute x3, starting transfers between devices, swap(): return lax.ppermute(x, 'member', [(i, i ^ 1) for i in range(16)])  8.4 us
    pallas_call x1, Pallas kernels, edge_forecast(): pl.pallas_call(edge_kernel, in_specs=[VMEM] * 4, out_specs=[VMEM] * 8, ou...  4.98 us
    ppermute x1, starting transfers between devices, shards(): halo = lax.ppermute(halo, ('member', 'domain'), pairs)  3.1 us
    pallas_call x1, Pallas kernels, own_forecast(): pl.pallas_call(own_kernel, in_specs=[VMEM] * 2, out_specs=[VMEM] * 4, out...  2.46 us
  transfers between devices with their start and end apart: 34, of which 7 were waited for; matrix products, arithmetic and copies ran while one was open for 1% of the time, Pallas kernels for 13%

profile of v3, /device:TPU:7, one launch (start us, length us, event | category | flops | bytes accessed | tf_op | source)
XLA Modules:
  0.0 119.3 jit_solution(17969070036161189463)
XLA Ops:
  3.1 2.5 %own_forecast.1 = (f32[5,6,8,512]{3,2,1,0:T(8,128)S(1)}, f32[5,6,8,512]{3,2,1,0:T(8,128)S(1)}, bf16[8,8,16,256]{3,2,1,0:T(8,128)(2,1)S(1)}, bf16[9,2,16,512]{3,2,1,0:T(8,128)(2,1)S(1)}) custom-call(bf16[16,8,16,512]{3,2,1,0:T(8,128)(2,1)S(1)} %copy-done, f32[3,16,512]{2,1,0:T(8,128)S(1)} %select_select_fusion.numbers), custom_call_target="tpu_custom_call" | custom-call | flops 300000000 | bytes 6000000 | tf_op jit(solution)/shard_map/own_forecast/pallas_call | solution.py:195
  5.7 2.4 %sib_forecast.1 = (bf16[2,8,16,256]{3,2,1,0:T(8,128)(2,1)S(1)}, bf16[2,8,16,256]{3,2,1,0:T(8,128)(2,1)S(1)}, bf16[2,8,16,256]{3,2,1,0:T(8,128)(2,1)S(1)}, bf16[2...) custom-call(bf16[16,8,16,512]{3,2,1,0:T(8,128)(2,1)S(1)} %collective, ...), custom_call_target="tpu_custom_call" | custom-call | flops 300000000 | bytes 6000000 | tf_op jit(solution)/shard_map/sib_forecast/pallas_call | solution.py:213
  8.0 3.1 %collective-permute-start.17 = (bf16[9,2,32,512]{3,2,1,0:T(8,128)(2,1)S(1)}, bf16[9,2,32,512]{3,2,1,0:T(8,128)(2,1)S(1)}, u32[]{:S(2)}, u32[]{:S(2)}) collective-permute-start(bf16[9,2,32,512]{3,2,1,0:T(8,128)(2,1)S(1)} %get-tuple-element.66), channel_id=1, source_target_pairs={{16,1},{1,16},{17,2},{2,17},{18,3},{3,18},{19,4},{4,19},{20,5},{5,... | collective-permute-start | bytes 1769480 | tf_op jit(solution)/shard_map/ppermute | solution.py:506
  11.2 4.4 %collective-permute-start.1 = (bf16[2,8,16,256]{3,2,1,0:T(8,128)(2,1)S(1)}, bf16[2,8,16,256]{3,2,1,0:T(8,128)(2,1)S(1)}, u32[]{:S(2)}, u32[]{:S(2)}) collective-permute-start(bf16[2,8,16,256]{3,2,1,0:T(8,128)(2,1)S(1)} %get-tuple-element.47), channel_id=1, source_target_pairs={{0,96},{16,112},{32,128},{48,144},{64,160},{80,176},{96,192},{112,... | collective-permute-start | bytes 393224 | tf_op jit(solution)/shard_map/ppermute | solution.py:476
  15.6 2.2 %collective-permute-start.4 = (bf16[2,8,16,256]{3,2,1,0:T(8,128)(2,1)S(1)}, bf16[2,8,16,256]{3,2,1,0:T(8,128)(2,1)S(1)}, u32[]{:S(2)}, u32[]{:S(2)}) collective-permute-start(bf16[2,8,16,256]{3,2,1,0:T(8,128)(2,1)S(1)} %get-tuple-element.50), channel_id=1, source_target_pairs={{0,160},{16,176},{32,192},{48,208},{64,224},{80,240},{96,0},{112,1... | collective-permute-start | bytes 393224 | tf_op jit(solution)/shard_map/ppermute | solution.py:476
  19.0 2.8 %collective-permute-start.6 = (bf16[2,8,16,256]{3,2,1,0:T(8,128)(2,1)S(1)}, bf16[2,8,16,256]{3,2,1,0:T(8,128)(2,1)S(1)}, u32[]{:S(2)}, u32[]{:S(2)}) collective-permute-start(bf16[2,8,16,256]{3,2,1,0:T(8,128)(2,1)S(1)} %get-tuple-element.52), channel_id=1, source_target_pairs={{0,192},{16,208},{32,224},{48,240},{64,0},{80,16},{96,32},{112,48}... | collective-permute-start | bytes 393224 | tf_op jit(solution)/shard_map/ppermute | solution.py:476
  21.8 4.7 %collective-permute-start.7 = (bf16[2,8,16,256]{3,2,1,0:T(8,128)(2,1)S(1)}, bf16[2,8,16,256]{3,2,1,0:T(8,128)(2,1)S(1)}, u32[]{:S(2)}, u32[]{:S(2)}) collective-permute-start(bf16[2,8,16,256]{3,2,1,0:T(8,128)(2,1)S(1)} %get-tuple-element.53), channel_id=1, source_target_pairs={{0,128},{16,144},{32,160},{48,176},{64,192},{80,208},{96,224},{112... | collective-permute-start | bytes 393224 | tf_op jit(solution)/shard_map/ppermute | solution.py:476
  26.5 5.0 %edge_forecast.1 = (bf16[2,8,16,256]{3,2,1,0:T(8,128)(2,1)S(1)}, bf16[2,8,16,256]{3,2,1,0:T(8,128)(2,1)S(1)}, bf16[2,8,16,256]{3,2,1,0:T(8,128)(2,1)S(1)}, bf16[...) custom-call(bf16[16,8,16,512]{3,2,1,0:T(8,128)(2,1)S(1)} %copy-done., ...), custom_call_target="tpu_custom_call" | custom-call | flops 300000000 | bytes 6000000 | tf_op jit(solution)/shard_map/edge_forecast/pallas_call | solution.py:231
  34.6 4.1 %collective-permute-start.19 = (bf16[2,8,16,256]{3,2,1,0:T(8,128)(2,1)S(1)}, bf16[2,8,16,256]{3,2,1,0:T(8,128)(2,1)S(1)}, u32[]{:S(2)}, u32[]{:S(2)}) collective-permute-start(bf16[2,8,16,256]{3,2,1,0:T(8,128)(2,1)S(1)} %get-tuple-element.68), channel_id=1, source_target_pairs={{0,160},{16,176},{32,192},{48,208},{64,224},{80,240},{96,0},{112,1... | collective-permute-start | bytes 393224 | tf_op jit(solution)/shard_map/ppermute | solution.py:476
  38.8 8.2 %collective-permute-start.2 = (f32[1,4,4,128]{3,2,1,0:T(4,128)S(1)}, f32[1,4,4,128]{3,2,1,0:T(4,128)S(1)}, u32[]{:S(2)}, u32[]{:S(2)}) collective-permute-start(f32[1,4,4,128]{3,2,1,0:T(4,128)S(1)} %select_select_fusion.1), channel_id=1, source_target_pairs={{0,32},{16,96},{32,160},{48,224},{64,0},{80,64},{96,128},{112,192}... | collective-permute-start | bytes 24584 | tf_op jit(solution)/shard_map/ppermute | solution.py:511
  47.0 3.5 %collective-permute-start.3 = (f32[1,4,4,128]{3,2,1,0:T(4,128)S(1)}, f32[1,4,4,128]{3,2,1,0:T(4,128)S(1)}, u32[]{:S(2)}, u32[]{:S(2)}) collective-permute-start(f32[1,4,4,128]{3,2,1,0:T(4,128)S(1)} %select_select_fusion.1), channel_id=1, source_target_pairs={{0,0},{16,64},{32,128},{48,192},{64,32},{80,96},{96,160},{112,224}... | collective-permute-start | bytes 24584 | tf_op jit(solution)/shard_map/ppermute | solution.py:511
  50.6 3.6 %collective-permute-start.21 = (bf16[2,8,16,256]{3,2,1,0:T(8,128)(2,1)S(1)}, bf16[2,8,16,256]{3,2,1,0:T(8,128)(2,1)S(1)}, u32[]{:S(2)}, u32[]{:S(2)}) collective-permute-start(bf16[2,8,16,256]{3,2,1,0:T(8,128)(2,1)S(1)} %get-tuple-element.70), channel_id=1, source_target_pairs={{0,192},{16,208},{32,224},{48,240},{64,0},{80,16},{96,32},{112,48}... | collective-permute-start | bytes 393224 | tf_op jit(solution)/shard_map/ppermute | solution.py:476
  59.2 4.2 %inner_analysis.1 = (bf16[2,8,16,256]{3,2,1,0:T(8,128)(2,1)S(1)}, bf16[2,8,16,256]{3,2,1,0:T(8,128)(2,1)S(1)}, bf16[2,8,16,256]{3,2,1,0:T(8,128)(2,1)S(1)}, bf16...) custom-call(f32[1,4,4,128]{3,2,1,0:T(4,128)S(1)} %collective-permute, ...), custom_call_target="tpu_custom_call" | custom-call | flops 2000000000 | bytes 6000000 | tf_op jit(solution)/shard_map/inner_analysis/pallas_call | solution.py:386
  64.8 3.1 %collective-permute-start.11 = (bf16[2,8,16,256]{3,2,1,0:T(8,128)(2,1)S(1)}, bf16[2,8,16,256]{3,2,1,0:T(8,128)(2,1)S(1)}, u32[]{:S(2)}, u32[]{:S(2)}) collective-permute-start(bf16[2,8,16,256]{3,2,1,0:T(8,128)(2,1)S(1)} %get-tuple-element.58), channel_id=1, source_target_pairs={{0,160},{16,176},{32,192},{48,208},{64,224},{80,240},{96,0},{112,1... | collective-permute-start | bytes 393224 | tf_op jit(solution)/shard_map/ppermute | solution.py:476
  68.2 3.3 %collective-permute-start.13 = (bf16[2,8,16,256]{3,2,1,0:T(8,128)(2,1)S(1)}, bf16[2,8,16,256]{3,2,1,0:T(8,128)(2,1)S(1)}, u32[]{:S(2)}, u32[]{:S(2)}) collective-permute-start(bf16[2,8,16,256]{3,2,1,0:T(8,128)(2,1)S(1)} %get-tuple-element.60), channel_id=1, source_target_pairs={{0,192},{16,208},{32,224},{48,240},{64,0},{80,16},{96,32},{112,48}... | collective-permute-start | bytes 393224 | tf_op jit(solution)/shard_map/ppermute | solution.py:476
  71.5 3.7 %collective-permute-start.14 = (bf16[2,8,16,256]{3,2,1,0:T(8,128)(2,1)S(1)}, bf16[2,8,16,256]{3,2,1,0:T(8,128)(2,1)S(1)}, u32[]{:S(2)}, u32[]{:S(2)}) collective-permute-start(bf16[2,8,16,256]{3,2,1,0:T(8,128)(2,1)S(1)} %get-tuple-element.61), channel_id=1, source_target_pairs={{0,128},{16,144},{32,160},{48,176},{64,192},{80,208},{96,224},{112... | collective-permute-start | bytes 393224 | tf_op jit(solution)/shard_map/ppermute | solution.py:476
  75.3 4.2 %edge_analysis.1 = (bf16[2,8,16,256]{3,2,1,0:T(8,128)(2,1)S(1)}, bf16[2,8,16,256]{3,2,1,0:T(8,128)(2,1)S(1)}, bf16[2,8,16,256]{3,2,1,0:T(8,128)(2,1)S(1)}, bf16[...) custom-call(f32[1,4,4,128]{3,2,1,0:T(4,128)S(1)} %collective-permute, ...), custom_call_target="tpu_custom_call" | custom-call | flops 2000000000 | bytes 6000000 | tf_op jit(solution)/shard_map/edge_analysis/pallas_call | solution.py:386
  82.5 4.5 %collective-permute-start.26 = (bf16[2,8,16,256]{3,2,1,0:T(8,128)(2,1)S(1)}, bf16[2,8,16,256]{3,2,1,0:T(8,128)(2,1)S(1)}, u32[]{:S(2)}, u32[]{:S(2)}) collective-permute-start(bf16[2,8,16,256]{3,2,1,0:T(8,128)(2,1)S(1)} %get-tuple-element.76), channel_id=1, source_target_pairs={{0,160},{16,176},{32,192},{48,208},{64,224},{80,240},{96,0},{112,1... | collective-permute-start | bytes 393224 | tf_op jit(solution)/shard_map/ppermute | solution.py:476
  91.8 3.3 %collective-permute-start.29 = (bf16[2,8,16,256]{3,2,1,0:T(8,128)(2,1)S(1)}, bf16[2,8,16,256]{3,2,1,0:T(8,128)(2,1)S(1)}, u32[]{:S(2)}, u32[]{:S(2)}) collective-permute-start(bf16[2,8,16,256]{3,2,1,0:T(8,128)(2,1)S(1)} %get-tuple-element.79), channel_id=1, source_target_pairs={{0,128},{16,144},{32,160},{48,176},{64,192},{80,208},{96,224},{112... | collective-permute-start | bytes 393224 | tf_op jit(solution)/shard_map/ppermute | solution.py:476
  95.1 3.8 %collective-permute-done.25.refs_0_.refs_8_ = bf16[2,8,16,256]{3,2,1,0:T(8,128)(2,1)S(1)} collective-permute-done((bf16[2,8,16,256]{3,2,1,0:T(8,128)(2,1)S(1)}, bf16[2,8,16,256]{3,2,1,0:T(8,128)(2,1)S(1)}, u32[]{:S(2)}, u32[]{:S(2)}) %collective-permute-start.25) | collective-permute-done | bytes 131104 | tf_op jit(solution)/shard_map/ppermute | solution.py:476
  99.0 2.7 %collective-permute-start.31 = (bf16[2,8,16,256]{3,2,1,0:T(8,128)(2,1)S(1)}, bf16[2,8,16,256]{3,2,1,0:T(8,128)(2,1)S(1)}, u32[]{:S(2)}, u32[]{:S(2)}) collective-permute-start(bf16[2,8,16,256]{3,2,1,0:T(8,128)(2,1)S(1)} %get-tuple-element.81), channel_id=1, source_target_pairs={{0,224},{16,240},{32,0},{48,16},{64,32},{80,48},{96,64},{112,80},{... | collective-permute-start | bytes 393224 | tf_op jit(solution)/shard_map/ppermute | solution.py:476
  102.0 6.0 %collective-permute-start.32 = (bf16[8,8,16,256]{3,2,1,0:T(8,128)(2,1)S(1)}, bf16[8,8,16,256]{3,2,1,0:T(8,128)(2,1)S(1)}, u32[]{:S(2)}, u32[]{:S(2)}) collective-permute-start(bf16[8,8,16,256]{3,2,1,0:T(8,128)(2,1)S(1)} %inner_pack.1), channel_id=1, source_target_pairs={{0,16},{16,0},{32,48},{48,32},{64,80},{80,64},{96,112},{112,96},{1... | collective-permute-start | bytes 1572872 | tf_op jit(solution)/shard_map/ppermute | solution.py:472
  108.0 3.9 %collective-permute-done.30.refs_5_.refs_13_ = bf16[2,8,16,256]{3,2,1,0:T(8,128)(2,1)S(1)} collective-permute-done((bf16[2,8,16,256]{3,2,1,0:T(8,128)(2,1)S(1)}, bf16[2,8,16,256]{3,2,1,0:T(8,128)(2,1)S(1)}, u32[]{:S(2)}, u32[]{:S(2)}) %collective-permute-start.30) | collective-permute-done | bytes 131104 | tf_op jit(solution)/shard_map/ppermute | solution.py:476
  116.9 2.2 %result.1 = bf16[16,8,16,512]{3,2,1,0:T(8,128)(2,1)} custom-call(bf16[2,8,16,256]{3,2,1,0:T(8,128)(2,1)S(1)} %collective-permute-done.10.refs_0_, bf16[2,8,16,256]{3,2,1,0:T(8,128)(2,1)S(1)} %collective-permute-done.11.refs_1_, bf16[2,8,16,256]{3,2,1,0:T(8,128)(2,1)S(1)} %collective-permute-done.12.refs_2_, ...), custom_call_target="tpu_custom_call" | custom-call | tf_op jit(solution)/shard_map/result/pallas_call | solution.py:446
  (71 shorter events, 27.6 us)
Async XLA Ops:
  8.0 13.7 %collective-permute-start.17 = (bf16[9,2,32,512]{3,2,1,0:T(8,128)(2,1)S(1)}, bf16[9,2,32,512]{3,2,1,0:T(8,128)(2,1)S(1)}, u32[]{:S(2)}, u32[]{:S(2)}) collective-permute-start(bf16[9,2,32,512]{3,2,1,0:T(8,128)(2,1)S(1)} %get-tuple-element.66), channel_id=1, source_target_pairs={{16,1},{1,16},{17,2},{2,17},{18,3},{3,18},{19,4},{4,19},{20,5},{5,... | collective-permute-start | bytes 1769480 | tf_op jit(solution)/shard_map/ppermute | solution.py:506
  11.2 20.3 %collective-permute-start.1 = (bf16[2,8,16,256]{3,2,1,0:T(8,128)(2,1)S(1)}, bf16[2,8,16,256]{3,2,1,0:T(8,128)(2,1)S(1)}, u32[]{:S(2)}, u32[]{:S(2)}) collective-permute-start(bf16[2,8,16,256]{3,2,1,0:T(8,128)(2,1)S(1)} %get-tuple-element.47), channel_id=1, source_target_pairs={{0,96},{16,112},{32,128},{48,144},{64,160},{80,176},{96,192},{112,... | collective-permute-start | bytes 393224 | tf_op jit(solution)/shard_map/ppermute | solution.py:476
  15.6 16.7 %collective-permute-start.4 = (bf16[2,8,16,256]{3,2,1,0:T(8,128)(2,1)S(1)}, bf16[2,8,16,256]{3,2,1,0:T(8,128)(2,1)S(1)}, u32[]{:S(2)}, u32[]{:S(2)}) collective-permute-start(bf16[2,8,16,256]{3,2,1,0:T(8,128)(2,1)S(1)} %get-tuple-element.50), channel_id=1, source_target_pairs={{0,160},{16,176},{32,192},{48,208},{64,224},{80,240},{96,0},{112,1... | collective-permute-start | bytes 393224 | tf_op jit(solution)/shard_map/ppermute | solution.py:476
  17.8 16.4 %collective-permute-start.5 = (bf16[2,8,16,256]{3,2,1,0:T(8,128)(2,1)S(1)}, bf16[2,8,16,256]{3,2,1,0:T(8,128)(2,1)S(1)}, u32[]{:S(2)}, u32[]{:S(2)}) collective-permute-start(bf16[2,8,16,256]{3,2,1,0:T(8,128)(2,1)S(1)} %get-tuple-element.51), channel_id=1, source_target_pairs={{0,64},{16,80},{32,96},{48,112},{64,128},{80,144},{96,160},{112,17... | collective-permute-start | bytes 393224 | tf_op jit(solution)/shard_map/ppermute | solution.py:476
  19.0 15.6 %collective-permute-start.6 = (bf16[2,8,16,256]{3,2,1,0:T(8,128)(2,1)S(1)}, bf16[2,8,16,256]{3,2,1,0:T(8,128)(2,1)S(1)}, u32[]{:S(2)}, u32[]{:S(2)}) collective-permute-start(bf16[2,8,16,256]{3,2,1,0:T(8,128)(2,1)S(1)} %get-tuple-element.52), channel_id=1, source_target_pairs={{0,192},{16,208},{32,224},{48,240},{64,0},{80,16},{96,32},{112,48}... | collective-permute-start | bytes 393224 | tf_op jit(solution)/shard_map/ppermute | solution.py:476
  21.8 17.0 %collective-permute-start.7 = (bf16[2,8,16,256]{3,2,1,0:T(8,128)(2,1)S(1)}, bf16[2,8,16,256]{3,2,1,0:T(8,128)(2,1)S(1)}, u32[]{:S(2)}, u32[]{:S(2)}) collective-permute-start(bf16[2,8,16,256]{3,2,1,0:T(8,128)(2,1)S(1)} %get-tuple-element.53), channel_id=1, source_target_pairs={{0,128},{16,144},{32,160},{48,176},{64,192},{80,208},{96,224},{112... | collective-permute-start | bytes 393224 | tf_op jit(solution)/shard_map/ppermute | solution.py:476
  31.5 15.5 %collective-permute-start.8 = (bf16[2,8,16,256]{3,2,1,0:T(8,128)(2,1)S(1)}, bf16[2,8,16,256]{3,2,1,0:T(8,128)(2,1)S(1)}, u32[]{:S(2)}, u32[]{:S(2)}) collective-permute-start(bf16[2,8,16,256]{3,2,1,0:T(8,128)(2,1)S(1)} %get-tuple-element.54), channel_id=1, source_target_pairs={{0,32},{16,48},{32,64},{48,80},{64,96},{80,112},{96,128},{112,144}... | collective-permute-start | bytes 393224 | tf_op jit(solution)/shard_map/ppermute | solution.py:476
  32.3 18.2 %collective-permute-start.9 = (bf16[2,8,16,256]{3,2,1,0:T(8,128)(2,1)S(1)}, bf16[2,8,16,256]{3,2,1,0:T(8,128)(2,1)S(1)}, u32[]{:S(2)}, u32[]{:S(2)}) collective-permute-start(bf16[2,8,16,256]{3,2,1,0:T(8,128)(2,1)S(1)} %get-tuple-element.55), channel_id=1, source_target_pairs={{0,224},{16,240},{32,0},{48,16},{64,32},{80,48},{96,64},{112,80},{... | collective-permute-start | bytes 393224 | tf_op jit(solution)/shard_map/ppermute | solution.py:476
  34.2 22.3 %collective-permute-start.18 = (bf16[2,8,16,256]{3,2,1,0:T(8,128)(2,1)S(1)}, bf16[2,8,16,256]{3,2,1,0:T(8,128)(2,1)S(1)}, u32[]{:S(2)}, u32[]{:S(2)}) collective-permute-start(bf16[2,8,16,256]{3,2,1,0:T(8,128)(2,1)S(1)} %get-tuple-element.67), channel_id=1, source_target_pairs={{0,96},{16,112},{32,128},{48,144},{64,160},{80,176},{96,192},{112,... | collective-permute-start | bytes 393224 | tf_op jit(solution)/shard_map/ppermute | solution.py:476
  34.6 22.7 %collective-permute-start.19 = (bf16[2,8,16,256]{3,2,1,0:T(8,128)(2,1)S(1)}, bf16[2,8,16,256]{3,2,1,0:T(8,128)(2,1)S(1)}, u32[]{:S(2)}, u32[]{:S(2)}) collective-permute-start(bf16[2,8,16,256]{3,2,1,0:T(8,128)(2,1)S(1)} %get-tuple-element.68), channel_id=1, source_target_pairs={{0,160},{16,176},{32,192},{48,208},{64,224},{80,240},{96,0},{112,1... | collective-permute-start | bytes 393224 | tf_op jit(solution)/shard_map/ppermute | solution.py:476
  50.6 14.2 %collective-permute-start.21 = (bf16[2,8,16,256]{3,2,1,0:T(8,128)(2,1)S(1)}, bf16[2,8,16,256]{3,2,1,0:T(8,128)(2,1)S(1)}, u32[]{:S(2)}, u32[]{:S(2)}) collective-permute-start(bf16[2,8,16,256]{3,2,1,0:T(8,128)(2,1)S(1)} %get-tuple-element.70), channel_id=1, source_target_pairs={{0,192},{16,208},{32,224},{48,240},{64,0},{80,16},{96,32},{112,48}... | collective-permute-start | bytes 393224 | tf_op jit(solution)/shard_map/ppermute | solution.py:476
  57.4 14.2 %collective-permute-start.24 = (bf16[2,8,16,256]{3,2,1,0:T(8,128)(2,1)S(1)}, bf16[2,8,16,256]{3,2,1,0:T(8,128)(2,1)S(1)}, u32[]{:S(2)}, u32[]{:S(2)}) collective-permute-start(bf16[2,8,16,256]{3,2,1,0:T(8,128)(2,1)S(1)} %get-tuple-element.73), channel_id=1, source_target_pairs={{0,224},{16,240},{32,0},{48,16},{64,32},{80,48},{96,64},{112,80},{... | collective-permute-start | bytes 393224 | tf_op jit(solution)/shard_map/ppermute | solution.py:476
  63.4 16.1 %collective-permute-start.10 = (bf16[2,8,16,256]{3,2,1,0:T(8,128)(2,1)S(1)}, bf16[2,8,16,256]{3,2,1,0:T(8,128)(2,1)S(1)}, u32[]{:S(2)}, u32[]{:S(2)}) collective-permute-start(bf16[2,8,16,256]{3,2,1,0:T(8,128)(2,1)S(1)} %get-tuple-element.57), channel_id=1, source_target_pairs={{0,96},{16,112},{32,128},{48,144},{64,160},{80,176},{96,192},{112,... | collective-permute-start | bytes 393224 | tf_op jit(solution)/shard_map/ppermute | solution.py:476
  64.8 15.4 %collective-permute-start.11 = (bf16[2,8,16,256]{3,2,1,0:T(8,128)(2,1)S(1)}, bf16[2,8,16,256]{3,2,1,0:T(8,128)(2,1)S(1)}, u32[]{:S(2)}, u32[]{:S(2)}) collective-permute-start(bf16[2,8,16,256]{3,2,1,0:T(8,128)(2,1)S(1)} %get-tuple-element.58), channel_id=1, source_target_pairs={{0,160},{16,176},{32,192},{48,208},{64,224},{80,240},{96,0},{112,1... | collective-permute-start | bytes 393224 | tf_op jit(solution)/shard_map/ppermute | solution.py:476
  68.0 14.5 %collective-permute-start.12 = (bf16[2,8,16,256]{3,2,1,0:T(8,128)(2,1)S(1)}, bf16[2,8,16,256]{3,2,1,0:T(8,128)(2,1)S(1)}, u32[]{:S(2)}, u32[]{:S(2)}) collective-permute-start(bf16[2,8,16,256]{3,2,1,0:T(8,128)(2,1)S(1)} %get-tuple-element.59), channel_id=1, source_target_pairs={{0,64},{16,80},{32,96},{48,112},{64,128},{80,144},{96,160},{112,17... | collective-permute-start | bytes 393224 | tf_op jit(solution)/shard_map/ppermute | solution.py:476
  68.2 14.3 %collective-permute-start.13 = (bf16[2,8,16,256]{3,2,1,0:T(8,128)(2,1)S(1)}, bf16[2,8,16,256]{3,2,1,0:T(8,128)(2,1)S(1)}, u32[]{:S(2)}, u32[]{:S(2)}) collective-permute-start(bf16[2,8,16,256]{3,2,1,0:T(8,128)(2,1)S(1)} %get-tuple-element.60), channel_id=1, source_target_pairs={{0,192},{16,208},{32,224},{48,240},{64,0},{80,16},{96,32},{112,48}... | collective-permute-start | bytes 393224 | tf_op jit(solution)/shard_map/ppermute | solution.py:476
  71.5 15.4 %collective-permute-start.14 = (bf16[2,8,16,256]{3,2,1,0:T(8,128)(2,1)S(1)}, bf16[2,8,16,256]{3,2,1,0:T(8,128)(2,1)S(1)}, u32[]{:S(2)}, u32[]{:S(2)}) collective-permute-start(bf16[2,8,16,256]{3,2,1,0:T(8,128)(2,1)S(1)} %get-tuple-element.61), channel_id=1, source_target_pairs={{0,128},{16,144},{32,160},{48,176},{64,192},{80,208},{96,224},{112... | collective-permute-start | bytes 393224 | tf_op jit(solution)/shard_map/ppermute | solution.py:476
  82.5 16.5 %collective-permute-start.25 = (bf16[2,8,16,256]{3,2,1,0:T(8,128)(2,1)S(1)}, bf16[2,8,16,256]{3,2,1,0:T(8,128)(2,1)S(1)}, u32[]{:S(2)}, u32[]{:S(2)}) collective-permute-start(bf16[2,8,16,256]{3,2,1,0:T(8,128)(2,1)S(1)} %get-tuple-element.75), channel_id=1, source_target_pairs={{0,96},{16,112},{32,128},{48,144},{64,160},{80,176},{96,192},{112,... | collective-permute-start | bytes 393224 | tf_op jit(solution)/shard_map/ppermute | solution.py:476
  82.5 16.5 %collective-permute-start.26 = (bf16[2,8,16,256]{3,2,1,0:T(8,128)(2,1)S(1)}, bf16[2,8,16,256]{3,2,1,0:T(8,128)(2,1)S(1)}, u32[]{:S(2)}, u32[]{:S(2)}) collective-permute-start(bf16[2,8,16,256]{3,2,1,0:T(8,128)(2,1)S(1)} %get-tuple-element.76), channel_id=1, source_target_pairs={{0,160},{16,176},{32,192},{48,208},{64,224},{80,240},{96,0},{112,1... | collective-permute-start | bytes 393224 | tf_op jit(solution)/shard_map/ppermute | solution.py:476
  87.0 15.0 %collective-permute-start.27 = (bf16[2,8,16,256]{3,2,1,0:T(8,128)(2,1)S(1)}, bf16[2,8,16,256]{3,2,1,0:T(8,128)(2,1)S(1)}, u32[]{:S(2)}, u32[]{:S(2)}) collective-permute-start(bf16[2,8,16,256]{3,2,1,0:T(8,128)(2,1)S(1)} %get-tuple-element.77), channel_id=1, source_target_pairs={{0,64},{16,80},{32,96},{48,112},{64,128},{80,144},{96,160},{112,17... | collective-permute-start | bytes 393224 | tf_op jit(solution)/shard_map/ppermute | solution.py:476
  89.7 18.3 %collective-permute-start.28 = (bf16[2,8,16,256]{3,2,1,0:T(8,128)(2,1)S(1)}, bf16[2,8,16,256]{3,2,1,0:T(8,128)(2,1)S(1)}, u32[]{:S(2)}, u32[]{:S(2)}) collective-permute-start(bf16[2,8,16,256]{3,2,1,0:T(8,128)(2,1)S(1)} %get-tuple-element.78), channel_id=1, source_target_pairs={{0,192},{16,208},{32,224},{48,240},{64,0},{80,16},{96,32},{112,48}... | collective-permute-start | bytes 393224 | tf_op jit(solution)/shard_map/ppermute | solution.py:476
  91.8 16.2 %collective-permute-start.29 = (bf16[2,8,16,256]{3,2,1,0:T(8,128)(2,1)S(1)}, bf16[2,8,16,256]{3,2,1,0:T(8,128)(2,1)S(1)}, u32[]{:S(2)}, u32[]{:S(2)}) collective-permute-start(bf16[2,8,16,256]{3,2,1,0:T(8,128)(2,1)S(1)} %get-tuple-element.79), channel_id=1, source_target_pairs={{0,128},{16,144},{32,160},{48,176},{64,192},{80,208},{96,224},{112... | collective-permute-start | bytes 393224 | tf_op jit(solution)/shard_map/ppermute | solution.py:476
  99.0 14.6 %collective-permute-start.31 = (bf16[2,8,16,256]{3,2,1,0:T(8,128)(2,1)S(1)}, bf16[2,8,16,256]{3,2,1,0:T(8,128)(2,1)S(1)}, u32[]{:S(2)}, u32[]{:S(2)}) collective-permute-start(bf16[2,8,16,256]{3,2,1,0:T(8,128)(2,1)S(1)} %get-tuple-element.81), channel_id=1, source_target_pairs={{0,224},{16,240},{32,0},{48,16},{64,32},{80,48},{96,64},{112,80},{... | collective-permute-start | bytes 393224 | tf_op jit(solution)/shard_map/ppermute | solution.py:476
  102.0 13.4 %collective-permute-start.32 = (bf16[8,8,16,256]{3,2,1,0:T(8,128)(2,1)S(1)}, bf16[8,8,16,256]{3,2,1,0:T(8,128)(2,1)S(1)}, u32[]{:S(2)}, u32[]{:S(2)}) collective-permute-start(bf16[8,8,16,256]{3,2,1,0:T(8,128)(2,1)S(1)} %inner_pack.1), channel_id=1, source_target_pairs={{0,16},{16,0},{32,48},{48,32},{64,80},{80,64},{96,112},{112,96},{1... | collective-permute-start | bytes 1572872 | tf_op jit(solution)/shard_map/ppermute | solution.py:472
  (16 other events, 158.8 us)

commit v4 on v3

--- a/solution.py
+++ b/solution.py
@@ -506,8 +506,8 @@
     halo = lax.ppermute(halo, ("member", "domain"), pairs)
     outer = edge_forecast(state, sib, edge_coef, halo)
     outer = exchange(outer)
-    first, obs = lax.optimization_barrier((inner[0], obs))
-    inner = [first, *inner[1:]]
+    tied, obs = lax.optimization_barrier((inner[4], obs))
+    inner[4] = tied
     obs = [lax.ppermute(obs, "member", pairs) for pairs in obs_pairs()]
     inner = exchange(analysis(False, obs, inner))
     inner_sib = swap(pack(inner, "inner_pack"))

time: 121 us -> 120 us (level); the launches traced: 119 us -> 120 us
  waiting for transfers between devices: 13.6 us -> 21.6 us
  starting transfers between devices: 82.2 us -> 74.5 us
    ppermute x28, waiting for transfers between devices: 11.3 us -> 19.9 us  [around(): lax.ppermute(x, 'member', [(i, (i + 2 * distance) % 16) for i in range(16)])]
    ppermute x2, starting transfers between devices: 11.7 us -> 8.45 us  [shards(): obs = [lax.ppermute(obs, 'member', pairs) for pairs in obs_pairs()]]
    ppermute x3, starting transfers between devices: 8.4 us -> 5.86 us  [swap(): return lax.ppermute(x, 'member', [(i, i ^ 1) for i in range(16)])]
    ppermute x28, starting transfers between devices: 59 us -> 57.1 us  [around(): lax.ppermute(x, 'member', [(i, (i + 2 * distance) % 16) for i in range(16)])]
  transfers between devices with their start and end apart: 34 -> 34, of which waited for: 7 -> 10; matrix products, arithmetic and copies ran while one was open for 1% -> 1% of each run, Pallas kernels for 13% -> 13%
where the time goes in v4:
time: 120 us
  starting transfers between devices  74.5 us (62%)
  waiting for transfers between devices  21.6 us (18%)
  Pallas kernels  20.5 us (17%)
  local copies, waits for them, and re-layouts  1.61 us (1%)
    ppermute x28, starting transfers between devices, around(): lax.ppermute(x, 'member', [(i, (i + 2 * distance) % 16) for i in range(16)])  57.1 us
    ppermute x28, waiting for transfers between devices, around(): lax.ppermute(x, 'member', [(i, (i + 2 * distance) % 16) for i in range(16)])  19.9 us
    ppermute x2, starting transfers between devices, shards(): obs = [lax.ppermute(obs, 'member', pairs) for pairs in obs_pairs()]  8.45 us
    pallas_call x2, Pallas kernels, analysis(): pl.pallas_call(functools.partial(analysis_kernel, edge), in_specs=[VMEM]...  8.41 us
    ppermute x3, starting transfers between devices, swap(): return lax.ppermute(x, 'member', [(i, i ^ 1) for i in range(16)])  5.86 us
    pallas_call x1, Pallas kernels, edge_forecast(): pl.pallas_call(edge_kernel, in_specs=[VMEM] * 4, out_specs=[VMEM] * 8, ou...  4.98 us
    ppermute x1, starting transfers between devices, shards(): halo = lax.ppermute(halo, ('member', 'domain'), pairs)  3.1 us
    pallas_call x1, Pallas kernels, own_forecast(): pl.pallas_call(own_kernel, in_specs=[VMEM] * 2, out_specs=[VMEM] * 4, out...  2.46 us
  transfers between devices with their start and end apart: 34, of which 10 were waited for; matrix products, arithmetic and copies ran while one was open for 1% of the time, Pallas kernels for 13%

profile of v4, /device:TPU:7, one launch (start us, length us, event | category | flops | bytes accessed | tf_op | source)
XLA Modules:
  0.0 119.6 jit_solution(12638376904700762719)
XLA Ops:
  3.1 2.5 %own_forecast.1 = (f32[5,6,8,512]{3,2,1,0:T(8,128)S(1)}, f32[5,6,8,512]{3,2,1,0:T(8,128)S(1)}, bf16[8,8,16,256]{3,2,1,0:T(8,128)(2,1)S(1)}, bf16[9,2,16,512]{3,2,1,0:T(8,128)(2,1)S(1)}) custom-call(bf16[16,8,16,512]{3,2,1,0:T(8,128)(2,1)S(1)} %copy-done, f32[3,16,512]{2,1,0:T(8,128)S(1)} %select_select_fusion.numbers), custom_call_target="tpu_custom_call" | custom-call | flops 300000000 | bytes 6000000 | tf_op jit(solution)/shard_map/own_forecast/pallas_call | solution.py:195
  8.0 3.1 %collective-permute-start.17 = (bf16[9,2,32,512]{3,2,1,0:T(8,128)(2,1)S(1)}, bf16[9,2,32,512]{3,2,1,0:T(8,128)(2,1)S(1)}, u32[]{:S(2)}, u32[]{:S(2)}) collective-permute-start(bf16[9,2,32,512]{3,2,1,0:T(8,128)(2,1)S(1)} %get-tuple-element.66), channel_id=1, source_target_pairs={{16,1},{1,16},{17,2},{2,17},{18,3},{3,18},{19,4},{4,19},{20,5},{5,... | collective-permute-start | bytes 1769480 | tf_op jit(solution)/shard_map/ppermute | solution.py:506
  11.2 7.0 %collective-permute-start.1 = (bf16[2,8,16,256]{3,2,1,0:T(8,128)(2,1)S(1)}, bf16[2,8,16,256]{3,2,1,0:T(8,128)(2,1)S(1)}, u32[]{:S(2)}, u32[]{:S(2)}) collective-permute-start(bf16[2,8,16,256]{3,2,1,0:T(8,128)(2,1)S(1)} %get-tuple-element.47), channel_id=1, source_target_pairs={{0,128},{16,144},{32,160},{48,176},{64,192},{80,208},{96,224},{112... | collective-permute-start | bytes 393224 | tf_op jit(solution)/shard_map/ppermute | solution.py:476
  19.8 2.9 %collective-permute-start.5 = (bf16[2,8,16,256]{3,2,1,0:T(8,128)(2,1)S(1)}, bf16[2,8,16,256]{3,2,1,0:T(8,128)(2,1)S(1)}, u32[]{:S(2)}, u32[]{:S(2)}) collective-permute-start(bf16[2,8,16,256]{3,2,1,0:T(8,128)(2,1)S(1)} %get-tuple-element.50), channel_id=1, source_target_pairs={{0,160},{16,176},{32,192},{48,208},{64,224},{80,240},{96,0},{112,1... | collective-permute-start | bytes 393224 | tf_op jit(solution)/shard_map/ppermute | solution.py:476
  23.9 2.4 %collective-permute-start.7 = (bf16[2,8,16,256]{3,2,1,0:T(8,128)(2,1)S(1)}, bf16[2,8,16,256]{3,2,1,0:T(8,128)(2,1)S(1)}, u32[]{:S(2)}, u32[]{:S(2)}) collective-permute-start(bf16[2,8,16,256]{3,2,1,0:T(8,128)(2,1)S(1)} %get-tuple-element.52), channel_id=1, source_target_pairs={{0,192},{16,208},{32,224},{48,240},{64,0},{80,16},{96,32},{112,48}... | collective-permute-start | bytes 393224 | tf_op jit(solution)/shard_map/ppermute | solution.py:476
  26.3 5.0 %edge_forecast.1 = (bf16[2,8,16,256]{3,2,1,0:T(8,128)(2,1)S(1)}, bf16[2,8,16,256]{3,2,1,0:T(8,128)(2,1)S(1)}, bf16[2,8,16,256]{3,2,1,0:T(8,128)(2,1)S(1)}, bf16[...) custom-call(bf16[16,8,16,512]{3,2,1,0:T(8,128)(2,1)S(1)} %copy-done., ...), custom_call_target="tpu_custom_call" | custom-call | flops 300000000 | bytes 6000000 | tf_op jit(solution)/shard_map/edge_forecast/pallas_call | solution.py:231
  32.1 4.1 %collective-permute-done.4.rest_0_ = bf16[2,8,16,256]{3,2,1,0:T(8,128)(2,1)S(1)} collective-permute-done((bf16[2,8,16,256]{3,2,1,0:T(8,128)(2,1)S(1)}, bf16[2,8,16,256]{3,2,1,0:T(8,128)(2,1)S(1)}, u32[]{:S(2)}, u32[]{:S(2)}) %collective-permute-start.4) | collective-permute-done | bytes 131104 | tf_op jit(solution)/shard_map/ppermute | solution.py:476
  38.4 3.0 %collective-permute-start.19 = (bf16[2,8,16,256]{3,2,1,0:T(8,128)(2,1)S(1)}, bf16[2,8,16,256]{3,2,1,0:T(8,128)(2,1)S(1)}, u32[]{:S(2)}, u32[]{:S(2)}) collective-permute-start(bf16[2,8,16,256]{3,2,1,0:T(8,128)(2,1)S(1)} %get-tuple-element.68), channel_id=1, source_target_pairs={{0,160},{16,176},{32,192},{48,208},{64,224},{80,240},{96,0},{112,1... | collective-permute-start | bytes 393224 | tf_op jit(solution)/shard_map/ppermute | solution.py:476
  41.5 5.1 %collective-permute-start.2 = (f32[1,4,4,128]{3,2,1,0:T(4,128)S(1)}, f32[1,4,4,128]{3,2,1,0:T(4,128)S(1)}, u32[]{:S(2)}, u32[]{:S(2)}) collective-permute-start(f32[1,4,4,128]{3,2,1,0:T(4,128)S(1)} %select_select_fusion.1), channel_id=1, source_target_pairs={{0,32},{16,96},{32,160},{48,224},{64,0},{80,64},{96,128},{112,192}... | collective-permute-start | bytes 24584 | tf_op jit(solution)/shard_map/ppermute | solution.py:511
  46.6 3.3 %collective-permute-start.3 = (f32[1,4,4,128]{3,2,1,0:T(4,128)S(1)}, f32[1,4,4,128]{3,2,1,0:T(4,128)S(1)}, u32[]{:S(2)}, u32[]{:S(2)}) collective-permute-start(f32[1,4,4,128]{3,2,1,0:T(4,128)S(1)} %select_select_fusion.1), channel_id=1, source_target_pairs={{0,0},{16,64},{32,128},{48,192},{64,32},{80,96},{96,160},{112,224}... | collective-permute-start | bytes 24584 | tf_op jit(solution)/shard_map/ppermute | solution.py:511
  50.6 3.1 %collective-permute-start.21 = (bf16[2,8,16,256]{3,2,1,0:T(8,128)(2,1)S(1)}, bf16[2,8,16,256]{3,2,1,0:T(8,128)(2,1)S(1)}, u32[]{:S(2)}, u32[]{:S(2)}) collective-permute-start(bf16[2,8,16,256]{3,2,1,0:T(8,128)(2,1)S(1)} %get-tuple-element.70), channel_id=1, source_target_pairs={{0,192},{16,208},{32,224},{48,240},{64,0},{80,16},{96,32},{112,48}... | collective-permute-start | bytes 393224 | tf_op jit(solution)/shard_map/ppermute | solution.py:476
  53.7 4.5 %collective-permute-start.22 = (bf16[2,8,16,256]{3,2,1,0:T(8,128)(2,1)S(1)}, bf16[2,8,16,256]{3,2,1,0:T(8,128)(2,1)S(1)}, u32[]{:S(2)}, u32[]{:S(2)}) collective-permute-start(bf16[2,8,16,256]{3,2,1,0:T(8,128)(2,1)S(1)} %get-tuple-element.71), channel_id=1, source_target_pairs={{0,128},{16,144},{32,160},{48,176},{64,192},{80,208},{96,224},{112... | collective-permute-start | bytes 393224 | tf_op jit(solution)/shard_map/ppermute | solution.py:476
  58.2 2.7 %collective-permute-start.24 = (bf16[2,8,16,256]{3,2,1,0:T(8,128)(2,1)S(1)}, bf16[2,8,16,256]{3,2,1,0:T(8,128)(2,1)S(1)}, u32[]{:S(2)}, u32[]{:S(2)}) collective-permute-start(bf16[2,8,16,256]{3,2,1,0:T(8,128)(2,1)S(1)} %get-tuple-element.73), channel_id=1, source_target_pairs={{0,224},{16,240},{32,0},{48,16},{64,32},{80,48},{96,64},{112,80},{... | collective-permute-start | bytes 393224 | tf_op jit(solution)/shard_map/ppermute | solution.py:476
  60.9 4.2 %inner_analysis.1 = (bf16[2,8,16,256]{3,2,1,0:T(8,128)(2,1)S(1)}, bf16[2,8,16,256]{3,2,1,0:T(8,128)(2,1)S(1)}, bf16[2,8,16,256]{3,2,1,0:T(8,128)(2,1)S(1)}, bf16...) custom-call(f32[1,4,4,128]{3,2,1,0:T(4,128)S(1)} %collective-permute, ...), custom_call_target="tpu_custom_call" | custom-call | flops 2000000000 | bytes 6000000 | tf_op jit(solution)/shard_map/inner_analysis/pallas_call | solution.py:386
  66.7 3.0 %collective-permute-start.11 = (bf16[2,8,16,256]{3,2,1,0:T(8,128)(2,1)S(1)}, bf16[2,8,16,256]{3,2,1,0:T(8,128)(2,1)S(1)}, u32[]{:S(2)}, u32[]{:S(2)}) collective-permute-start(bf16[2,8,16,256]{3,2,1,0:T(8,128)(2,1)S(1)} %get-tuple-element.58), channel_id=1, source_target_pairs={{0,160},{16,176},{32,192},{48,208},{64,224},{80,240},{96,0},{112,1... | collective-permute-start | bytes 393224 | tf_op jit(solution)/shard_map/ppermute | solution.py:476
  69.7 3.6 %collective-permute-start.13 = (bf16[2,8,16,256]{3,2,1,0:T(8,128)(2,1)S(1)}, bf16[2,8,16,256]{3,2,1,0:T(8,128)(2,1)S(1)}, u32[]{:S(2)}, u32[]{:S(2)}) collective-permute-start(bf16[2,8,16,256]{3,2,1,0:T(8,128)(2,1)S(1)} %get-tuple-element.60), channel_id=1, source_target_pairs={{0,192},{16,208},{32,224},{48,240},{64,0},{80,16},{96,32},{112,48}... | collective-permute-start | bytes 393224 | tf_op jit(solution)/shard_map/ppermute | solution.py:476
  74.8 4.2 %edge_analysis.1 = (bf16[2,8,16,256]{3,2,1,0:T(8,128)(2,1)S(1)}, bf16[2,8,16,256]{3,2,1,0:T(8,128)(2,1)S(1)}, bf16[2,8,16,256]{3,2,1,0:T(8,128)(2,1)S(1)}, bf16[...) custom-call(f32[1,4,4,128]{3,2,1,0:T(4,128)S(1)} %collective-permute, ...), custom_call_target="tpu_custom_call" | custom-call | flops 2000000000 | bytes 6000000 | tf_op jit(solution)/shard_map/edge_analysis/pallas_call | solution.py:386
  83.8 2.7 %collective-permute-start.26 = (bf16[2,8,16,256]{3,2,1,0:T(8,128)(2,1)S(1)}, bf16[2,8,16,256]{3,2,1,0:T(8,128)(2,1)S(1)}, u32[]{:S(2)}, u32[]{:S(2)}) collective-permute-start(bf16[2,8,16,256]{3,2,1,0:T(8,128)(2,1)S(1)} %get-tuple-element.76), channel_id=1, source_target_pairs={{0,160},{16,176},{32,192},{48,208},{64,224},{80,240},{96,0},{112,1... | collective-permute-start | bytes 393224 | tf_op jit(solution)/shard_map/ppermute | solution.py:476
  87.6 2.8 %collective-permute-start.27 = (bf16[2,8,16,256]{3,2,1,0:T(8,128)(2,1)S(1)}, bf16[2,8,16,256]{3,2,1,0:T(8,128)(2,1)S(1)}, u32[]{:S(2)}, u32[]{:S(2)}) collective-permute-start(bf16[2,8,16,256]{3,2,1,0:T(8,128)(2,1)S(1)} %get-tuple-element.77), channel_id=1, source_target_pairs={{0,64},{16,80},{32,96},{48,112},{64,128},{80,144},{96,160},{112,17... | collective-permute-start | bytes 393224 | tf_op jit(solution)/shard_map/ppermute | solution.py:476
  93.9 2.4 %collective-permute-start.29 = (bf16[2,8,16,256]{3,2,1,0:T(8,128)(2,1)S(1)}, bf16[2,8,16,256]{3,2,1,0:T(8,128)(2,1)S(1)}, u32[]{:S(2)}, u32[]{:S(2)}) collective-permute-start(bf16[2,8,16,256]{3,2,1,0:T(8,128)(2,1)S(1)} %get-tuple-element.79), channel_id=1, source_target_pairs={{0,128},{16,144},{32,160},{48,176},{64,192},{80,208},{96,224},{112... | collective-permute-start | bytes 393224 | tf_op jit(solution)/shard_map/ppermute | solution.py:476
  96.3 4.8 %collective-permute-done.25.refs_0_.refs_8_ = bf16[2,8,16,256]{3,2,1,0:T(8,128)(2,1)S(1)} collective-permute-done((bf16[2,8,16,256]{3,2,1,0:T(8,128)(2,1)S(1)}, bf16[2,8,16,256]{3,2,1,0:T(8,128)(2,1)S(1)}, u32[]{:S(2)}, u32[]{:S(2)}) %collective-permute-start.25) | collective-permute-done | bytes 131104 | tf_op jit(solution)/shard_map/ppermute | solution.py:476
  101.1 2.7 %collective-permute-start.31 = (bf16[2,8,16,256]{3,2,1,0:T(8,128)(2,1)S(1)}, bf16[2,8,16,256]{3,2,1,0:T(8,128)(2,1)S(1)}, u32[]{:S(2)}, u32[]{:S(2)}) collective-permute-start(bf16[2,8,16,256]{3,2,1,0:T(8,128)(2,1)S(1)} %get-tuple-element.81), channel_id=1, source_target_pairs={{0,224},{16,240},{32,0},{48,16},{64,32},{80,48},{96,64},{112,80},{... | collective-permute-start | bytes 393224 | tf_op jit(solution)/shard_map/ppermute | solution.py:476
  103.8 3.3 %collective-permute-start.32 = (bf16[8,8,16,256]{3,2,1,0:T(8,128)(2,1)S(1)}, bf16[8,8,16,256]{3,2,1,0:T(8,128)(2,1)S(1)}, u32[]{:S(2)}, u32[]{:S(2)}) collective-permute-start(bf16[8,8,16,256]{3,2,1,0:T(8,128)(2,1)S(1)} %inner_pack.1), channel_id=1, source_target_pairs={{0,16},{16,0},{32,48},{48,32},{64,80},{80,64},{96,112},{112,96},{1... | collective-permute-start | bytes 1572872 | tf_op jit(solution)/shard_map/ppermute | solution.py:472
  107.5 6.3 %collective-permute-done.30.refs_5_.refs_13_ = bf16[2,8,16,256]{3,2,1,0:T(8,128)(2,1)S(1)} collective-permute-done((bf16[2,8,16,256]{3,2,1,0:T(8,128)(2,1)S(1)}, bf16[2,8,16,256]{3,2,1,0:T(8,128)(2,1)S(1)}, u32[]{:S(2)}, u32[]{:S(2)}) %collective-permute-start.30) | collective-permute-done | bytes 131104 | tf_op jit(solution)/shard_map/ppermute | solution.py:476
  (71 shorter events, 30.7 us)
Async XLA Ops:
  8.0 15.8 %collective-permute-start.17 = (bf16[9,2,32,512]{3,2,1,0:T(8,128)(2,1)S(1)}, bf16[9,2,32,512]{3,2,1,0:T(8,128)(2,1)S(1)}, u32[]{:S(2)}, u32[]{:S(2)}) collective-permute-start(bf16[9,2,32,512]{3,2,1,0:T(8,128)(2,1)S(1)} %get-tuple-element.66), channel_id=1, source_target_pairs={{16,1},{1,16},{17,2},{2,17},{18,3},{3,18},{19,4},{4,19},{20,5},{5,... | collective-permute-start | bytes 1769480 | tf_op jit(solution)/shard_map/ppermute | solution.py:506
  11.2 20.1 %collective-permute-start.1 = (bf16[2,8,16,256]{3,2,1,0:T(8,128)(2,1)S(1)}, bf16[2,8,16,256]{3,2,1,0:T(8,128)(2,1)S(1)}, u32[]{:S(2)}, u32[]{:S(2)}) collective-permute-start(bf16[2,8,16,256]{3,2,1,0:T(8,128)(2,1)S(1)} %get-tuple-element.47), channel_id=1, source_target_pairs={{0,128},{16,144},{32,160},{48,176},{64,192},{80,208},{96,224},{112... | collective-permute-start | bytes 393224 | tf_op jit(solution)/shard_map/ppermute | solution.py:476
  18.2 17.9 %collective-permute-start.4 = (bf16[2,8,16,256]{3,2,1,0:T(8,128)(2,1)S(1)}, bf16[2,8,16,256]{3,2,1,0:T(8,128)(2,1)S(1)}, u32[]{:S(2)}, u32[]{:S(2)}) collective-permute-start(bf16[2,8,16,256]{3,2,1,0:T(8,128)(2,1)S(1)} %get-tuple-element.49), channel_id=1, source_target_pairs={{0,96},{16,112},{32,128},{48,144},{64,160},{80,176},{96,192},{112,... | collective-permute-start | bytes 393224 | tf_op jit(solution)/shard_map/ppermute | solution.py:476
  19.8 16.3 %collective-permute-start.5 = (bf16[2,8,16,256]{3,2,1,0:T(8,128)(2,1)S(1)}, bf16[2,8,16,256]{3,2,1,0:T(8,128)(2,1)S(1)}, u32[]{:S(2)}, u32[]{:S(2)}) collective-permute-start(bf16[2,8,16,256]{3,2,1,0:T(8,128)(2,1)S(1)} %get-tuple-element.50), channel_id=1, source_target_pairs={{0,160},{16,176},{32,192},{48,208},{64,224},{80,240},{96,0},{112,1... | collective-permute-start | bytes 393224 | tf_op jit(solution)/shard_map/ppermute | solution.py:476
  22.7 15.7 %collective-permute-start.6 = (bf16[2,8,16,256]{3,2,1,0:T(8,128)(2,1)S(1)}, bf16[2,8,16,256]{3,2,1,0:T(8,128)(2,1)S(1)}, u32[]{:S(2)}, u32[]{:S(2)}) collective-permute-start(bf16[2,8,16,256]{3,2,1,0:T(8,128)(2,1)S(1)} %get-tuple-element.51), channel_id=1, source_target_pairs={{0,64},{16,80},{32,96},{48,112},{64,128},{80,144},{96,160},{112,17... | collective-permute-start | bytes 393224 | tf_op jit(solution)/shard_map/ppermute | solution.py:476
  23.9 17.6 %collective-permute-start.7 = (bf16[2,8,16,256]{3,2,1,0:T(8,128)(2,1)S(1)}, bf16[2,8,16,256]{3,2,1,0:T(8,128)(2,1)S(1)}, u32[]{:S(2)}, u32[]{:S(2)}) collective-permute-start(bf16[2,8,16,256]{3,2,1,0:T(8,128)(2,1)S(1)} %get-tuple-element.52), channel_id=1, source_target_pairs={{0,192},{16,208},{32,224},{48,240},{64,0},{80,16},{96,32},{112,48}... | collective-permute-start | bytes 393224 | tf_op jit(solution)/shard_map/ppermute | solution.py:476
  31.3 15.3 %collective-permute-start.8 = (bf16[2,8,16,256]{3,2,1,0:T(8,128)(2,1)S(1)}, bf16[2,8,16,256]{3,2,1,0:T(8,128)(2,1)S(1)}, u32[]{:S(2)}, u32[]{:S(2)}) collective-permute-start(bf16[2,8,16,256]{3,2,1,0:T(8,128)(2,1)S(1)} %get-tuple-element.54), channel_id=1, source_target_pairs={{0,32},{16,48},{32,64},{48,80},{64,96},{80,112},{96,128},{112,144}... | collective-permute-start | bytes 393224 | tf_op jit(solution)/shard_map/ppermute | solution.py:476
  36.2 13.8 %collective-permute-start.9 = (bf16[2,8,16,256]{3,2,1,0:T(8,128)(2,1)S(1)}, bf16[2,8,16,256]{3,2,1,0:T(8,128)(2,1)S(1)}, u32[]{:S(2)}, u32[]{:S(2)}) collective-permute-start(bf16[2,8,16,256]{3,2,1,0:T(8,128)(2,1)S(1)} %get-tuple-element.55), channel_id=1, source_target_pairs={{0,224},{16,240},{32,0},{48,16},{64,32},{80,48},{96,64},{112,80},{... | collective-permute-start | bytes 393224 | tf_op jit(solution)/shard_map/ppermute | solution.py:476
  36.2 22.1 %collective-permute-start.18 = (bf16[2,8,16,256]{3,2,1,0:T(8,128)(2,1)S(1)}, bf16[2,8,16,256]{3,2,1,0:T(8,128)(2,1)S(1)}, u32[]{:S(2)}, u32[]{:S(2)}) collective-permute-start(bf16[2,8,16,256]{3,2,1,0:T(8,128)(2,1)S(1)} %get-tuple-element.67), channel_id=1, source_target_pairs={{0,96},{16,112},{32,128},{48,144},{64,160},{80,176},{96,192},{112,... | collective-permute-start | bytes 393224 | tf_op jit(solution)/shard_map/ppermute | solution.py:476
  38.4 19.8 %collective-permute-start.19 = (bf16[2,8,16,256]{3,2,1,0:T(8,128)(2,1)S(1)}, bf16[2,8,16,256]{3,2,1,0:T(8,128)(2,1)S(1)}, u32[]{:S(2)}, u32[]{:S(2)}) collective-permute-start(bf16[2,8,16,256]{3,2,1,0:T(8,128)(2,1)S(1)} %get-tuple-element.68), channel_id=1, source_target_pairs={{0,160},{16,176},{32,192},{48,208},{64,224},{80,240},{96,0},{112,1... | collective-permute-start | bytes 393224 | tf_op jit(solution)/shard_map/ppermute | solution.py:476
  50.0 15.1 %collective-permute-start.20 = (bf16[2,8,16,256]{3,2,1,0:T(8,128)(2,1)S(1)}, bf16[2,8,16,256]{3,2,1,0:T(8,128)(2,1)S(1)}, u32[]{:S(2)}, u32[]{:S(2)}) collective-permute-start(bf16[2,8,16,256]{3,2,1,0:T(8,128)(2,1)S(1)} %get-tuple-element.69), channel_id=1, source_target_pairs={{0,64},{16,80},{32,96},{48,112},{64,128},{80,144},{96,160},{112,17... | collective-permute-start | bytes 393224 | tf_op jit(solution)/shard_map/ppermute | solution.py:476
  50.6 16.1 %collective-permute-start.21 = (bf16[2,8,16,256]{3,2,1,0:T(8,128)(2,1)S(1)}, bf16[2,8,16,256]{3,2,1,0:T(8,128)(2,1)S(1)}, u32[]{:S(2)}, u32[]{:S(2)}) collective-permute-start(bf16[2,8,16,256]{3,2,1,0:T(8,128)(2,1)S(1)} %get-tuple-element.70), channel_id=1, source_target_pairs={{0,192},{16,208},{32,224},{48,240},{64,0},{80,16},{96,32},{112,48}... | collective-permute-start | bytes 393224 | tf_op jit(solution)/shard_map/ppermute | solution.py:476
  53.7 16.0 %collective-permute-start.22 = (bf16[2,8,16,256]{3,2,1,0:T(8,128)(2,1)S(1)}, bf16[2,8,16,256]{3,2,1,0:T(8,128)(2,1)S(1)}, u32[]{:S(2)}, u32[]{:S(2)}) collective-permute-start(bf16[2,8,16,256]{3,2,1,0:T(8,128)(2,1)S(1)} %get-tuple-element.71), channel_id=1, source_target_pairs={{0,128},{16,144},{32,160},{48,176},{64,192},{80,208},{96,224},{112... | collective-permute-start | bytes 393224 | tf_op jit(solution)/shard_map/ppermute | solution.py:476
  58.2 15.0 %collective-permute-start.24 = (bf16[2,8,16,256]{3,2,1,0:T(8,128)(2,1)S(1)}, bf16[2,8,16,256]{3,2,1,0:T(8,128)(2,1)S(1)}, u32[]{:S(2)}, u32[]{:S(2)}) collective-permute-start(bf16[2,8,16,256]{3,2,1,0:T(8,128)(2,1)S(1)} %get-tuple-element.73), channel_id=1, source_target_pairs={{0,224},{16,240},{32,0},{48,16},{64,32},{80,48},{96,64},{112,80},{... | collective-permute-start | bytes 393224 | tf_op jit(solution)/shard_map/ppermute | solution.py:476
  65.1 13.9 %collective-permute-start.10 = (bf16[2,8,16,256]{3,2,1,0:T(8,128)(2,1)S(1)}, bf16[2,8,16,256]{3,2,1,0:T(8,128)(2,1)S(1)}, u32[]{:S(2)}, u32[]{:S(2)}) collective-permute-start(bf16[2,8,16,256]{3,2,1,0:T(8,128)(2,1)S(1)} %get-tuple-element.57), channel_id=1, source_target_pairs={{0,96},{16,112},{32,128},{48,144},{64,160},{80,176},{96,192},{112,... | collective-permute-start | bytes 393224 | tf_op jit(solution)/shard_map/ppermute | solution.py:476
  66.7 14.4 %collective-permute-start.11 = (bf16[2,8,16,256]{3,2,1,0:T(8,128)(2,1)S(1)}, bf16[2,8,16,256]{3,2,1,0:T(8,128)(2,1)S(1)}, u32[]{:S(2)}, u32[]{:S(2)}) collective-permute-start(bf16[2,8,16,256]{3,2,1,0:T(8,128)(2,1)S(1)} %get-tuple-element.58), channel_id=1, source_target_pairs={{0,160},{16,176},{32,192},{48,208},{64,224},{80,240},{96,0},{112,1... | collective-permute-start | bytes 393224 | tf_op jit(solution)/shard_map/ppermute | solution.py:476
  69.7 14.1 %collective-permute-start.13 = (bf16[2,8,16,256]{3,2,1,0:T(8,128)(2,1)S(1)}, bf16[2,8,16,256]{3,2,1,0:T(8,128)(2,1)S(1)}, u32[]{:S(2)}, u32[]{:S(2)}) collective-permute-start(bf16[2,8,16,256]{3,2,1,0:T(8,128)(2,1)S(1)} %get-tuple-element.60), channel_id=1, source_target_pairs={{0,192},{16,208},{32,224},{48,240},{64,0},{80,16},{96,32},{112,48}... | collective-permute-start | bytes 393224 | tf_op jit(solution)/shard_map/ppermute | solution.py:476
  73.3 14.4 %collective-permute-start.14 = (bf16[2,8,16,256]{3,2,1,0:T(8,128)(2,1)S(1)}, bf16[2,8,16,256]{3,2,1,0:T(8,128)(2,1)S(1)}, u32[]{:S(2)}, u32[]{:S(2)}) collective-permute-start(bf16[2,8,16,256]{3,2,1,0:T(8,128)(2,1)S(1)} %get-tuple-element.61), channel_id=1, source_target_pairs={{0,128},{16,144},{32,160},{48,176},{64,192},{80,208},{96,224},{112... | collective-permute-start | bytes 393224 | tf_op jit(solution)/shard_map/ppermute | solution.py:476
  79.0 13.0 %collective-permute-start.15 = (bf16[2,8,16,256]{3,2,1,0:T(8,128)(2,1)S(1)}, bf16[2,8,16,256]{3,2,1,0:T(8,128)(2,1)S(1)}, u32[]{:S(2)}, u32[]{:S(2)}) collective-permute-start(bf16[2,8,16,256]{3,2,1,0:T(8,128)(2,1)S(1)} %get-tuple-element.62), channel_id=1, source_target_pairs={{0,32},{16,48},{32,64},{48,80},{64,96},{80,112},{96,128},{112,144}... | collective-permute-start | bytes 393224 | tf_op jit(solution)/shard_map/ppermute | solution.py:476
  82.0 19.1 %collective-permute-start.25 = (bf16[2,8,16,256]{3,2,1,0:T(8,128)(2,1)S(1)}, bf16[2,8,16,256]{3,2,1,0:T(8,128)(2,1)S(1)}, u32[]{:S(2)}, u32[]{:S(2)}) collective-permute-start(bf16[2,8,16,256]{3,2,1,0:T(8,128)(2,1)S(1)} %get-tuple-element.75), channel_id=1, source_target_pairs={{0,96},{16,112},{32,128},{48,144},{64,160},{80,176},{96,192},{112,... | collective-permute-start | bytes 393224 | tf_op jit(solution)/shard_map/ppermute | solution.py:476
  83.8 17.3 %collective-permute-start.26 = (bf16[2,8,16,256]{3,2,1,0:T(8,128)(2,1)S(1)}, bf16[2,8,16,256]{3,2,1,0:T(8,128)(2,1)S(1)}, u32[]{:S(2)}, u32[]{:S(2)}) collective-permute-start(bf16[2,8,16,256]{3,2,1,0:T(8,128)(2,1)S(1)} %get-tuple-element.76), channel_id=1, source_target_pairs={{0,160},{16,176},{32,192},{48,208},{64,224},{80,240},{96,0},{112,1... | collective-permute-start | bytes 393224 | tf_op jit(solution)/shard_map/ppermute | solution.py:476
  87.6 16.2 %collective-permute-start.27 = (bf16[2,8,16,256]{3,2,1,0:T(8,128)(2,1)S(1)}, bf16[2,8,16,256]{3,2,1,0:T(8,128)(2,1)S(1)}, u32[]{:S(2)}, u32[]{:S(2)}) collective-permute-start(bf16[2,8,16,256]{3,2,1,0:T(8,128)(2,1)S(1)} %get-tuple-element.77), channel_id=1, source_target_pairs={{0,64},{16,80},{32,96},{48,112},{64,128},{80,144},{96,160},{112,17... | collective-permute-start | bytes 393224 | tf_op jit(solution)/shard_map/ppermute | solution.py:476
  92.0 15.2 %collective-permute-start.28 = (bf16[2,8,16,256]{3,2,1,0:T(8,128)(2,1)S(1)}, bf16[2,8,16,256]{3,2,1,0:T(8,128)(2,1)S(1)}, u32[]{:S(2)}, u32[]{:S(2)}) collective-permute-start(bf16[2,8,16,256]{3,2,1,0:T(8,128)(2,1)S(1)} %get-tuple-element.78), channel_id=1, source_target_pairs={{0,192},{16,208},{32,224},{48,240},{64,0},{80,16},{96,32},{112,48}... | collective-permute-start | bytes 393224 | tf_op jit(solution)/shard_map/ppermute | solution.py:476
  93.9 13.5 %collective-permute-start.29 = (bf16[2,8,16,256]{3,2,1,0:T(8,128)(2,1)S(1)}, bf16[2,8,16,256]{3,2,1,0:T(8,128)(2,1)S(1)}, u32[]{:S(2)}, u32[]{:S(2)}) collective-permute-start(bf16[2,8,16,256]{3,2,1,0:T(8,128)(2,1)S(1)} %get-tuple-element.79), channel_id=1, source_target_pairs={{0,128},{16,144},{32,160},{48,176},{64,192},{80,208},{96,224},{112... | collective-permute-start | bytes 393224 | tf_op jit(solution)/shard_map/ppermute | solution.py:476
  (16 other events, 162.6 us)

commit v5 on v4

--- a/solution.py
+++ b/solution.py
@@ -204,7 +204,7 @@
             pltpu.VMEM((2, 8, 16, 256), BF16),
         ],
         compiler_params=LIMIT,
-        cost_estimate=cost(300_000_000, 6_000_000),
+        cost_estimate=cost(3_000_000_000, 6_000_000),
         name="own_forecast",
     )(own, numbers)
 
@@ -222,7 +222,7 @@
             pltpu.VMEM((2, 8, 16, 256), BF16),
         ],
         compiler_params=LIMIT,
-        cost_estimate=cost(300_000_000, 6_000_000),
+        cost_estimate=cost(3_000_000_000, 6_000_000),
         name="sib_forecast",
     )(sib, coef, part, halo)
 
@@ -241,7 +241,7 @@
             pltpu.VMEM((2, 8, 32, 256), BF16),
         ],
         compiler_params=LIMIT,
-        cost_estimate=cost(300_000_000, 6_000_000),
+        cost_estimate=cost(3_000_000_000, 6_000_000),
         name="edge_forecast",
     )(own, sib, coef, halo)
 
@@ -390,7 +390,7 @@
         out_shape=[jax.ShapeDtypeStruct(PIECE, BF16)] * 8,
         scratch_shapes=[pltpu.VMEM((2, 256, 1024), BF16)],
         compiler_params=LIMIT,
-        cost_estimate=cost(2_000_000_000, 6_000_000),
+        cost_estimate=cost(5_000_000_000, 6_000_000),
         name="edge_analysis" if edge else "inner_analysis",
     )(*obs, *pieces)
 

time: 120 us -> 120 us (level)
  no operation moved by 1% of the time
where the time goes in v5:
time: 120 us
  starting transfers between devices  75.6 us (63%)
  Pallas kernels  20.5 us (17%)
  waiting for transfers between devices  20.5 us (17%)
  local copies, waits for them, and re-layouts  1.61 us (1%)
    ppermute x28, starting transfers between devices, around(): lax.ppermute(x, 'member', [(i, (i + 2 * distance) % 16) for i in range(16)])  57.9 us
    ppermute x28, waiting for transfers between devices, around(): lax.ppermute(x, 'member', [(i, (i + 2 * distance) % 16) for i in range(16)])  18.9 us
    ppermute x2, starting transfers between devices, shards(): obs = [lax.ppermute(obs, 'member', pairs) for pairs in obs_pairs()]  8.45 us
    pallas_call x2, Pallas kernels, analysis(): pl.pallas_call(functools.partial(analysis_kernel, edge), in_specs=[VMEM]...  8.41 us
    ppermute x3, starting transfers between devices, swap(): return lax.ppermute(x, 'member', [(i, i ^ 1) for i in range(16)])  6.13 us
    pallas_call x1, Pallas kernels, edge_forecast(): pl.pallas_call(edge_kernel, in_specs=[VMEM] * 4, out_specs=[VMEM] * 8, ou...  4.98 us
    ppermute x1, starting transfers between devices, shards(): halo = lax.ppermute(halo, ('member', 'domain'), pairs)  3.1 us
    pallas_call x1, Pallas kernels, own_forecast(): pl.pallas_call(own_kernel, in_specs=[VMEM] * 2, out_specs=[VMEM] * 4, out...  2.46 us
  transfers between devices with their start and end apart: 34, of which 10 were waited for; matrix products, arithmetic and copies ran while one was open for 1% of the time, Pallas kernels for 13%

profile of v5, /device:TPU:7, one launch (start us, length us, event | category | flops | bytes accessed | tf_op | source)
XLA Modules:
  0.0 119.6 jit_solution(17178765436719012747)
XLA Ops:
  3.1 2.5 %own_forecast.1 = (f32[5,6,8,512]{3,2,1,0:T(8,128)S(1)}, f32[5,6,8,512]{3,2,1,0:T(8,128)S(1)}, bf16[8,8,16,256]{3,2,1,0:T(8,128)(2,1)S(1)}, bf16[9,2,16,512]{3,2,1,0:T(8,128)(2,1)S(1)}) custom-call(bf16[16,8,16,512]{3,2,1,0:T(8,128)(2,1)S(1)} %copy-done, f32[3,16,512]{2,1,0:T(8,128)S(1)} %select_select_fusion.numbers), custom_call_target="tpu_custom_call" | custom-call | flops 3000000000 | bytes 6000000 | tf_op jit(solution)/shard_map/own_forecast/pallas_call | solution.py:195
  8.0 3.1 %collective-permute-start.17 = (bf16[9,2,32,512]{3,2,1,0:T(8,128)(2,1)S(1)}, bf16[9,2,32,512]{3,2,1,0:T(8,128)(2,1)S(1)}, u32[]{:S(2)}, u32[]{:S(2)}) collective-permute-start(bf16[9,2,32,512]{3,2,1,0:T(8,128)(2,1)S(1)} %get-tuple-element.66), channel_id=1, source_target_pairs={{16,1},{1,16},{17,2},{2,17},{18,3},{3,18},{19,4},{4,19},{20,5},{5,... | collective-permute-start | bytes 1769480 | tf_op jit(solution)/shard_map/ppermute | solution.py:506
  11.2 7.0 %collective-permute-start.1 = (bf16[2,8,16,256]{3,2,1,0:T(8,128)(2,1)S(1)}, bf16[2,8,16,256]{3,2,1,0:T(8,128)(2,1)S(1)}, u32[]{:S(2)}, u32[]{:S(2)}) collective-permute-start(bf16[2,8,16,256]{3,2,1,0:T(8,128)(2,1)S(1)} %get-tuple-element.47), channel_id=1, source_target_pairs={{0,128},{16,144},{32,160},{48,176},{64,192},{80,208},{96,224},{112... | collective-permute-start | bytes 393224 | tf_op jit(solution)/shard_map/ppermute | solution.py:476
  19.8 2.9 %collective-permute-start.5 = (bf16[2,8,16,256]{3,2,1,0:T(8,128)(2,1)S(1)}, bf16[2,8,16,256]{3,2,1,0:T(8,128)(2,1)S(1)}, u32[]{:S(2)}, u32[]{:S(2)}) collective-permute-start(bf16[2,8,16,256]{3,2,1,0:T(8,128)(2,1)S(1)} %get-tuple-element.50), channel_id=1, source_target_pairs={{0,160},{16,176},{32,192},{48,208},{64,224},{80,240},{96,0},{112,1... | collective-permute-start | bytes 393224 | tf_op jit(solution)/shard_map/ppermute | solution.py:476
  23.9 2.4 %collective-permute-start.7 = (bf16[2,8,16,256]{3,2,1,0:T(8,128)(2,1)S(1)}, bf16[2,8,16,256]{3,2,1,0:T(8,128)(2,1)S(1)}, u32[]{:S(2)}, u32[]{:S(2)}) collective-permute-start(bf16[2,8,16,256]{3,2,1,0:T(8,128)(2,1)S(1)} %get-tuple-element.52), channel_id=1, source_target_pairs={{0,192},{16,208},{32,224},{48,240},{64,0},{80,16},{96,32},{112,48}... | collective-permute-start | bytes 393224 | tf_op jit(solution)/shard_map/ppermute | solution.py:476
  26.3 5.0 %edge_forecast.1 = (bf16[2,8,16,256]{3,2,1,0:T(8,128)(2,1)S(1)}, bf16[2,8,16,256]{3,2,1,0:T(8,128)(2,1)S(1)}, bf16[2,8,16,256]{3,2,1,0:T(8,128)(2,1)S(1)}, bf16[...) custom-call(bf16[16,8,16,512]{3,2,1,0:T(8,128)(2,1)S(1)} %copy-done., ...), custom_call_target="tpu_custom_call" | custom-call | flops 3000000000 | bytes 6000000 | tf_op jit(solution)/shard_map/edge_forecast/pallas_call | solution.py:231
  32.1 4.1 %collective-permute-done.4.rest_0_ = bf16[2,8,16,256]{3,2,1,0:T(8,128)(2,1)S(1)} collective-permute-done((bf16[2,8,16,256]{3,2,1,0:T(8,128)(2,1)S(1)}, bf16[2,8,16,256]{3,2,1,0:T(8,128)(2,1)S(1)}, u32[]{:S(2)}, u32[]{:S(2)}) %collective-permute-start.4) | collective-permute-done | bytes 131104 | tf_op jit(solution)/shard_map/ppermute | solution.py:476
  38.4 3.0 %collective-permute-start.19 = (bf16[2,8,16,256]{3,2,1,0:T(8,128)(2,1)S(1)}, bf16[2,8,16,256]{3,2,1,0:T(8,128)(2,1)S(1)}, u32[]{:S(2)}, u32[]{:S(2)}) collective-permute-start(bf16[2,8,16,256]{3,2,1,0:T(8,128)(2,1)S(1)} %get-tuple-element.68), channel_id=1, source_target_pairs={{0,160},{16,176},{32,192},{48,208},{64,224},{80,240},{96,0},{112,1... | collective-permute-start | bytes 393224 | tf_op jit(solution)/shard_map/ppermute | solution.py:476
  41.5 5.1 %collective-permute-start.2 = (f32[1,4,4,128]{3,2,1,0:T(4,128)S(1)}, f32[1,4,4,128]{3,2,1,0:T(4,128)S(1)}, u32[]{:S(2)}, u32[]{:S(2)}) collective-permute-start(f32[1,4,4,128]{3,2,1,0:T(4,128)S(1)} %select_select_fusion.1), channel_id=1, source_target_pairs={{0,32},{16,96},{32,160},{48,224},{64,0},{80,64},{96,128},{112,192}... | collective-permute-start | bytes 24584 | tf_op jit(solution)/shard_map/ppermute | solution.py:511
  46.6 3.3 %collective-permute-start.3 = (f32[1,4,4,128]{3,2,1,0:T(4,128)S(1)}, f32[1,4,4,128]{3,2,1,0:T(4,128)S(1)}, u32[]{:S(2)}, u32[]{:S(2)}) collective-permute-start(f32[1,4,4,128]{3,2,1,0:T(4,128)S(1)} %select_select_fusion.1), channel_id=1, source_target_pairs={{0,0},{16,64},{32,128},{48,192},{64,32},{80,96},{96,160},{112,224}... | collective-permute-start | bytes 24584 | tf_op jit(solution)/shard_map/ppermute | solution.py:511
  50.6 3.0 %collective-permute-start.21 = (bf16[2,8,16,256]{3,2,1,0:T(8,128)(2,1)S(1)}, bf16[2,8,16,256]{3,2,1,0:T(8,128)(2,1)S(1)}, u32[]{:S(2)}, u32[]{:S(2)}) collective-permute-start(bf16[2,8,16,256]{3,2,1,0:T(8,128)(2,1)S(1)} %get-tuple-element.70), channel_id=1, source_target_pairs={{0,192},{16,208},{32,224},{48,240},{64,0},{80,16},{96,32},{112,48}... | collective-permute-start | bytes 393224 | tf_op jit(solution)/shard_map/ppermute | solution.py:476
  53.7 4.5 %collective-permute-start.22 = (bf16[2,8,16,256]{3,2,1,0:T(8,128)(2,1)S(1)}, bf16[2,8,16,256]{3,2,1,0:T(8,128)(2,1)S(1)}, u32[]{:S(2)}, u32[]{:S(2)}) collective-permute-start(bf16[2,8,16,256]{3,2,1,0:T(8,128)(2,1)S(1)} %get-tuple-element.71), channel_id=1, source_target_pairs={{0,128},{16,144},{32,160},{48,176},{64,192},{80,208},{96,224},{112... | collective-permute-start | bytes 393224 | tf_op jit(solution)/shard_map/ppermute | solution.py:476
  58.3 2.7 %collective-permute-start.24 = (bf16[2,8,16,256]{3,2,1,0:T(8,128)(2,1)S(1)}, bf16[2,8,16,256]{3,2,1,0:T(8,128)(2,1)S(1)}, u32[]{:S(2)}, u32[]{:S(2)}) collective-permute-start(bf16[2,8,16,256]{3,2,1,0:T(8,128)(2,1)S(1)} %get-tuple-element.73), channel_id=1, source_target_pairs={{0,224},{16,240},{32,0},{48,16},{64,32},{80,48},{96,64},{112,80},{... | collective-permute-start | bytes 393224 | tf_op jit(solution)/shard_map/ppermute | solution.py:476
  60.9 4.2 %inner_analysis.1 = (bf16[2,8,16,256]{3,2,1,0:T(8,128)(2,1)S(1)}, bf16[2,8,16,256]{3,2,1,0:T(8,128)(2,1)S(1)}, bf16[2,8,16,256]{3,2,1,0:T(8,128)(2,1)S(1)}, bf16...) custom-call(f32[1,4,4,128]{3,2,1,0:T(4,128)S(1)} %collective-permute, ...), custom_call_target="tpu_custom_call" | custom-call | flops 5000000000 | bytes 6000000 | tf_op jit(solution)/shard_map/inner_analysis/pallas_call | solution.py:386
  66.7 3.0 %collective-permute-start.11 = (bf16[2,8,16,256]{3,2,1,0:T(8,128)(2,1)S(1)}, bf16[2,8,16,256]{3,2,1,0:T(8,128)(2,1)S(1)}, u32[]{:S(2)}, u32[]{:S(2)}) collective-permute-start(bf16[2,8,16,256]{3,2,1,0:T(8,128)(2,1)S(1)} %get-tuple-element.58), channel_id=1, source_target_pairs={{0,160},{16,176},{32,192},{48,208},{64,224},{80,240},{96,0},{112,1... | collective-permute-start | bytes 393224 | tf_op jit(solution)/shard_map/ppermute | solution.py:476
  69.7 3.6 %collective-permute-start.13 = (bf16[2,8,16,256]{3,2,1,0:T(8,128)(2,1)S(1)}, bf16[2,8,16,256]{3,2,1,0:T(8,128)(2,1)S(1)}, u32[]{:S(2)}, u32[]{:S(2)}) collective-permute-start(bf16[2,8,16,256]{3,2,1,0:T(8,128)(2,1)S(1)} %get-tuple-element.60), channel_id=1, source_target_pairs={{0,192},{16,208},{32,224},{48,240},{64,0},{80,16},{96,32},{112,48}... | collective-permute-start | bytes 393224 | tf_op jit(solution)/shard_map/ppermute | solution.py:476
  74.8 4.2 %edge_analysis.1 = (bf16[2,8,16,256]{3,2,1,0:T(8,128)(2,1)S(1)}, bf16[2,8,16,256]{3,2,1,0:T(8,128)(2,1)S(1)}, bf16[2,8,16,256]{3,2,1,0:T(8,128)(2,1)S(1)}, bf16[...) custom-call(f32[1,4,4,128]{3,2,1,0:T(4,128)S(1)} %collective-permute, ...), custom_call_target="tpu_custom_call" | custom-call | flops 5000000000 | bytes 6000000 | tf_op jit(solution)/shard_map/edge_analysis/pallas_call | solution.py:386
  83.8 2.7 %collective-permute-start.26 = (bf16[2,8,16,256]{3,2,1,0:T(8,128)(2,1)S(1)}, bf16[2,8,16,256]{3,2,1,0:T(8,128)(2,1)S(1)}, u32[]{:S(2)}, u32[]{:S(2)}) collective-permute-start(bf16[2,8,16,256]{3,2,1,0:T(8,128)(2,1)S(1)} %get-tuple-element.76), channel_id=1, source_target_pairs={{0,160},{16,176},{32,192},{48,208},{64,224},{80,240},{96,0},{112,1... | collective-permute-start | bytes 393224 | tf_op jit(solution)/shard_map/ppermute | solution.py:476
  86.8 3.6 %collective-permute-start.27 = (bf16[2,8,16,256]{3,2,1,0:T(8,128)(2,1)S(1)}, bf16[2,8,16,256]{3,2,1,0:T(8,128)(2,1)S(1)}, u32[]{:S(2)}, u32[]{:S(2)}) collective-permute-start(bf16[2,8,16,256]{3,2,1,0:T(8,128)(2,1)S(1)} %get-tuple-element.77), channel_id=1, source_target_pairs={{0,64},{16,80},{32,96},{48,112},{64,128},{80,144},{96,160},{112,17... | collective-permute-start | bytes 393224 | tf_op jit(solution)/shard_map/ppermute | solution.py:476
  93.9 2.4 %collective-permute-start.29 = (bf16[2,8,16,256]{3,2,1,0:T(8,128)(2,1)S(1)}, bf16[2,8,16,256]{3,2,1,0:T(8,128)(2,1)S(1)}, u32[]{:S(2)}, u32[]{:S(2)}) collective-permute-start(bf16[2,8,16,256]{3,2,1,0:T(8,128)(2,1)S(1)} %get-tuple-element.79), channel_id=1, source_target_pairs={{0,128},{16,144},{32,160},{48,176},{64,192},{80,208},{96,224},{112... | collective-permute-start | bytes 393224 | tf_op jit(solution)/shard_map/ppermute | solution.py:476
  96.3 4.5 %collective-permute-done.25.refs_0_.refs_8_ = bf16[2,8,16,256]{3,2,1,0:T(8,128)(2,1)S(1)} collective-permute-done((bf16[2,8,16,256]{3,2,1,0:T(8,128)(2,1)S(1)}, bf16[2,8,16,256]{3,2,1,0:T(8,128)(2,1)S(1)}, u32[]{:S(2)}, u32[]{:S(2)}) %collective-permute-start.25) | collective-permute-done | bytes 131104 | tf_op jit(solution)/shard_map/ppermute | solution.py:476
  100.9 2.7 %collective-permute-start.31 = (bf16[2,8,16,256]{3,2,1,0:T(8,128)(2,1)S(1)}, bf16[2,8,16,256]{3,2,1,0:T(8,128)(2,1)S(1)}, u32[]{:S(2)}, u32[]{:S(2)}) collective-permute-start(bf16[2,8,16,256]{3,2,1,0:T(8,128)(2,1)S(1)} %get-tuple-element.81), channel_id=1, source_target_pairs={{0,224},{16,240},{32,0},{48,16},{64,32},{80,48},{96,64},{112,80},{... | collective-permute-start | bytes 393224 | tf_op jit(solution)/shard_map/ppermute | solution.py:476
  103.6 3.6 %collective-permute-start.32 = (bf16[8,8,16,256]{3,2,1,0:T(8,128)(2,1)S(1)}, bf16[8,8,16,256]{3,2,1,0:T(8,128)(2,1)S(1)}, u32[]{:S(2)}, u32[]{:S(2)}) collective-permute-start(bf16[8,8,16,256]{3,2,1,0:T(8,128)(2,1)S(1)} %inner_pack.1), channel_id=1, source_target_pairs={{0,16},{16,0},{32,48},{48,32},{64,80},{80,64},{96,112},{112,96},{1... | collective-permute-start | bytes 1572872 | tf_op jit(solution)/shard_map/ppermute | solution.py:472
  107.5 6.3 %collective-permute-done.30.refs_5_.refs_13_ = bf16[2,8,16,256]{3,2,1,0:T(8,128)(2,1)S(1)} collective-permute-done((bf16[2,8,16,256]{3,2,1,0:T(8,128)(2,1)S(1)}, bf16[2,8,16,256]{3,2,1,0:T(8,128)(2,1)S(1)}, u32[]{:S(2)}, u32[]{:S(2)}) %collective-permute-start.30) | collective-permute-done | bytes 131104 | tf_op jit(solution)/shard_map/ppermute | solution.py:476
  (71 shorter events, 29.9 us)
Async XLA Ops:
  8.0 15.8 %collective-permute-start.17 = (bf16[9,2,32,512]{3,2,1,0:T(8,128)(2,1)S(1)}, bf16[9,2,32,512]{3,2,1,0:T(8,128)(2,1)S(1)}, u32[]{:S(2)}, u32[]{:S(2)}) collective-permute-start(bf16[9,2,32,512]{3,2,1,0:T(8,128)(2,1)S(1)} %get-tuple-element.66), channel_id=1, source_target_pairs={{16,1},{1,16},{17,2},{2,17},{18,3},{3,18},{19,4},{4,19},{20,5},{5,... | collective-permute-start | bytes 1769480 | tf_op jit(solution)/shard_map/ppermute | solution.py:506
  11.2 20.1 %collective-permute-start.1 = (bf16[2,8,16,256]{3,2,1,0:T(8,128)(2,1)S(1)}, bf16[2,8,16,256]{3,2,1,0:T(8,128)(2,1)S(1)}, u32[]{:S(2)}, u32[]{:S(2)}) collective-permute-start(bf16[2,8,16,256]{3,2,1,0:T(8,128)(2,1)S(1)} %get-tuple-element.47), channel_id=1, source_target_pairs={{0,128},{16,144},{32,160},{48,176},{64,192},{80,208},{96,224},{112... | collective-permute-start | bytes 393224 | tf_op jit(solution)/shard_map/ppermute | solution.py:476
  18.2 17.9 %collective-permute-start.4 = (bf16[2,8,16,256]{3,2,1,0:T(8,128)(2,1)S(1)}, bf16[2,8,16,256]{3,2,1,0:T(8,128)(2,1)S(1)}, u32[]{:S(2)}, u32[]{:S(2)}) collective-permute-start(bf16[2,8,16,256]{3,2,1,0:T(8,128)(2,1)S(1)} %get-tuple-element.49), channel_id=1, source_target_pairs={{0,96},{16,112},{32,128},{48,144},{64,160},{80,176},{96,192},{112,... | collective-permute-start | bytes 393224 | tf_op jit(solution)/shard_map/ppermute | solution.py:476
  19.8 16.3 %collective-permute-start.5 = (bf16[2,8,16,256]{3,2,1,0:T(8,128)(2,1)S(1)}, bf16[2,8,16,256]{3,2,1,0:T(8,128)(2,1)S(1)}, u32[]{:S(2)}, u32[]{:S(2)}) collective-permute-start(bf16[2,8,16,256]{3,2,1,0:T(8,128)(2,1)S(1)} %get-tuple-element.50), channel_id=1, source_target_pairs={{0,160},{16,176},{32,192},{48,208},{64,224},{80,240},{96,0},{112,1... | collective-permute-start | bytes 393224 | tf_op jit(solution)/shard_map/ppermute | solution.py:476
  22.7 15.7 %collective-permute-start.6 = (bf16[2,8,16,256]{3,2,1,0:T(8,128)(2,1)S(1)}, bf16[2,8,16,256]{3,2,1,0:T(8,128)(2,1)S(1)}, u32[]{:S(2)}, u32[]{:S(2)}) collective-permute-start(bf16[2,8,16,256]{3,2,1,0:T(8,128)(2,1)S(1)} %get-tuple-element.51), channel_id=1, source_target_pairs={{0,64},{16,80},{32,96},{48,112},{64,128},{80,144},{96,160},{112,17... | collective-permute-start | bytes 393224 | tf_op jit(solution)/shard_map/ppermute | solution.py:476
  23.9 17.6 %collective-permute-start.7 = (bf16[2,8,16,256]{3,2,1,0:T(8,128)(2,1)S(1)}, bf16[2,8,16,256]{3,2,1,0:T(8,128)(2,1)S(1)}, u32[]{:S(2)}, u32[]{:S(2)}) collective-permute-start(bf16[2,8,16,256]{3,2,1,0:T(8,128)(2,1)S(1)} %get-tuple-element.52), channel_id=1, source_target_pairs={{0,192},{16,208},{32,224},{48,240},{64,0},{80,16},{96,32},{112,48}... | collective-permute-start | bytes 393224 | tf_op jit(solution)/shard_map/ppermute | solution.py:476
  31.3 15.4 %collective-permute-start.8 = (bf16[2,8,16,256]{3,2,1,0:T(8,128)(2,1)S(1)}, bf16[2,8,16,256]{3,2,1,0:T(8,128)(2,1)S(1)}, u32[]{:S(2)}, u32[]{:S(2)}) collective-permute-start(bf16[2,8,16,256]{3,2,1,0:T(8,128)(2,1)S(1)} %get-tuple-element.54), channel_id=1, source_target_pairs={{0,32},{16,48},{32,64},{48,80},{64,96},{80,112},{96,128},{112,144}... | collective-permute-start | bytes 393224 | tf_op jit(solution)/shard_map/ppermute | solution.py:476
  36.2 13.8 %collective-permute-start.9 = (bf16[2,8,16,256]{3,2,1,0:T(8,128)(2,1)S(1)}, bf16[2,8,16,256]{3,2,1,0:T(8,128)(2,1)S(1)}, u32[]{:S(2)}, u32[]{:S(2)}) collective-permute-start(bf16[2,8,16,256]{3,2,1,0:T(8,128)(2,1)S(1)} %get-tuple-element.55), channel_id=1, source_target_pairs={{0,224},{16,240},{32,0},{48,16},{64,32},{80,48},{96,64},{112,80},{... | collective-permute-start | bytes 393224 | tf_op jit(solution)/shard_map/ppermute | solution.py:476
  36.2 22.1 %collective-permute-start.18 = (bf16[2,8,16,256]{3,2,1,0:T(8,128)(2,1)S(1)}, bf16[2,8,16,256]{3,2,1,0:T(8,128)(2,1)S(1)}, u32[]{:S(2)}, u32[]{:S(2)}) collective-permute-start(bf16[2,8,16,256]{3,2,1,0:T(8,128)(2,1)S(1)} %get-tuple-element.67), channel_id=1, source_target_pairs={{0,96},{16,112},{32,128},{48,144},{64,160},{80,176},{96,192},{112,... | collective-permute-start | bytes 393224 | tf_op jit(solution)/shard_map/ppermute | solution.py:476
  38.4 19.8 %collective-permute-start.19 = (bf16[2,8,16,256]{3,2,1,0:T(8,128)(2,1)S(1)}, bf16[2,8,16,256]{3,2,1,0:T(8,128)(2,1)S(1)}, u32[]{:S(2)}, u32[]{:S(2)}) collective-permute-start(bf16[2,8,16,256]{3,2,1,0:T(8,128)(2,1)S(1)} %get-tuple-element.68), channel_id=1, source_target_pairs={{0,160},{16,176},{32,192},{48,208},{64,224},{80,240},{96,0},{112,1... | collective-permute-start | bytes 393224 | tf_op jit(solution)/shard_map/ppermute | solution.py:476
  50.0 15.1 %collective-permute-start.20 = (bf16[2,8,16,256]{3,2,1,0:T(8,128)(2,1)S(1)}, bf16[2,8,16,256]{3,2,1,0:T(8,128)(2,1)S(1)}, u32[]{:S(2)}, u32[]{:S(2)}) collective-permute-start(bf16[2,8,16,256]{3,2,1,0:T(8,128)(2,1)S(1)} %get-tuple-element.69), channel_id=1, source_target_pairs={{0,64},{16,80},{32,96},{48,112},{64,128},{80,144},{96,160},{112,17... | collective-permute-start | bytes 393224 | tf_op jit(solution)/shard_map/ppermute | solution.py:476
  50.6 16.1 %collective-permute-start.21 = (bf16[2,8,16,256]{3,2,1,0:T(8,128)(2,1)S(1)}, bf16[2,8,16,256]{3,2,1,0:T(8,128)(2,1)S(1)}, u32[]{:S(2)}, u32[]{:S(2)}) collective-permute-start(bf16[2,8,16,256]{3,2,1,0:T(8,128)(2,1)S(1)} %get-tuple-element.70), channel_id=1, source_target_pairs={{0,192},{16,208},{32,224},{48,240},{64,0},{80,16},{96,32},{112,48}... | collective-permute-start | bytes 393224 | tf_op jit(solution)/shard_map/ppermute | solution.py:476
  53.7 16.0 %collective-permute-start.22 = (bf16[2,8,16,256]{3,2,1,0:T(8,128)(2,1)S(1)}, bf16[2,8,16,256]{3,2,1,0:T(8,128)(2,1)S(1)}, u32[]{:S(2)}, u32[]{:S(2)}) collective-permute-start(bf16[2,8,16,256]{3,2,1,0:T(8,128)(2,1)S(1)} %get-tuple-element.71), channel_id=1, source_target_pairs={{0,128},{16,144},{32,160},{48,176},{64,192},{80,208},{96,224},{112... | collective-permute-start | bytes 393224 | tf_op jit(solution)/shard_map/ppermute | solution.py:476
  58.3 15.0 %collective-permute-start.24 = (bf16[2,8,16,256]{3,2,1,0:T(8,128)(2,1)S(1)}, bf16[2,8,16,256]{3,2,1,0:T(8,128)(2,1)S(1)}, u32[]{:S(2)}, u32[]{:S(2)}) collective-permute-start(bf16[2,8,16,256]{3,2,1,0:T(8,128)(2,1)S(1)} %get-tuple-element.73), channel_id=1, source_target_pairs={{0,224},{16,240},{32,0},{48,16},{64,32},{80,48},{96,64},{112,80},{... | collective-permute-start | bytes 393224 | tf_op jit(solution)/shard_map/ppermute | solution.py:476
  65.1 13.9 %collective-permute-start.10 = (bf16[2,8,16,256]{3,2,1,0:T(8,128)(2,1)S(1)}, bf16[2,8,16,256]{3,2,1,0:T(8,128)(2,1)S(1)}, u32[]{:S(2)}, u32[]{:S(2)}) collective-permute-start(bf16[2,8,16,256]{3,2,1,0:T(8,128)(2,1)S(1)} %get-tuple-element.57), channel_id=1, source_target_pairs={{0,96},{16,112},{32,128},{48,144},{64,160},{80,176},{96,192},{112,... | collective-permute-start | bytes 393224 | tf_op jit(solution)/shard_map/ppermute | solution.py:476
  66.7 14.4 %collective-permute-start.11 = (bf16[2,8,16,256]{3,2,1,0:T(8,128)(2,1)S(1)}, bf16[2,8,16,256]{3,2,1,0:T(8,128)(2,1)S(1)}, u32[]{:S(2)}, u32[]{:S(2)}) collective-permute-start(bf16[2,8,16,256]{3,2,1,0:T(8,128)(2,1)S(1)} %get-tuple-element.58), channel_id=1, source_target_pairs={{0,160},{16,176},{32,192},{48,208},{64,224},{80,240},{96,0},{112,1... | collective-permute-start | bytes 393224 | tf_op jit(solution)/shard_map/ppermute | solution.py:476
  69.7 14.1 %collective-permute-start.13 = (bf16[2,8,16,256]{3,2,1,0:T(8,128)(2,1)S(1)}, bf16[2,8,16,256]{3,2,1,0:T(8,128)(2,1)S(1)}, u32[]{:S(2)}, u32[]{:S(2)}) collective-permute-start(bf16[2,8,16,256]{3,2,1,0:T(8,128)(2,1)S(1)} %get-tuple-element.60), channel_id=1, source_target_pairs={{0,192},{16,208},{32,224},{48,240},{64,0},{80,16},{96,32},{112,48}... | collective-permute-start | bytes 393224 | tf_op jit(solution)/shard_map/ppermute | solution.py:476
  73.3 13.6 %collective-permute-start.14 = (bf16[2,8,16,256]{3,2,1,0:T(8,128)(2,1)S(1)}, bf16[2,8,16,256]{3,2,1,0:T(8,128)(2,1)S(1)}, u32[]{:S(2)}, u32[]{:S(2)}) collective-permute-start(bf16[2,8,16,256]{3,2,1,0:T(8,128)(2,1)S(1)} %get-tuple-element.61), channel_id=1, source_target_pairs={{0,128},{16,144},{32,160},{48,176},{64,192},{80,208},{96,224},{112... | collective-permute-start | bytes 393224 | tf_op jit(solution)/shard_map/ppermute | solution.py:476
  79.0 13.0 %collective-permute-start.15 = (bf16[2,8,16,256]{3,2,1,0:T(8,128)(2,1)S(1)}, bf16[2,8,16,256]{3,2,1,0:T(8,128)(2,1)S(1)}, u32[]{:S(2)}, u32[]{:S(2)}) collective-permute-start(bf16[2,8,16,256]{3,2,1,0:T(8,128)(2,1)S(1)} %get-tuple-element.62), channel_id=1, source_target_pairs={{0,32},{16,48},{32,64},{48,80},{64,96},{80,112},{96,128},{112,144}... | collective-permute-start | bytes 393224 | tf_op jit(solution)/shard_map/ppermute | solution.py:476
  82.0 18.9 %collective-permute-start.25 = (bf16[2,8,16,256]{3,2,1,0:T(8,128)(2,1)S(1)}, bf16[2,8,16,256]{3,2,1,0:T(8,128)(2,1)S(1)}, u32[]{:S(2)}, u32[]{:S(2)}) collective-permute-start(bf16[2,8,16,256]{3,2,1,0:T(8,128)(2,1)S(1)} %get-tuple-element.75), channel_id=1, source_target_pairs={{0,96},{16,112},{32,128},{48,144},{64,160},{80,176},{96,192},{112,... | collective-permute-start | bytes 393224 | tf_op jit(solution)/shard_map/ppermute | solution.py:476
  83.8 17.1 %collective-permute-start.26 = (bf16[2,8,16,256]{3,2,1,0:T(8,128)(2,1)S(1)}, bf16[2,8,16,256]{3,2,1,0:T(8,128)(2,1)S(1)}, u32[]{:S(2)}, u32[]{:S(2)}) collective-permute-start(bf16[2,8,16,256]{3,2,1,0:T(8,128)(2,1)S(1)} %get-tuple-element.76), channel_id=1, source_target_pairs={{0,160},{16,176},{32,192},{48,208},{64,224},{80,240},{96,0},{112,1... | collective-permute-start | bytes 393224 | tf_op jit(solution)/shard_map/ppermute | solution.py:476
  86.8 16.8 %collective-permute-start.27 = (bf16[2,8,16,256]{3,2,1,0:T(8,128)(2,1)S(1)}, bf16[2,8,16,256]{3,2,1,0:T(8,128)(2,1)S(1)}, u32[]{:S(2)}, u32[]{:S(2)}) collective-permute-start(bf16[2,8,16,256]{3,2,1,0:T(8,128)(2,1)S(1)} %get-tuple-element.77), channel_id=1, source_target_pairs={{0,64},{16,80},{32,96},{48,112},{64,128},{80,144},{96,160},{112,17... | collective-permute-start | bytes 393224 | tf_op jit(solution)/shard_map/ppermute | solution.py:476
  92.0 15.2 %collective-permute-start.28 = (bf16[2,8,16,256]{3,2,1,0:T(8,128)(2,1)S(1)}, bf16[2,8,16,256]{3,2,1,0:T(8,128)(2,1)S(1)}, u32[]{:S(2)}, u32[]{:S(2)}) collective-permute-start(bf16[2,8,16,256]{3,2,1,0:T(8,128)(2,1)S(1)} %get-tuple-element.78), channel_id=1, source_target_pairs={{0,192},{16,208},{32,224},{48,240},{64,0},{80,16},{96,32},{112,48}... | collective-permute-start | bytes 393224 | tf_op jit(solution)/shard_map/ppermute | solution.py:476
  93.9 13.6 %collective-permute-start.29 = (bf16[2,8,16,256]{3,2,1,0:T(8,128)(2,1)S(1)}, bf16[2,8,16,256]{3,2,1,0:T(8,128)(2,1)S(1)}, u32[]{:S(2)}, u32[]{:S(2)}) collective-permute-start(bf16[2,8,16,256]{3,2,1,0:T(8,128)(2,1)S(1)} %get-tuple-element.79), channel_id=1, source_target_pairs={{0,128},{16,144},{32,160},{48,176},{64,192},{80,208},{96,224},{112... | collective-permute-start | bytes 393224 | tf_op jit(solution)/shard_map/ppermute | solution.py:476
  (16 other events, 163.2 us)
